TPU v7x, 32 devices: a whole 2x2x4 slice. The times are simulated.
32 devices in a mesh: dp: 8 (over z, y), expert: 4 (over x, core).
Axes of the slice: x: 2, y: 2, z: 4, core: 2. Of those that a mesh axis runs over, the one named last changes fastest.
Arguments:
- tokens: bfloat16 [4096, 2048], P(('dp', 'expert')), may hold values from -6 to 6
- choice_rows: int32 [8, 4, 128], P('dp', 'expert'), may hold values from 0 to 511, as said below
- gate_weights: float32 [8, 4, 128], P('dp', 'expert'), may hold values from 0.1 to 1
- w_gate: bfloat16 [4, 2048, 1024], P('expert', 'dp'), may hold values from -0.125 to 0.125
- w_up: bfloat16 [4, 2048, 1024], P('expert', 'dp'), may hold values from -0.125 to 0.125
- w_down: bfloat16 [4, 1024, 2048], P('expert', 'dp'), may hold values from -0.1875 to 0.1875
Outputs:
- mixed: bfloat16 [4096, 2048], P(('dp', 'expert'))
Inputs may be any that keep to these rules, and one draw needn't show every extreme that they name: `choice_rows`: for each group and expert the 128 numbers are distinct; at most 64 of them lie among the 128 tokens of one device of the group (numbers k * 128 to (k + 1) * 128 - 1 belong to device k of the expert axis), and for every expert and group some device gives exactly 64.
All inputs are finite; a program needn't handle non-finite values.
Results may differ from a plain program's by a relative error of at most 0.0057.
Values may be sent and summed in bfloat16 or wider, within the bound.
No kernel may reach another device: no remote copies, remote signals or barrier semaphores. Data moves between devices by JAX's collectives and lax.ppermute only.
A program may use at most 64 MiB of HBM per device.

v0:
```python
import jax
import jax.numpy as jnp
from jax import lax
from jax.sharding import PartitionSpec as P


def from_partner(value, axis, bit):
    mask = 2**bit
    pairs = [(source, source ^ mask) for source in range(lax.axis_size(axis))]
    return lax.ppermute(value, axis, pairs)


def arrange_halves(shard, replicas):
    rows_shard, units = shard.shape
    split_view = shard.reshape(rows_shard, 2, units // 2).transpose(1, 0, 2)
    return jnp.tile(split_view, (replicas // 2, 1, 1)).reshape(replicas * rows_shard, units // 2)


def per_device(tokens, choice_rows, gate_weights, w_gate, w_up, w_down):
    experts = lax.axis_size("expert")
    tok_dev, width = tokens.shape
    most = tok_dev // 2
    own_rows = choice_rows[0, 0]
    capacity = own_rows.shape[0]
    every_rows = lax.all_gather(choice_rows, "expert", axis=1, tiled=True)[0]
    myself = lax.axis_index("expert")
    source = every_rows // tok_dev
    local_rows = every_rows % tok_dev
    hits = (source == myself).astype(jnp.int32)
    ranks = jnp.cumsum(hits, axis=1) - 1
    slot_hot = (
        (ranks[:, :, None] == jnp.arange(most)[None, None, :]) & (hits[:, :, None] > 0)
    ).astype(jnp.bfloat16)
    token_hot = (local_rows[:, :, None] == jnp.arange(tok_dev)[None, None, :]).astype(jnp.bfloat16)
    select = jnp.einsum(
        "ecm,ect->emt", slot_hot, token_hot, preferred_element_type=jnp.float32
    ).astype(jnp.bfloat16)
    own_source = own_rows // tok_dev
    source_hot = (own_source[:, None] == jnp.arange(experts)[None, :]).astype(jnp.int32)
    running = jnp.cumsum(source_hot, axis=0) - 1
    own_rank = jnp.sum(running * source_hot, axis=1)
    position = own_source * most + own_rank
    group_rows = lax.all_gather(tokens, "expert", axis=0, tiled=True)
    picked = jnp.take(group_rows, own_rows, axis=0)
    gate_shard = w_gate[0]
    up_shard = w_up[0]
    replicas = lax.axis_size("dp")
    half = lax.axis_index("dp") % 2
    gate_half, up_half = (
        lax.all_to_all(
            arrange_halves(gate_shard, replicas), "dp", split_axis=0, concat_axis=0, tiled=True
        ),
        lax.all_to_all(
            arrange_halves(up_shard, replicas), "dp", split_axis=0, concat_axis=0, tiled=True
        ),
    )
    partner = from_partner(picked, "dp", 0)
    both_rows = jnp.concatenate([picked, partner], axis=0)
    gate_part = jnp.dot(both_rows, gate_half, preferred_element_type=jnp.float32)
    up_part = jnp.dot(both_rows, up_half, preferred_element_type=jnp.float32)
    hidden_part = (jax.nn.silu(gate_part) * up_part).astype(jnp.bfloat16)
    other_half = from_partner(hidden_part[capacity:], "dp", 0)
    mine_half = hidden_part[:capacity]
    first_half = jnp.where(half == 0, mine_half, other_half)
    second_half = jnp.where(half == 0, other_half, mine_half)
    hidden = jnp.concatenate([first_half, second_half], axis=1)
    expert_out = jnp.dot(
        hidden,
        lax.all_gather(w_down[0], "dp", axis=0, tiled=True),
        preferred_element_type=jnp.float32,
    )
    contribution = (gate_weights[0, 0][:, None] * expert_out).astype(jnp.bfloat16)
    outgoing = jnp.zeros((experts * most, width), jnp.bfloat16).at[position].set(contribution)
    returned = lax.all_to_all(outgoing, "expert", split_axis=0, concat_axis=0, tiled=True)
    mixed = jnp.einsum(
        "emt,emd->td",
        select,
        returned.reshape(experts, most, width),
        preferred_element_type=jnp.float32,
    )
    return mixed.astype(jnp.bfloat16)


def solution(mesh):
    return jax.shard_map(
        per_device,
        mesh=mesh,
        in_specs=(
            P(("dp", "expert"), None),
            P("dp", "expert", None),
            P("dp", "expert", None),
            P("expert", "dp", None),
            P("expert", "dp", None),
            P("expert", "dp", None),
        ),
        out_specs=P(("dp", "expert"), None),
        check_vma=False,
    )
```

profile of v0, /device:TPU:0, one launch (start us, length us, event | category | flops | bytes accessed | tf_op | source)
XLA Modules:
  0.0 207.7 jit_solution(6045171415970842148)
XLA Ops:
  6.5 0.7 all-gather.4.cloned.1.call-update
  7.3 1.4 reshape_squeeze.6
  8.8 1.5 tile.16
  10.3 7.4 %all-to-all-start = ((bf16[8,256,512]{2,1,0:T(8,128)(2,1)}), bf16[8,256,512]{2,1,0:T(8,128)(2,1)S(1)}, u32[]{:S(2)}, u32[]{:S(2)}) async-start(bf16[8,256,512]{2,1,0:T(8,128)(2,1)} %bitcast.9), calls=%async_computation | async-start | bytes 4194304 | tf_op jit(solution)/shard_map/all_to_all | solution.py:50
  17.7 0.7 all-gather.6.cloned.1.call-update
  18.4 0.4 reshape_squeeze.7
  18.9 63.9 %all-to-all-done = bf16[8,256,512]{2,1,0:T(8,128)(2,1)S(1)} async-done(((bf16[8,256,512]{2,1,0:T(8,128)(2,1)}), bf16[8,256,512]{2,1,0:T(8,128)(2,1)S(1)}, u32[]{:S(2)}, u32[]{:S(2)}) %all-to-all-start) | async-done | bytes 2097184 | tf_op jit(solution)/shard_map/all_to_all | solution.py:50
  82.8 1.5 tile.18
  84.3 4.5 %all-to-all-start.1 = ((bf16[8,256,512]{2,1,0:T(8,128)(2,1)}), bf16[8,256,512]{2,1,0:T(8,128)(2,1)}, u32[]{:S(2)}, u32[]{:S(2)}) async-start(bf16[8,256,512]{2,1,0:T(8,128)(2,1)} %bitcast.12), calls=%async_computation.1 | async-start | bytes 4194304 | tf_op jit(solution)/shard_map/all_to_all | solution.py:53
  88.9 0.2 reduce_window_sum.23
  89.4 3.3 %gather_fusion = bf16[128,2048]{1,0:T(8,128)(2,1)S(1)} fusion(bf16[512,2048]{1,0:T(8,128)(2,1)} %all-gather.4.cloned.1.call-done, s32[1024]{0:T(1024)S(1)} %pad_clamp_fusion), kind=kCustom, calls=%fused_computation | custom fusion | bytes 1049088 | tf_op jit(solution)/shard_map/jit(_take)/gather | solution.py:44
  92.8 2.0 collective-permute-start
  94.7 47.6 %collective-permute-done = bf16[128,2048]{1,0:T(8,128)(2,1)S(1)} collective-permute-done((bf16[128,2048]{1,0:T(8,128)(2,1)S(1)}, bf16[128,2048]{1,0:T(8,128)(2,1)S(1)}, u32[]{:S(2)}, u32[]{:S(2)}) %collective-permute-start) | collective-permute-done | bytes 524320 | tf_op jit(solution)/shard_map/ppermute | solution.py:10
  142.4 1.5 fusion.10
  143.9 23.0 %all-to-all-done.1 = bf16[8,256,512]{2,1,0:T(8,128)(2,1)} async-done(((bf16[8,256,512]{2,1,0:T(8,128)(2,1)}), bf16[8,256,512]{2,1,0:T(8,128)(2,1)}, u32[]{:S(2)}, u32[]{:S(2)}) %all-to-all-start.1) | async-done | bytes 2097184 | tf_op jit(solution)/shard_map/all_to_all | solution.py:53
  166.9 2.4 %multiply_convert_fusion = bf16[256,512]{1,0:T(8,128)(2,1)S(1)} fusion(f32[256,512]{1,0:T(8,128)} %fusion.10, bf16[2048,512]{1,0:T(8,128)(2,1)} %bitcast.13, bf16[128,2048]{1,0:T(8,128)(2,1)S(1)} %collective-permute-done, bf16[128,2048]{1,0:T(8,128)(2,1)S(1)} %broadcast_select_fusion), kind=kOutput, calls=%fused_computation.12 | convolution fusion | flops 539754496 | bytes 3932160 | tf_op jit(solution)/shard_map/dot_general | solution.py:60
  169.3 1.5 collective-permute-start.1
  170.8 3.9 %collective-permute-done.1 = bf16[128,512]{1,0:T(8,128)(2,1)S(1)} collective-permute-done((bf16[128,512]{1,0:T(8,128)(2,1)S(1)}, bf16[128,512]{1,0:T(8,128)(2,1)S(1)}, u32[]{:S(2)}, u32[]{:S(2)}) %collective-permute-start.1) | collective-permute-done | bytes 131104 | tf_op jit(solution)/shard_map/ppermute | solution.py:10
  174.8 2.9 %fusion.6 = bf16[128,2048]{1,0:T(8,128)(2,1)S(1)} fusion(bf16[1,1024,2048]{2,1,0:T(8,128)(2,1)} %all-gather.6.cloned.1.call-done, f32[128]{0:T(128)S(1)} %bitcast.58, bf16[128,512]{1,0:T(8,128)(2,1)S(1)} %get-tuple-element.8, bf16[128,512]{1,0:T(8,128)(2,1)S(1)} %get-tuple-element.7), kind=kOutput, calls=%fused_computation.7 | convolution fusion | flops 537919488 | bytes 4981248 | tf_op jit(solution)/shard_map/dot_general | solution.py:67
  177.7 2.4 %scatter_custom_fusion = bf16[256,2048]{1,0:T(8,128)(2,1)} fusion(s32[128]{0:T(128)S(1)} %get-tuple-element.10, bf16[128,2048]{1,0:T(8,128)(2,1)S(1)} %fusion.6, bf16[]{:T(256)} %constant.85.clone.1), kind=kCustom, calls=%fused_computation.13 | custom fusion | bytes 1048578 | tf_op jit(solution)/shard_map/scatter | solution.py:73
  180.2 3.5 %all-to-all-start.2 = ((bf16[4,64,2048]{2,1,0:T(8,128)(2,1)}), bf16[4,64,2048]{2,1,0:T(8,128)(2,1)S(1)}, u32[]{:S(2)}, u32[]{:S(2)}) async-start(bf16[4,64,2048]{2,1,0:T(8,128)(2,1)} %bitcast.15), calls=%async_computation.2 | async-start | bytes 2097152 | tf_op jit(solution)/shard_map/all_to_all | solution.py:74
  183.7 15.3 %all_gather.9 = s32[1,4,128]{2,0,1:T(1,128)S(1)} all-gather(s32[1,1,128]{2,0,1:T(1,128)S(1)} %bitcast.57), channel_id=1, replica_groups=mesh['dp'=8,'expert'=4] {'expert'}, dimensions={1}, use_global_device_ids=true | all-gather | bytes 2560 | tf_op jit(solution)/shard_map/all_gather | solution.py:25
  199.0 0.3 reduce_window_sum.22
  199.3 1.6 fusion.5
  (24 shorter events, 0.7 us)
Async XLA Ops:
  6.5 82.8 %all-gather.4.cloned.1.call-start = ((), (), s32[]{:S(2)}) async-start(), calls=%async_computation.3 | async-start | bytes 2621440 | tf_op jit(solution)/shard_map/all_gather | solution.py:43
  10.3 8.2 %copy-start = (bf16[1,256,1024]{2,1,0:T(8,128)(2,1)S(1)}, bf16[1,256,1024]{2,1,0:T(8,128)(2,1)}, u32[]{:S(2)}) copy-start(bf16[1,256,1024]{2,1,0:T(8,128)(2,1)} %param.10) | copy-start | bytes 1572868
  10.3 72.5 %all-to-all-start = ((bf16[8,256,512]{2,1,0:T(8,128)(2,1)}), bf16[8,256,512]{2,1,0:T(8,128)(2,1)S(1)}, u32[]{:S(2)}, u32[]{:S(2)}) async-start(bf16[8,256,512]{2,1,0:T(8,128)(2,1)} %bitcast.9), calls=%async_computation | async-start | bytes 4194304 | tf_op jit(solution)/shard_map/all_to_all | solution.py:50
  17.7 157.0 %all-gather.6.cloned.1.call-start = ((), (), s32[]{:S(2)}) async-start(), calls=%async_computation.4 | async-start | bytes 4718592 | tf_op jit(solution)/shard_map/all_gather | solution.py:69
  84.3 4.5 %copy-start.1 = (s32[1,1,128]{2,1,0:T(1,128)S(1)}, s32[1,1,128]{2,1,0:T(1,128)}, u32[]{:S(2)}) copy-start(s32[1,1,128]{2,1,0:T(1,128)} %param.7) | copy-start | bytes 1540
  84.3 82.6 %all-to-all-start.1 = ((bf16[8,256,512]{2,1,0:T(8,128)(2,1)}), bf16[8,256,512]{2,1,0:T(8,128)(2,1)}, u32[]{:S(2)}, u32[]{:S(2)}) async-start(bf16[8,256,512]{2,1,0:T(8,128)(2,1)} %bitcast.12), calls=%async_computation.1 | async-start | bytes 4194304 | tf_op jit(solution)/shard_map/all_to_all | solution.py:53
  92.8 49.6 %collective-permute-start = (bf16[128,2048]{1,0:T(8,128)(2,1)S(1)}, bf16[128,2048]{1,0:T(8,128)(2,1)S(1)}, u32[]{:S(2)}, u32[]{:S(2)}) collective-permute-start(bf16[128,2048]{1,0:T(8,128)(2,1)S(1)} %broadcast_select_fusion), channel_id=1, source_target_pairs={{0,4},{4,0},{8,12},{12,8},{16,20},{20,16},{24,28},{28,24},{1,5},{5... | collective-permute-start | bytes 1572872 | tf_op jit(solution)/shard_map/ppermute | solution.py:10
  166.9 7.9 %copy-start.2 = (f32[1,1,128]{2,1,0:T(1,128)S(1)}, f32[1,1,128]{2,1,0:T(1,128)}, u32[]{:S(2)}) copy-start(f32[1,1,128]{2,1,0:T(1,128)} %param.8) | copy-start | bytes 1540
  169.3 5.4 %collective-permute-start.1 = (bf16[128,512]{1,0:T(8,128)(2,1)S(1)}, bf16[128,512]{1,0:T(8,128)(2,1)S(1)}, u32[]{:S(2)}, u32[]{:S(2)}) collective-permute-start(bf16[128,512]{1,0:T(8,128)(2,1)S(1)} %slice.11), channel_id=1, source_target_pairs={{0,4},{4,0},{8,12},{12,8},{16,20},{20,16},{24,28},{28,24},{1,5},{5... | collective-permute-start | bytes 393224 | tf_op jit(solution)/shard_map/ppermute | solution.py:10
  180.2 19.2 %all-to-all-start.2 = ((bf16[4,64,2048]{2,1,0:T(8,128)(2,1)}), bf16[4,64,2048]{2,1,0:T(8,128)(2,1)S(1)}, u32[]{:S(2)}, u32[]{:S(2)}) async-start(bf16[4,64,2048]{2,1,0:T(8,128)(2,1)} %bitcast.15), calls=%async_computation.2 | async-start | bytes 2097152 | tf_op jit(solution)/shard_map/all_to_all | solution.py:74
Sparse Core Ops, SparseCore 0:
  8.9 25.2 all-gather.3
  36.4 127.6 all-gather.5
where the time goes:
time: 208 us
  waiting for transfers between devices  140 us (67%)
  starting transfers between devices  18.9 us (9%)
  blocking collectives  15.3 us (7%)
  between operations  13.6 us (7%)
  local copies, waits for them, and re-layouts  10.7 us (5%)
  matrix products  8.42 us (4%)
    all_to_all x1, waiting for transfers between devices, per_device(): lax.all_to_all(arrange_halves(gate_shard, replicas), 'dp', split_axis=0,...  63.9 us
    ppermute x2, waiting for transfers between devices, from_partner(): return lax.ppermute(value, axis, pairs)  51.5 us
    all_to_all x1, waiting for transfers between devices, per_device(): lax.all_to_all(arrange_halves(up_shard, replicas), 'dp', split_axis=0, co...  23 us
    all_gather x1, blocking collectives, per_device(): every_rows = lax.all_gather(choice_rows, 'expert', axis=1, tiled=True)[0]  15.3 us
    all_to_all x1, starting transfers between devices, per_device(): lax.all_to_all(arrange_halves(gate_shard, replicas), 'dp', split_axis=0,...  7.41 us
    all_to_all x1, starting transfers between devices, per_device(): lax.all_to_all(arrange_halves(up_shard, replicas), 'dp', split_axis=0, co...  4.48 us
  transfers between devices with their start and end apart: 7, of which 4 were waited for; matrix products, arithmetic and copies ran while one was open for 6% of the time, Pallas kernels for 0%

commit v1 on v0

v1 whole, which is shorter than its diff:
```python
import functools

import jax
import jax.numpy as jnp
from jax import lax
from jax.experimental import pallas as pl
from jax.experimental.pallas import tpu as pltpu
from jax.sharding import PartitionSpec as P

CHUNKS = 2
F32 = jnp.float32
BF16 = jnp.bfloat16


def swap(value, axis, mask):
    pairs = [(source, source ^ mask) for source in range(lax.axis_size(axis))]
    return lax.ppermute(value, axis, pairs)


def after(value, *others):
    return lax.optimization_barrier((value, *others))[0]


def call(kernel, out_shape, *args, flops=0, scalars=0):
    in_specs = [pl.BlockSpec(memory_space=pltpu.SMEM)] * scalars
    in_specs += [pl.BlockSpec(memory_space=pltpu.VMEM)] * (len(args) - scalars)
    outs = out_shape if isinstance(out_shape, (list, tuple)) else [out_shape]
    size = sum(a.size * a.dtype.itemsize for a in (*args, *outs))
    return pl.pallas_call(
        kernel,
        out_shape=out_shape,
        in_specs=in_specs,
        out_specs=jax.tree.map(lambda _: pl.BlockSpec(memory_space=pltpu.VMEM), out_shape),
        compiler_params=pltpu.CompilerParams(vmem_limit_bytes=40 * 2**20),
        cost_estimate=pl.CostEstimate(flops=flops, bytes_accessed=size, transcendentals=0),
    )(*args)


def shape(*dims, dtype=BF16):
    return jax.ShapeDtypeStruct(dims, dtype)


def dot(a, b):
    return jnp.dot(a, b, preferred_element_type=F32)


def split_units(quarter_ref, gate_ref, up_ref, *out_refs, replicas):
    quarter = quarter_ref[0]
    rows, units = gate_ref.shape[1:]
    block = units // replicas
    for part in range(4):
        pieces = [
            ref[0, :, (4 * j + part) * block : (4 * j + part + 1) * block]
            for ref in (gate_ref, up_ref)
            for j in range(replicas // 4)
        ]
        value = jnp.concatenate(pieces, axis=1)
        for low in range(4):

            @pl.when((quarter ^ low) == part)
            def _():
                out_refs[low][...] = value


def ranks_of(hits):
    c = hits.shape[1]
    before = lax.broadcasted_iota(jnp.int32, (c, c), 0) < lax.broadcasted_iota(jnp.int32, (c, c), 1)
    return dot(hits.astype(BF16), before.astype(BF16)).astype(jnp.int32)


def own_tables(expert_ref, rows_ref, pick_ref, place_ref, *, experts, tok_dev):
    rows = rows_ref[...]
    capacity = rows.shape[1]
    block = (rows // tok_dev) ^ expert_ref[0]
    local = rows % tok_dev
    bits = experts.bit_length() - 1
    seat = jnp.zeros_like(block)
    for bit in range(bits):
        seat = seat | (((block >> bit) & 1) << (bits - 1 - bit))
    place = seat * tok_dev + local
    count = experts * tok_dev
    pick_ref[...] = (lax.broadcasted_iota(jnp.int32, (count, capacity), 0) == place).astype(BF16)
    hot = lax.broadcasted_iota(jnp.int32, (experts, capacity), 0) == block
    rank = jnp.sum(jnp.where(hot, ranks_of(hot.astype(F32)), 0), axis=0, keepdims=True)
    most = tok_dev // 2
    position = block * most + rank
    place_ref[...] = (
        lax.broadcasted_iota(jnp.int32, (experts * most, capacity), 0) == position
    ).astype(BF16)


def back_table(expert_ref, rows_ref, select_ref, *, experts, tok_dev):
    rows = rows_ref[...]
    capacity = rows.shape[1]
    most = tok_dev // 2
    hits = (rows // tok_dev) == expert_ref[0]
    local = jnp.where(hits, rows % tok_dev, -1)
    rank = ranks_of(hits.astype(F32))
    bits = experts.bit_length() - 1
    for mask in range(experts):
        seat = int(f"{mask:0{bits}b}"[::-1], 2) if bits else 0
        token = lax.broadcasted_iota(jnp.int32, (tok_dev, capacity), 0) == local[seat : seat + 1]
        slot = lax.broadcasted_iota(jnp.int32, (most, capacity), 0) == rank[seat : seat + 1]
        table = lax.dot_general(
            token.astype(BF16), slot.astype(BF16), (((1,), (1,)), ((), ())), preferred_element_type=F32
        )
        select_ref[:, mask * most : (mask + 1) * most] = table.astype(BF16)


def pick_rows(pick_ref, *refs):
    out_ref = refs[-1]
    total, start = 0.0, 0
    for ref in refs[:-1]:
        rows = ref.shape[0]
        total = total + lax.dot_general(
            pick_ref[start : start + rows, :],
            ref[...],
            (((0,), (0,)), ((), ())),
            preferred_element_type=F32,
        )
        start += rows
    out_ref[...] = total.astype(BF16)


def hidden_units(where_ref, own_ref, other_ref, *refs, pieces, reorder):
    weights, (keep_ref, send_ref, total) = refs[:pieces], refs[pieces:]
    tall = own_ref.shape[0]
    for index in range(pieces):
        rows = weights[index].shape[0]
        columns = pl.ds(pl.multiple_of(where_ref[index] * rows, min(rows, 256)), rows)
        for side, ref in enumerate((own_ref, other_ref)):
            lines = pl.ds(side * tall, tall)
            product = dot(ref[:, columns], weights[index][...])
            if index == 0:
                total[lines, :] = product
            else:
                total[lines, :] += product
    half = total.shape[1] // 2
    block = half // reorder
    for side, out_ref in enumerate((keep_ref, send_ref)):
        lines = pl.ds(side * tall, tall)
        for j in range(reorder):
            if reorder == 1:
                first, second = pl.ds(0, half), pl.ds(half, half)
            else:
                at = (where_ref[0] // 4) ^ j
                first = pl.ds(pl.multiple_of(at * block, 128), block)
                second = pl.ds(pl.multiple_of(half + at * block, 128), block)
            gate, up = total[lines, first], total[lines, second]
            out_ref[:, j * block : (j + 1) * block] = (gate / (1.0 + jnp.exp(-gate)) * up).astype(BF16)


def down_units(keep_ref, came_ref, *refs, pieces):
    own, other, (out_ref, away_ref) = refs[:pieces], refs[pieces : 2 * pieces], refs[2 * pieces :]
    capacity = out_ref.shape[0]
    for side, target in enumerate((out_ref, away_ref)):
        lines = pl.ds(side * capacity, capacity)
        total = 0.0
        for hidden, parts in ((keep_ref, own), (came_ref, other)):
            start = 0
            for part in parts:
                rows = part.shape[0]
                total = total + dot(hidden[lines, start : start + rows], part[...])
                start += rows
        target[...] = total.astype(target.dtype)


def weigh(place_ref, weights_ref, out_ref, away_ref, *sent_refs):
    total = out_ref[...] + away_ref[...].astype(F32)
    contribution = (weights_ref[...] * total).astype(BF16)
    most = sent_refs[0].shape[0]
    for block, ref in enumerate(sent_refs):
        ref[...] = dot(place_ref[block * most : (block + 1) * most, :], contribution).astype(BF16)


def mix(select_ref, *refs):
    returned, out_ref = refs[:-1], refs[-1]
    most = returned[0].shape[0]
    total = 0.0
    for block, ref in enumerate(returned):
        total = total + dot(select_ref[:, block * most : (block + 1) * most], ref[...])
    out_ref[...] = total.astype(BF16)


def per_device(tokens, choice_rows, gate_weights, w_gate, w_up, w_down):
    experts = lax.axis_size("expert")
    replicas = lax.axis_size("dp")
    expert = lax.axis_index("expert").astype(jnp.int32)
    replica = lax.axis_index("dp").astype(jnp.int32)
    tok_dev, width = tokens.shape
    most = tok_dev // 2
    own_rows = choice_rows[0]
    capacity = own_rows.shape[1]
    rows_shard, units = w_gate.shape[1:]
    block = units // replicas

    outgoing = call(
        functools.partial(split_units, replicas=replicas),
        [shape(rows_shard, units // 2)] * 4,
        (replica % 4)[None],
        w_gate,
        w_up,
        scalars=1,
    )
    weights = [outgoing[0]] + [None] * (replicas - 1)
    for mask in range(replicas - 1, 0, -1):
        weights[mask] = swap(outgoing[mask % 4], "dp", mask)

    group, every = [tokens], own_rows
    bit = experts // 2
    while bit > 0:
        have = group[0] if len(group) == 1 else jnp.concatenate(group, axis=0)
        group.append(swap(have, "expert", bit))
        every = jnp.concatenate([every, swap(every, "expert", bit)], axis=0)
        bit //= 2
    pick_hot, place_hot = call(
        functools.partial(own_tables, experts=experts, tok_dev=tok_dev),
        [shape(experts * tok_dev, capacity), shape(experts * most, capacity)],
        expert[None],
        own_rows,
        scalars=1,
    )
    picked = call(
        pick_rows,
        shape(capacity, width),
        pick_hot,
        *group,
        flops=2 * experts * tok_dev * capacity * width,
    )

    pair = jnp.concatenate([picked, swap(picked, "dp", 2)], axis=0)
    other_pair = swap(pair, "dp", 1)
    order = replica ^ jnp.arange(replicas, dtype=jnp.int32)
    aligned = rows_shard % 128 == 0
    if not aligned:
        weights = [jnp.take(jnp.stack(weights), order, axis=0).reshape(-1, units // 2)]
        order = jnp.zeros((1,), jnp.int32)
    reorder = replicas // 4 if block % 128 == 0 else 1
    keep, send = pl.pallas_call(
        functools.partial(hidden_units, pieces=len(weights), reorder=reorder),
        out_shape=[shape(2 * capacity, units // 4)] * 2,
        in_specs=[pl.BlockSpec(memory_space=pltpu.SMEM)]
        + [pl.BlockSpec(memory_space=pltpu.VMEM)] * (2 + len(weights)),
        out_specs=[pl.BlockSpec(memory_space=pltpu.VMEM)] * 2,
        scratch_shapes=[pltpu.VMEM((4 * capacity, units // 2), F32)],
        compiler_params=pltpu.CompilerParams(vmem_limit_bytes=40 * 2**20),
        cost_estimate=pl.CostEstimate(
            flops=4 * capacity * width * units, bytes_accessed=2**23, transcendentals=0
        ),
    )(order, pair, other_pair, *weights)
    came = swap(send, "dp", 1)

    gate_column = gate_weights[0, 0][:, None]
    step = width // CHUNKS
    select = call(
        functools.partial(back_table, experts=experts, tok_dev=tok_dev),
        shape(tok_dev, experts * most),
        expert[None],
        every,
        scalars=1,
    )
    results = []
    for chunk in range(CHUNKS):
        own = [after(w_down[0, :, chunk * step : (chunk + 1) * step], weights[-1])]
        other = [swap(own[0], "dp", 1)]
        bit = 4
        while bit < replicas:
            have = own[0] if len(own) == 1 else jnp.concatenate(own, axis=0)
            own.append(swap(have, "dp", bit))
            other.append(swap(own[-1], "dp", 1))
            bit *= 2
        if block % 128 != 0:
            turn = (replica // 4) ^ jnp.arange(replicas // 4, dtype=jnp.int32)
            own, other = (
                [jnp.concatenate(x, axis=0).reshape(replicas // 4, block, step)[turn].reshape(-1, step)]
                for x in (own, other)
            )
        out, away = call(
            functools.partial(down_units, pieces=len(own)),
            [shape(capacity, step, dtype=F32), shape(capacity, step)],
            keep,
            came,
            *own,
            *other,
            flops=2 * capacity * units * step,
        )
        sent = call(
            weigh,
            [shape(most, step)] * experts,
            place_hot,
            gate_column,
            out,
            swap(away, "dp", 2),
            flops=2 * experts * most * capacity * step,
        )
        returned = [sent[0]] + [swap(sent[c], "expert", c) for c in range(1, experts)]
        results.append(
            call(
                mix,
                shape(tok_dev, step),
                select,
                *returned,
                flops=2 * experts * most * tok_dev * step,
            )
        )
    return jnp.concatenate(results, axis=1)


def solution(mesh):
    return jax.shard_map(
        per_device,
        mesh=mesh,
        in_specs=(
            P(("dp", "expert"), None),
            P("dp", "expert", None),
            P("dp", "expert", None),
            P("expert", "dp", None),
            P("expert", "dp", None),
            P("expert", "dp", None),
        ),
        out_specs=P(("dp", "expert"), None),
        check_vma=False,
    )
```

time: 208 us -> 164 us (0.79)
  waiting for transfers between devices: 140 us -> 114 us
  starting transfers between devices: 18.9 us -> 40.2 us
  blocking collectives: 15.3 us -> 0 us
  between operations: 13.6 us -> 0.16 us
  local copies, waits for them, and re-layouts: 10.7 us -> 0.17 us
  matrix products: 8.42 us -> 0 us
  Pallas kernels: 0 us -> 6.47 us
  other arithmetic: 0.93 us -> 3.04 us
    all_to_all x3 -> x0, waiting for transfers between devices: 86.9 us -> none  [the longest x1 63.9 us: per_device(): lax.all_to_all(arrange_halves(gate_shard, replicas), 'dp', split_axis=0,...]
    ppermute x2 -> x28, waiting for transfers between devices: 51.5 us -> 114 us  [swap(): return lax.ppermute(value, axis, pairs)]
    ppermute x2 -> x28, starting transfers between devices: 3.42 us -> 40.2 us  [swap(): return lax.ppermute(value, axis, pairs)]
    all_to_all x3 -> x0, starting transfers between devices: 15.4 us -> none  [the longest x1 7.41 us: per_device(): lax.all_to_all(arrange_halves(gate_shard, replicas), 'dp', split_axis=0,...]
    all_gather x1 -> x0, blocking collectives: 15.3 us -> none  [per_device(): every_rows = lax.all_gather(choice_rows, 'expert', axis=1, tiled=True)[0]]
    dot_general x4 -> x0, matrix products: 8.42 us -> none  [the longest x1 2.95 us: per_device(): jnp.dot(hidden, lax.all_gather(w_down[0], 'dp', axis=0, tiled=True), pref...]
    pallas_call x0 -> x11, Pallas kernels: none -> 6.47 us  [the longest x10 4.48 us: call(): pl.pallas_call(kernel, out_shape=out_shape, in_specs=in_specs, out_specs=...]
    another operation x4 -> x1, local copies, waits for them, and re-layouts: 4.87 us -> 0.11 us  [per_device(): gate_column = gate_weights[0, 0][:, None]]
  transfers between devices with their start and end apart: 7 -> 28, of which waited for: 4 -> 15; matrix products, arithmetic and copies ran while one was open for 6% -> 0% of each run, Pallas kernels for 0% -> 3%
where the time goes in v1:
time: 164 us
  waiting for transfers between devices  114 us (70%)
  starting transfers between devices  40.2 us (25%)
  Pallas kernels  6.47 us (4%)
  other arithmetic  3.04 us (2%)
    ppermute x28, waiting for transfers between devices, swap(): return lax.ppermute(value, axis, pairs)  114 us
    ppermute x28, starting transfers between devices, swap(): return lax.ppermute(value, axis, pairs)  40.2 us
    pallas_call x10, Pallas kernels, call(): pl.pallas_call(kernel, out_shape=out_shape, in_specs=in_specs, out_specs=...  4.48 us
  transfers between devices with their start and end apart: 28, of which 15 were waited for; matrix products, arithmetic and copies ran while one was open for 0% of the time, Pallas kernels for 3%

profile of v1, /device:TPU:0, one launch (start us, length us, event | category | flops | bytes accessed | tf_op | source)
XLA Modules:
  0.0 163.7 jit_solution(13641180490120078982)
XLA Ops:
  0.0 2.9 %collective-permute-start.2 = (bf16[128,2048]{1,0:T(8,128)(2,1)}, bf16[128,2048]{1,0:T(8,128)(2,1)S(1)}, u32[]{:S(2)}, u32[]{:S(2)}) collective-permute-start(bf16[128,2048]{1,0:T(8,128)(2,1)} %refs_0_.1), channel_id=1, source_target_pairs={{0,2},{1,3},{2,0},{3,1},{4,6},{5,7},{6,4},{7,5},{8,10},{9,11},{10,... | collective-permute-start | bytes 1572872 | tf_op jit(solution)/shard_map/ppermute | solution.py:17
  2.9 12.2 %collective-permute-done.2.refs_1_ = bf16[128,2048]{1,0:T(8,128)(2,1)S(1)} collective-permute-done((bf16[128,2048]{1,0:T(8,128)(2,1)}, bf16[128,2048]{1,0:T(8,128)(2,1)S(1)}, u32[]{:S(2)}, u32[]{:S(2)}) %collective-permute-start.2) | collective-permute-done | bytes 524320 | tf_op jit(solution)/shard_map/ppermute | solution.py:17
  15.1 2.1 %pad_maximum_fusion = bf16[256,2048]{1,0:T(8,128)(2,1)} fusion(bf16[128,2048]{1,0:T(8,128)(2,1)S(1)} %collective-permute-done.2.refs_1_, bf16[128,2048]{1,0:T(8,128)(2,1)} %refs_0_.1), kind=kLoop, calls=%fused_computation | loop fusion | flops 2097152 | bytes 2097152 | tf_op jit(solution)/shard_map/concatenate | solution.py:212
  17.4 2.7 %collective-permute-done.3.refs_2_ = bf16[256,2048]{1,0:T(8,128)(2,1)S(1)} collective-permute-done((bf16[256,2048]{1,0:T(8,128)(2,1)}, bf16[256,2048]{1,0:T(8,128)(2,1)S(1)}, u32[]{:S(2)}, u32[]{:S(2)}) %collective-permute-start.3) | collective-permute-done | bytes 1048608 | tf_op jit(solution)/shard_map/ppermute | solution.py:17
  20.8 1.8 %collective-permute-start.4 = (bf16[128,2048]{1,0:T(8,128)(2,1)S(1)}, bf16[128,2048]{1,0:T(8,128)(2,1)S(1)}, u32[]{:S(2)}, u32[]{:S(2)}) collective-permute-start(bf16[128,2048]{1,0:T(8,128)(2,1)S(1)} %shard_map.66), channel_id=1, source_target_pairs={{0,8},{4,12},{8,0},{12,4},{16,24},{20,28},{24,16},{28,20},{1,9},{5... | collective-permute-start | bytes 1572872 | tf_op jit(solution)/shard_map/ppermute | solution.py:17
  22.6 12.2 %collective-permute-done.4 = bf16[128,2048]{1,0:T(8,128)(2,1)S(1)} collective-permute-done((bf16[128,2048]{1,0:T(8,128)(2,1)S(1)}, bf16[128,2048]{1,0:T(8,128)(2,1)S(1)}, u32[]{:S(2)}, u32[]{:S(2)}) %collective-permute-start.4) | collective-permute-done | bytes 524320 | tf_op jit(solution)/shard_map/ppermute | solution.py:17
  36.9 3.6 %collective-permute-start.12 = (bf16[256,512]{1,0:T(8,128)(2,1)S(1)}, bf16[256,512]{1,0:T(8,128)(2,1)S(1)}, u32[]{:S(2)}, u32[]{:S(2)}) collective-permute-start(bf16[256,512]{1,0:T(8,128)(2,1)S(1)} %get-tuple-element.32), channel_id=1, source_target_pairs={{0,28},{4,24},{8,20},{12,16},{16,12},{20,8},{24,4},{28,0},{1,29},{... | collective-permute-start | bytes 786440 | tf_op jit(solution)/shard_map/ppermute | solution.py:17
  42.1 2.0 %collective-permute-start.8 = (bf16[256,512]{1,0:T(8,128)(2,1)S(1)}, bf16[256,512]{1,0:T(8,128)(2,1)S(1)}, u32[]{:S(2)}, u32[]{:S(2)}) collective-permute-start(bf16[256,512]{1,0:T(8,128)(2,1)S(1)} %get-tuple-element.32), channel_id=1, source_target_pairs={{0,12},{4,8},{8,4},{12,0},{16,28},{20,24},{24,20},{28,16},{1,13},{... | collective-permute-start | bytes 786440 | tf_op jit(solution)/shard_map/ppermute | solution.py:17
  44.0 4.9 %collective-permute-done.12.refs_7_ = bf16[256,512]{1,0:T(8,128)(2,1)S(1)} collective-permute-done((bf16[256,512]{1,0:T(8,128)(2,1)S(1)}, bf16[256,512]{1,0:T(8,128)(2,1)S(1)}, u32[]{:S(2)}, u32[]{:S(2)}) %collective-permute-start.12) | collective-permute-done | bytes 262176 | tf_op jit(solution)/shard_map/ppermute | solution.py:17
  48.9 5.6 %collective-permute-start.9 = (bf16[256,512]{1,0:T(8,128)(2,1)S(1)}, bf16[256,512]{1,0:T(8,128)(2,1)S(1)}, u32[]{:S(2)}, u32[]{:S(2)}) collective-permute-start(bf16[256,512]{1,0:T(8,128)(2,1)S(1)} %get-tuple-element.29.refs_0_), channel_id=1, source_target_pairs={{0,16},{4,20},{8,24},{12,28},{16,0},{20,4},{24,8},{28,12},{1,17},{... | collective-permute-start | bytes 786440 | tf_op jit(solution)/shard_map/ppermute | solution.py:17
  54.6 21.6 %collective-permute-done.6.refs_1_ = bf16[256,512]{1,0:T(8,128)(2,1)S(1)} collective-permute-done((bf16[256,512]{1,0:T(8,128)(2,1)S(1)}, bf16[256,512]{1,0:T(8,128)(2,1)S(1)}, u32[]{:S(2)}, u32[]{:S(2)}) %collective-permute-start.6) | collective-permute-done | bytes 262176 | tf_op jit(solution)/shard_map/ppermute | solution.py:17
  76.2 3.7 %collective-permute-start.10 = (bf16[256,512]{1,0:T(8,128)(2,1)S(1)}, bf16[256,512]{1,0:T(8,128)(2,1)S(1)}, u32[]{:S(2)}, u32[]{:S(2)}) collective-permute-start(bf16[256,512]{1,0:T(8,128)(2,1)S(1)} %get-tuple-element.30), channel_id=1, source_target_pairs={{0,20},{4,16},{8,28},{12,24},{16,4},{20,0},{24,12},{28,8},{1,21},{... | collective-permute-start | bytes 786440 | tf_op jit(solution)/shard_map/ppermute | solution.py:17
  80.2 3.6 %collective-permute-start.11 = (bf16[256,512]{1,0:T(8,128)(2,1)S(1)}, bf16[256,512]{1,0:T(8,128)(2,1)S(1)}, u32[]{:S(2)}, u32[]{:S(2)}) collective-permute-start(bf16[256,512]{1,0:T(8,128)(2,1)S(1)} %get-tuple-element.31), channel_id=1, source_target_pairs={{0,24},{4,28},{8,16},{12,20},{16,8},{20,12},{24,0},{28,4},{1,25},{... | collective-permute-start | bytes 786440 | tf_op jit(solution)/shard_map/ppermute | solution.py:17
  83.8 24.6 %collective-permute-done.10.refs_5_ = bf16[256,512]{1,0:T(8,128)(2,1)S(1)} collective-permute-done((bf16[256,512]{1,0:T(8,128)(2,1)S(1)}, bf16[256,512]{1,0:T(8,128)(2,1)S(1)}, u32[]{:S(2)}, u32[]{:S(2)}) %collective-permute-start.10) | collective-permute-done | bytes 262176 | tf_op jit(solution)/shard_map/ppermute | solution.py:17
  110.0 4.2 %collective-permute-done.21.refs_1_ = bf16[128,1024]{1,0:T(8,128)(2,1)S(1)} collective-permute-done((bf16[128,1024]{1,0:T(8,128)(2,1)S(1)}, bf16[128,1024]{1,0:T(8,128)(2,1)S(1)}, u32[]{:S(2)}, u32[]{:S(2)}) %collective-permute-start.21) | collective-permute-done | bytes 262176 | tf_op jit(solution)/shard_map/ppermute | solution.py:17
  116.2 7.9 %collective-permute-done.14.refs_1_ = bf16[128,1024]{1,0:T(8,128)(2,1)S(1)} collective-permute-done((bf16[128,1024]{1,0:T(8,128)(2,1)S(1)}, bf16[128,1024]{1,0:T(8,128)(2,1)S(1)}, u32[]{:S(2)}, u32[]{:S(2)}) %collective-permute-start.14) | collective-permute-done | bytes 262176 | tf_op jit(solution)/shard_map/ppermute | solution.py:17
  124.7 2.0 %shard_map.68 = (bf16[256,256]{1,0:T(8,128)(2,1)S(1)}, bf16[256,256]{1,0:T(8,128)(2,1)S(1)}) custom-call(s32[8]{0:T(128)S(1)} %iota_xor_fusion.where_ref, bf16[256,2048]{1,0:T(8,128)(2,1)S(1)} %pad_maximum_fusion.1.own_ref, bf16[256,2048]{1,0:T(8,128)(2,1)S(1)} %collective-permute-done.5.other_ref, bf16[256,512]{1,0:T(8,128)(2,1)S(1)} %get-tuple-element.29.refs_0_, ...), custom_call_target="tpu_custom_call" | custom-call | flops 1073741824 | bytes 8388608 | tf_op jit(solution)/shard_map/pallas_call | solution.py:239
  128.2 6.2 %collective-permute-done.13.came_ref = bf16[256,256]{1,0:T(8,128)(2,1)S(1)} collective-permute-done((bf16[256,256]{1,0:T(8,128)(2,1)S(1)}, bf16[256,256]{1,0:T(8,128)(2,1)S(1)}, u32[]{:S(2)}, u32[]{:S(2)}) %collective-permute-start.13) | collective-permute-done | bytes 131104 | tf_op jit(solution)/shard_map/ppermute | solution.py:17
  138.1 6.3 %collective-permute-done.24.away_ref = bf16[128,1024]{1,0:T(8,128)(2,1)S(1)} collective-permute-done((bf16[128,1024]{1,0:T(8,128)(2,1)S(1)}, bf16[128,1024]{1,0:T(8,128)(2,1)S(1)}, u32[]{:S(2)}, u32[]{:S(2)}) %collective-permute-start.24) | collective-permute-done | bytes 262176 | tf_op jit(solution)/shard_map/ppermute | solution.py:17
  146.4 2.1 %collective-permute-done = s32[1,128]{1,0:T(1,128)S(1)} collective-permute-done((s32[1,128]{1,0:T(1,128)S(1)}, s32[1,128]{1,0:T(1,128)S(1)}, u32[]{:S(2)}, u32[]{:S(2)}) %collective-permute-start) | collective-permute-done | bytes 544 | tf_op jit(solution)/shard_map/ppermute | solution.py:17
  153.1 1.8 %collective-permute-done.26.refs_2_ = bf16[64,1024]{1,0:T(8,128)(2,1)S(1)} collective-permute-done((bf16[64,1024]{1,0:T(8,128)(2,1)S(1)}, bf16[64,1024]{1,0:T(8,128)(2,1)S(1)}, u32[]{:S(2)}, u32[]{:S(2)}) %collective-permute-start.26) | collective-permute-done | bytes 131104 | tf_op jit(solution)/shard_map/ppermute | solution.py:17
  154.9 1.9 %collective-permute-done.27.refs_3_ = bf16[64,1024]{1,0:T(8,128)(2,1)S(1)} collective-permute-done((bf16[64,1024]{1,0:T(8,128)(2,1)S(1)}, bf16[64,1024]{1,0:T(8,128)(2,1)S(1)}, u32[]{:S(2)}, u32[]{:S(2)}) %collective-permute-start.27) | collective-permute-done | bytes 131104 | tf_op jit(solution)/shard_map/ppermute | solution.py:17
  157.2 3.3 %collective-permute-done.19.refs_2_ = bf16[64,1024]{1,0:T(8,128)(2,1)S(1)} collective-permute-done((bf16[64,1024]{1,0:T(8,128)(2,1)S(1)}, bf16[64,1024]{1,0:T(8,128)(2,1)S(1)}, u32[]{:S(2)}, u32[]{:S(2)}) %collective-permute-start.19) | collective-permute-done | bytes 131104 | tf_op jit(solution)/shard_map/ppermute | solution.py:17
  160.5 1.9 %collective-permute-done.20.refs_3_ = bf16[64,1024]{1,0:T(8,128)(2,1)S(1)} collective-permute-done((bf16[64,1024]{1,0:T(8,128)(2,1)S(1)}, bf16[64,1024]{1,0:T(8,128)(2,1)S(1)}, u32[]{:S(2)}, u32[]{:S(2)}) %collective-permute-start.20) | collective-permute-done | bytes 131104 | tf_op jit(solution)/shard_map/ppermute | solution.py:17
  (63 shorter events, 22.5 us)
Async XLA Ops:
  0.0 15.1 %collective-permute-start.2 = (bf16[128,2048]{1,0:T(8,128)(2,1)}, bf16[128,2048]{1,0:T(8,128)(2,1)S(1)}, u32[]{:S(2)}, u32[]{:S(2)}) collective-permute-start(bf16[128,2048]{1,0:T(8,128)(2,1)} %refs_0_.1), channel_id=1, source_target_pairs={{0,2},{1,3},{2,0},{3,1},{4,6},{5,7},{6,4},{7,5},{8,10},{9,11},{10,... | collective-permute-start | bytes 1572872 | tf_op jit(solution)/shard_map/ppermute | solution.py:17
  20.8 14.0 %collective-permute-start.4 = (bf16[128,2048]{1,0:T(8,128)(2,1)S(1)}, bf16[128,2048]{1,0:T(8,128)(2,1)S(1)}, u32[]{:S(2)}, u32[]{:S(2)}) collective-permute-start(bf16[128,2048]{1,0:T(8,128)(2,1)S(1)} %shard_map.66), channel_id=1, source_target_pairs={{0,8},{4,12},{8,0},{12,4},{16,24},{20,28},{24,16},{28,20},{1,9},{5... | collective-permute-start | bytes 1572872 | tf_op jit(solution)/shard_map/ppermute | solution.py:17
  34.9 89.8 %collective-permute-start.5 = (bf16[256,2048]{1,0:T(8,128)(2,1)S(1)}, bf16[256,2048]{1,0:T(8,128)(2,1)S(1)}, u32[]{:S(2)}, u32[]{:S(2)}) collective-permute-start(bf16[256,2048]{1,0:T(8,128)(2,1)S(1)} %pad_maximum_fusion.1.own_ref), channel_id=1, source_target_pairs={{0,4},{4,0},{8,12},{12,8},{16,20},{20,16},{24,28},{28,24},{1,5},{5... | collective-permute-start | bytes 3145736 | tf_op jit(solution)/shard_map/ppermute | solution.py:17
  36.9 12.0 %collective-permute-start.12 = (bf16[256,512]{1,0:T(8,128)(2,1)S(1)}, bf16[256,512]{1,0:T(8,128)(2,1)S(1)}, u32[]{:S(2)}, u32[]{:S(2)}) collective-permute-start(bf16[256,512]{1,0:T(8,128)(2,1)S(1)} %get-tuple-element.32), channel_id=1, source_target_pairs={{0,28},{4,24},{8,20},{12,16},{16,12},{20,8},{24,4},{28,0},{1,29},{... | collective-permute-start | bytes 786440 | tf_op jit(solution)/shard_map/ppermute | solution.py:17
  40.5 35.6 %collective-permute-start.6 = (bf16[256,512]{1,0:T(8,128)(2,1)S(1)}, bf16[256,512]{1,0:T(8,128)(2,1)S(1)}, u32[]{:S(2)}, u32[]{:S(2)}) collective-permute-start(bf16[256,512]{1,0:T(8,128)(2,1)S(1)} %get-tuple-element.30), channel_id=1, source_target_pairs={{0,4},{4,0},{8,12},{12,8},{16,20},{20,16},{24,28},{28,24},{1,5},{5... | collective-permute-start | bytes 786440 | tf_op jit(solution)/shard_map/ppermute | solution.py:17
  42.0 37.8 %collective-permute-start.7 = (bf16[256,512]{1,0:T(8,128)(2,1)S(1)}, bf16[256,512]{1,0:T(8,128)(2,1)S(1)}, u32[]{:S(2)}, u32[]{:S(2)}) collective-permute-start(bf16[256,512]{1,0:T(8,128)(2,1)S(1)} %get-tuple-element.31), channel_id=1, source_target_pairs={{0,8},{4,12},{8,0},{12,4},{16,24},{20,28},{24,16},{28,20},{1,9},{5... | collective-permute-start | bytes 786440 | tf_op jit(solution)/shard_map/ppermute | solution.py:17
  42.1 38.2 %collective-permute-start.8 = (bf16[256,512]{1,0:T(8,128)(2,1)S(1)}, bf16[256,512]{1,0:T(8,128)(2,1)S(1)}, u32[]{:S(2)}, u32[]{:S(2)}) collective-permute-start(bf16[256,512]{1,0:T(8,128)(2,1)S(1)} %get-tuple-element.32), channel_id=1, source_target_pairs={{0,12},{4,8},{8,4},{12,0},{16,28},{20,24},{24,20},{28,16},{1,13},{... | collective-permute-start | bytes 786440 | tf_op jit(solution)/shard_map/ppermute | solution.py:17
  48.9 34.9 %collective-permute-start.9 = (bf16[256,512]{1,0:T(8,128)(2,1)S(1)}, bf16[256,512]{1,0:T(8,128)(2,1)S(1)}, u32[]{:S(2)}, u32[]{:S(2)}) collective-permute-start(bf16[256,512]{1,0:T(8,128)(2,1)S(1)} %get-tuple-element.29.refs_0_), channel_id=1, source_target_pairs={{0,16},{4,20},{8,24},{12,28},{16,0},{20,4},{24,8},{28,12},{1,17},{... | collective-permute-start | bytes 786440 | tf_op jit(solution)/shard_map/ppermute | solution.py:17
  76.2 32.2 %collective-permute-start.10 = (bf16[256,512]{1,0:T(8,128)(2,1)S(1)}, bf16[256,512]{1,0:T(8,128)(2,1)S(1)}, u32[]{:S(2)}, u32[]{:S(2)}) collective-permute-start(bf16[256,512]{1,0:T(8,128)(2,1)S(1)} %get-tuple-element.30), channel_id=1, source_target_pairs={{0,20},{4,16},{8,28},{12,24},{16,4},{20,0},{24,12},{28,8},{1,21},{... | collective-permute-start | bytes 786440 | tf_op jit(solution)/shard_map/ppermute | solution.py:17
  79.9 34.3 %collective-permute-start.21 = (bf16[128,1024]{1,0:T(8,128)(2,1)S(1)}, bf16[128,1024]{1,0:T(8,128)(2,1)S(1)}, u32[]{:S(2)}, u32[]{:S(2)}) collective-permute-start(bf16[128,1024]{1,0:T(8,128)(2,1)S(1)} %get-tuple-element.42.refs_0_), channel_id=1, source_target_pairs={{0,16},{4,20},{8,24},{12,28},{16,0},{20,4},{24,8},{28,12},{1,17},{... | collective-permute-start | bytes 786440 | tf_op jit(solution)/shard_map/ppermute | solution.py:17
  80.2 34.4 %collective-permute-start.11 = (bf16[256,512]{1,0:T(8,128)(2,1)S(1)}, bf16[256,512]{1,0:T(8,128)(2,1)S(1)}, u32[]{:S(2)}, u32[]{:S(2)}) collective-permute-start(bf16[256,512]{1,0:T(8,128)(2,1)S(1)} %get-tuple-element.31), channel_id=1, source_target_pairs={{0,24},{4,28},{8,16},{12,20},{16,8},{20,12},{24,0},{28,4},{1,25},{... | collective-permute-start | bytes 786440 | tf_op jit(solution)/shard_map/ppermute | solution.py:17
  83.8 40.3 %collective-permute-start.14 = (bf16[128,1024]{1,0:T(8,128)(2,1)S(1)}, bf16[128,1024]{1,0:T(8,128)(2,1)S(1)}, u32[]{:S(2)}, u32[]{:S(2)}) collective-permute-start(bf16[128,1024]{1,0:T(8,128)(2,1)S(1)} %get-tuple-element.35.refs_0_), channel_id=1, source_target_pairs={{0,16},{4,20},{8,24},{12,28},{16,0},{20,4},{24,8},{28,12},{1,17},{... | collective-permute-start | bytes 786440 | tf_op jit(solution)/shard_map/ppermute | solution.py:17
  108.4 19.8 %collective-permute-start.22 = (bf16[128,1024]{1,0:T(8,128)(2,1)S(1)}, bf16[128,1024]{1,0:T(8,128)(2,1)S(1)}, u32[]{:S(2)}, u32[]{:S(2)}) collective-permute-start(bf16[128,1024]{1,0:T(8,128)(2,1)S(1)} %get-tuple-element.42.refs_0_), channel_id=1, source_target_pairs={{0,4},{4,0},{8,12},{12,8},{16,20},{20,16},{24,28},{28,24},{1,5},{5... | collective-permute-start | bytes 786440 | tf_op jit(solution)/shard_map/ppermute | solution.py:17
  114.1 14.1 %collective-permute-start.23 = (bf16[128,1024]{1,0:T(8,128)(2,1)S(1)}, bf16[128,1024]{1,0:T(8,128)(2,1)S(1)}, u32[]{:S(2)}, u32[]{:S(2)}) collective-permute-start(bf16[128,1024]{1,0:T(8,128)(2,1)S(1)} %collective-permute-done.21.refs_1_), channel_id=1, source_target_pairs={{0,4},{4,0},{8,12},{12,8},{16,20},{20,16},{24,28},{28,24},{1,5},{5... | collective-permute-start | bytes 786440 | tf_op jit(solution)/shard_map/ppermute | solution.py:17
  114.6 22.1 %collective-permute-start.15 = (bf16[128,1024]{1,0:T(8,128)(2,1)S(1)}, bf16[128,1024]{1,0:T(8,128)(2,1)S(1)}, u32[]{:S(2)}, u32[]{:S(2)}) collective-permute-start(bf16[128,1024]{1,0:T(8,128)(2,1)S(1)} %get-tuple-element.35.refs_0_), channel_id=1, source_target_pairs={{0,4},{4,0},{8,12},{12,8},{16,20},{20,16},{24,28},{28,24},{1,5},{5... | collective-permute-start | bytes 786440 | tf_op jit(solution)/shard_map/ppermute | solution.py:17
  124.1 12.6 %collective-permute-start.16 = (bf16[128,1024]{1,0:T(8,128)(2,1)S(1)}, bf16[128,1024]{1,0:T(8,128)(2,1)S(1)}, u32[]{:S(2)}, u32[]{:S(2)}) collective-permute-start(bf16[128,1024]{1,0:T(8,128)(2,1)S(1)} %collective-permute-done.14.refs_1_), channel_id=1, source_target_pairs={{0,4},{4,0},{8,12},{12,8},{16,20},{20,16},{24,28},{28,24},{1,5},{5... | collective-permute-start | bytes 786440 | tf_op jit(solution)/shard_map/ppermute | solution.py:17
  126.7 7.7 %collective-permute-start.13 = (bf16[256,256]{1,0:T(8,128)(2,1)S(1)}, bf16[256,256]{1,0:T(8,128)(2,1)S(1)}, u32[]{:S(2)}, u32[]{:S(2)}) collective-permute-start(bf16[256,256]{1,0:T(8,128)(2,1)S(1)} %get-tuple-element.34), channel_id=1, source_target_pairs={{0,4},{4,0},{8,12},{12,8},{16,20},{20,16},{24,28},{28,24},{1,5},{5... | collective-permute-start | bytes 393224 | tf_op jit(solution)/shard_map/ppermute | solution.py:17
  135.1 9.3 %collective-permute-start.24 = (bf16[128,1024]{1,0:T(8,128)(2,1)S(1)}, bf16[128,1024]{1,0:T(8,128)(2,1)S(1)}, u32[]{:S(2)}, u32[]{:S(2)}) collective-permute-start(bf16[128,1024]{1,0:T(8,128)(2,1)S(1)} %get-tuple-element.44), channel_id=1, source_target_pairs={{0,8},{4,12},{8,0},{12,4},{16,24},{20,28},{24,16},{28,20},{1,9},{5... | collective-permute-start | bytes 786440 | tf_op jit(solution)/shard_map/ppermute | solution.py:17
  137.4 13.0 %collective-permute-start.17 = (bf16[128,1024]{1,0:T(8,128)(2,1)S(1)}, bf16[128,1024]{1,0:T(8,128)(2,1)S(1)}, u32[]{:S(2)}, u32[]{:S(2)}) collective-permute-start(bf16[128,1024]{1,0:T(8,128)(2,1)S(1)} %get-tuple-element.37), channel_id=1, source_target_pairs={{0,8},{4,12},{8,0},{12,4},{16,24},{20,28},{24,16},{28,20},{1,9},{5... | collective-permute-start | bytes 786440 | tf_op jit(solution)/shard_map/ppermute | solution.py:17
  144.8 7.8 %collective-permute-start.25 = (bf16[64,1024]{1,0:T(8,128)(2,1)S(1)}, bf16[64,1024]{1,0:T(8,128)(2,1)S(1)}, u32[]{:S(2)}, u32[]{:S(2)}) collective-permute-start(bf16[64,1024]{1,0:T(8,128)(2,1)S(1)} %get-tuple-element.46), channel_id=1, source_target_pairs={{0,1},{1,0},{2,3},{3,2},{4,5},{5,4},{6,7},{7,6},{8,9},{9,8},{10,11... | collective-permute-start | bytes 393224 | tf_op jit(solution)/shard_map/ppermute | solution.py:17
  150.1 6.7 %collective-permute-start.27 = (bf16[64,1024]{1,0:T(8,128)(2,1)S(1)}, bf16[64,1024]{1,0:T(8,128)(2,1)S(1)}, u32[]{:S(2)}, u32[]{:S(2)}) collective-permute-start(bf16[64,1024]{1,0:T(8,128)(2,1)S(1)} %get-tuple-element.48), channel_id=1, source_target_pairs={{0,3},{1,2},{2,1},{3,0},{4,7},{5,6},{6,5},{7,4},{8,11},{9,10},{10,... | collective-permute-start | bytes 393224 | tf_op jit(solution)/shard_map/ppermute | solution.py:17
  150.8 6.5 %collective-permute-start.18 = (bf16[64,1024]{1,0:T(8,128)(2,1)S(1)}, bf16[64,1024]{1,0:T(8,128)(2,1)S(1)}, u32[]{:S(2)}, u32[]{:S(2)}) collective-permute-start(bf16[64,1024]{1,0:T(8,128)(2,1)S(1)} %get-tuple-element.39), channel_id=1, source_target_pairs={{0,1},{1,0},{2,3},{3,2},{4,5},{5,4},{6,7},{7,6},{8,9},{9,8},{10,11... | collective-permute-start | bytes 393224 | tf_op jit(solution)/shard_map/ppermute | solution.py:17
  151.2 9.3 %collective-permute-start.19 = (bf16[64,1024]{1,0:T(8,128)(2,1)S(1)}, bf16[64,1024]{1,0:T(8,128)(2,1)S(1)}, u32[]{:S(2)}, u32[]{:S(2)}) collective-permute-start(bf16[64,1024]{1,0:T(8,128)(2,1)S(1)} %get-tuple-element.40), channel_id=1, source_target_pairs={{0,2},{1,3},{2,0},{3,1},{4,6},{5,7},{6,4},{7,5},{8,10},{9,11},{10,... | collective-permute-start | bytes 393224 | tf_op jit(solution)/shard_map/ppermute | solution.py:17
  152.6 9.7 %collective-permute-start.20 = (bf16[64,1024]{1,0:T(8,128)(2,1)S(1)}, bf16[64,1024]{1,0:T(8,128)(2,1)S(1)}, u32[]{:S(2)}, u32[]{:S(2)}) collective-permute-start(bf16[64,1024]{1,0:T(8,128)(2,1)S(1)} %get-tuple-element.41), channel_id=1, source_target_pairs={{0,3},{1,2},{2,1},{3,0},{4,7},{5,6},{6,5},{7,4},{8,11},{9,10},{10,... | collective-permute-start | bytes 393224 | tf_op jit(solution)/shard_map/ppermute | solution.py:17
  (10 other events, 106.2 us)

commit v2 on v1

v2 whole, which is shorter than its diff:
```python
import functools

import jax
import jax.numpy as jnp
from jax import lax
from jax.experimental import pallas as pl
from jax.experimental.pallas import tpu as pltpu
from jax.sharding import PartitionSpec as P

SHARES = (5, 3)
OPENING_LIMIT = 60 * 2**20
F32 = jnp.float32
BF16 = jnp.bfloat16


def swap(value, axis, mask):
    pairs = [(source, source ^ mask) for source in range(lax.axis_size(axis))]
    return lax.ppermute(value, axis, pairs)


def call(kernel, out_shape, *args, wait=(), flops=0, scalars=0):
    args = (*args[:scalars], *wait, *args[scalars:])
    in_specs = [pl.BlockSpec(memory_space=pltpu.SMEM)] * scalars
    in_specs += [pl.BlockSpec(memory_space=pl.ANY)] * len(wait)
    in_specs += [pl.BlockSpec(memory_space=pltpu.VMEM)] * (len(args) - scalars - len(wait))
    outs = out_shape if isinstance(out_shape, (list, tuple)) else [out_shape]
    size = sum(a.size * a.dtype.itemsize for a in (*args, *outs))

    def body(*refs):
        kernel(*refs[:scalars], *refs[scalars + len(wait) :])

    return pl.pallas_call(
        body,
        out_shape=out_shape,
        in_specs=in_specs,
        out_specs=jax.tree.map(lambda _: pl.BlockSpec(memory_space=pltpu.VMEM), out_shape),
        compiler_params=pltpu.CompilerParams(vmem_limit_bytes=4 * size + 2**23),
        cost_estimate=pl.CostEstimate(flops=flops, bytes_accessed=size, transcendentals=0),
    )(*args)


def shape(*dims, dtype=BF16):
    return jax.ShapeDtypeStruct(dims, dtype)


def dot(a, b):
    return jnp.dot(a, b, preferred_element_type=F32)


def opening(bit_ref, gate_ref, up_ref, same_ref, other_ref, sem):
    pairs = sem.shape[0] // 4
    wide = gate_ref.shape[2] // (2 * pairs)
    copies = []
    for flip, target in ((0, same_ref), (1, other_ref)):
        at = 0
        for ref in (gate_ref, up_ref):
            for j in range(pairs):
                start = pl.multiple_of((2 * j + (bit_ref[0] ^ flip)) * wide, 128)
                copies.append(
                    pltpu.make_async_copy(
                        ref.at[0, :, pl.ds(start, wide)], target.at[:, at : at + wide], sem.at[len(copies)]
                    )
                )
                at += wide
    for copy in copies:
        copy.start()
    for copy in copies:
        copy.wait()


def hand(in_ref, out_ref):
    out_ref[...] = in_ref[...]


def ranks_of(hits):
    c = hits.shape[1]
    before = lax.broadcasted_iota(jnp.int32, (c, c), 0) < lax.broadcasted_iota(jnp.int32, (c, c), 1)
    return dot(hits.astype(BF16), before.astype(BF16)).astype(jnp.int32)


def own_tables(expert_ref, rows_ref, pick_ref, place_ref, tag_ref, *, experts, tok_dev):
    rows = rows_ref[...]
    capacity = rows.shape[1]
    block = (rows // tok_dev) ^ expert_ref[0]
    local = rows % tok_dev
    bits = experts.bit_length() - 1
    seat = jnp.zeros_like(block)
    for bit in range(bits):
        seat = seat | (((block >> bit) & 1) << (bits - 1 - bit))
    place = seat * tok_dev + local
    count = experts * tok_dev
    pick_ref[...] = (lax.broadcasted_iota(jnp.int32, (count, capacity), 0) == place).astype(BF16)
    hot = lax.broadcasted_iota(jnp.int32, (experts, capacity), 0) == block
    rank = jnp.sum(jnp.where(hot, ranks_of(hot.astype(F32)), 0), axis=0, keepdims=True)
    most = tok_dev // 2
    position = block * most + rank
    here = lax.broadcasted_iota(jnp.int32, (experts * most, capacity), 0) == position
    place_ref[...] = here.astype(BF16)
    number = jnp.sum(jnp.where(here, local + 1, 0).astype(F32), axis=1, keepdims=True)
    tag_ref[...] = jnp.broadcast_to(number, tag_ref.shape).astype(BF16)


def pick_rows(pick_ref, *refs):
    out_ref = refs[-1]
    total, start = 0.0, 0
    for ref in refs[:-1]:
        rows = ref.shape[0]
        total = total + lax.dot_general(
            pick_ref[start : start + rows, :],
            ref[...],
            (((0,), (0,)), ((), ())),
            preferred_element_type=F32,
        )
        start += rows
    out_ref[...] = total.astype(BF16)


def cut(down_ref, out_ref, *, start):
    out_ref[...] = down_ref[0, :, start : start + out_ref.shape[1]]


def hidden_units(where_ref, own_ref, far_ref, *refs, pairs):
    *weights, out_ref, total = refs
    capacity = own_ref.shape[0]
    rows = weights[0].shape[0]
    for mask, block in enumerate(weights):
        columns = pl.ds(pl.multiple_of(where_ref[mask] * rows, min(rows, 256)), rows)
        for side, ref in enumerate((own_ref, far_ref)):
            lines = pl.ds(side * capacity, capacity)
            product = dot(ref[:, columns], block[...])
            if mask == 0:
                total[lines, :] = product
            else:
                total[lines, :] += product
    half = total.shape[1] // 2
    if pairs == 0:
        gate, up = total[:, :half], total[:, half:]
        out_ref[...] = (gate / (1.0 + jnp.exp(-gate)) * up).astype(BF16)
        return
    block = half // (2 * pairs)
    device = where_ref[0]
    for y in range(2):
        for j in range(pairs):
            at = (2 * ((device // 4) ^ j) + ((device % 2) ^ y)) * block
            first = pl.ds(pl.multiple_of(at, 128), block)
            second = pl.ds(pl.multiple_of(half + at, 128), block)
            gate, up = total[:, first], total[:, second]
            at = (y * pairs + j) * block
            out_ref[:, at : at + block] = (gate / (1.0 + jnp.exp(-gate)) * up).astype(BF16)


def down_units(hidden_ref, *refs, places):
    parts, (out_ref, away_ref) = refs[:-2], refs[-2:]
    capacity, step = out_ref.shape
    for side, target in enumerate((out_ref, away_ref)):
        lines = pl.ds(side * capacity, capacity)
        total, unit = 0.0, 0
        for part, at in zip(parts, places):
            rows = part.shape[0]
            total = total + dot(hidden_ref[lines, unit : unit + rows], part[:, at : at + step])
            unit += rows
        target[...] = total.astype(target.dtype)


def weigh(place_ref, tag_ref, weights_ref, out_ref, away_ref, *sent_refs):
    total = out_ref[...] + away_ref[...].astype(F32)
    contribution = (weights_ref[...] * total).astype(BF16)
    step = total.shape[1]
    most, wide = sent_refs[0].shape
    for block, ref in enumerate(sent_refs):
        lines = pl.ds(block * most, most)
        ref[:, :step] = dot(place_ref[lines, :], contribution).astype(BF16)
        if wide > step:
            ref[:, step:] = tag_ref[lines, :]


def mix(*refs, step):
    returned, (select_ref, out_ref) = refs[:-2], refs[-2:]
    most, tok_dev = returned[0].shape[0], out_ref.shape[0]
    total = 0.0
    for block, ref in enumerate(returned):
        number = ref[:, step : step + 1].astype(jnp.int32) - 1
        table = (lax.broadcasted_iota(jnp.int32, (most, tok_dev), 1) == number).astype(BF16)
        select_ref[block * most : (block + 1) * most, :] = table
        total = total + lax.dot_general(
            table, ref[:, :step], (((0,), (0,)), ((), ())), preferred_element_type=F32
        )
    out_ref[...] = total.astype(BF16)


def mix_more(select_ref, *refs, ready):
    done, returned, out_ref = refs[:ready], refs[ready:-1], refs[-1]
    most = returned[0].shape[0]
    start = 0
    for ref in done:
        out_ref[:, start : start + ref.shape[1]] = ref[...]
        start += ref.shape[1]
    total = 0.0
    for block, ref in enumerate(returned):
        total = total + lax.dot_general(
            select_ref[block * most : (block + 1) * most, :],
            ref[...],
            (((0,), (0,)), ((), ())),
            preferred_element_type=F32,
        )
    out_ref[:, start:] = total.astype(BF16)


def per_device(tokens, choice_rows, gate_weights, w_gate, w_up, w_down):
    experts = lax.axis_size("expert")
    replicas = lax.axis_size("dp")
    expert = lax.axis_index("expert").astype(jnp.int32)
    replica = lax.axis_index("dp").astype(jnp.int32)
    tok_dev, width = tokens.shape
    most = tok_dev // 2
    own_rows = choice_rows[0]
    capacity = own_rows.shape[1]
    rows_shard, units = w_gate.shape[1:]
    block = units // replicas

    limit = 16 * 2**20 if capacity <= 128 else 48 * 2**20
    starts = [sum(SHARES[:i]) * width // sum(SHARES) for i in range(len(SHARES) + 1)]
    steps = [end - start for start, end in zip(starts, starts[1:])]
    down_rows = w_down.shape[1]
    pairs = replicas // 4
    zbit = replica // 2 % 2
    whole_lanes = block % 128 == 0
    if whole_lanes:
        same_units, other_units = pl.pallas_call(
            opening,
            out_shape=[shape(rows_shard, units)] * 2,
            in_specs=[pl.BlockSpec(memory_space=pltpu.SMEM)] + [pl.BlockSpec(memory_space=pl.ANY)] * 2,
            out_specs=[pl.BlockSpec(memory_space=pltpu.VMEM)] * 2,
            scratch_shapes=[pltpu.SemaphoreType.DMA((4 * pairs,))],
            compiler_params=pltpu.CompilerParams(vmem_limit_bytes=OPENING_LIMIT),
            cost_estimate=pl.CostEstimate(flops=0, bytes_accessed=2**21, transcendentals=0),
        )(zbit[None], w_gate, w_up)
    else:
        same_units, other_units = (
            jnp.concatenate(
                [
                    lax.dynamic_index_in_dim(
                        w[0].reshape(rows_shard, pairs, 2, 2 * block), zbit ^ flip, axis=2, keepdims=False
                    ).reshape(rows_shard, units // 2)
                    for w in (w_gate, w_up)
                ],
                axis=1,
            )
            for flip in (0, 1)
        )
    far = [mask for mask in range(replicas - 2, 2, -2)]
    weights = {0: same_units}
    weights[1] = swap(same_units, "dp", 1)
    for mask in far[::2]:
        weights[mask] = swap(other_units, "dp", mask)

    group = [tokens]
    bit = experts // 2
    while bit > 0:
        if bit == 1:
            ready = group[-1]
        group += [swap(x, "expert", bit) for x in group]
        bit //= 2
    late_units = call(hand, shape(rows_shard, units), same_units, wait=[ready])
    for mask in far[1::2]:
        weights[mask] = swap(late_units, "dp", mask)
    pick_hot, place_hot, tags = call(
        functools.partial(own_tables, experts=experts, tok_dev=tok_dev),
        [shape(experts * tok_dev, capacity), shape(experts * most, capacity), shape(experts * most, 128)],
        expert[None],
        own_rows,
        scalars=1,
    )
    picked = call(
        pick_rows,
        shape(capacity, width),
        pick_hot,
        *group,
        flops=2 * experts * tok_dev * capacity * width,
    )
    picked_z = swap(picked, "dp", 2)
    weights[2] = swap(other_units, "dp", 2)
    down_y = swap(w_down[0], "dp", 1)
    for mask in [2, *far]:
        weights[mask + 1] = swap(weights[mask], "dp", 1)

    down = []
    for index in range(len(SHARES)):
        piece = call(
            functools.partial(cut, start=starts[index]),
            shape(down_rows, steps[index]),
            w_down,
            wait=[weights[far[min(index, len(far) - 1)]]],
        )
        own, bit = [piece], 4
        while bit < replicas:
            have = own[0] if len(own) == 1 else jnp.concatenate(own, axis=0)
            own.append(swap(have, "dp", bit))
            bit *= 2
        down.append(own[1:])

    arrays = [weights[mask] for mask in range(replicas)]
    order = replica ^ jnp.arange(replicas, dtype=jnp.int32)
    if rows_shard % 128 != 0:
        arrays = [jnp.take(jnp.stack(arrays), order, axis=0).reshape(-1, units)]
        order = jnp.zeros((1,), jnp.int32)
    hidden = pl.pallas_call(
        functools.partial(hidden_units, pairs=pairs if whole_lanes else 0),
        out_shape=shape(2 * capacity, units // 2),
        in_specs=[pl.BlockSpec(memory_space=pltpu.SMEM)]
        + [pl.BlockSpec(memory_space=pltpu.VMEM)] * (2 + len(arrays)),
        out_specs=pl.BlockSpec(memory_space=pltpu.VMEM),
        scratch_shapes=[pltpu.VMEM((2 * capacity, units), F32)],
        compiler_params=pltpu.CompilerParams(vmem_limit_bytes=limit),
        cost_estimate=pl.CostEstimate(
            flops=4 * capacity * width * units, bytes_accessed=2**23, transcendentals=0
        ),
    )(order, picked, picked_z, *arrays)
    if not whole_lanes:
        index = jnp.arange(2 * pairs, dtype=jnp.int32)
        turn = 2 * ((replica // 4) ^ (index % pairs)) + ((replica % 2) ^ (index // pairs))
        hidden = jnp.take(hidden.reshape(-1, 2 * pairs, block), turn, axis=1).reshape(hidden.shape)

    gate_column = gate_weights[0, 0][:, None]
    results = []
    for index, (start, step, far_rows) in enumerate(zip(starts, steps, down)):
        parts = [w_down[0], *far_rows, down_y, *[swap(x, "dp", 1) for x in far_rows]]
        out, away = call(
            functools.partial(down_units, places=[start if x.shape[1] == width else 0 for x in parts]),
            [shape(capacity, step, dtype=F32), shape(capacity, step)],
            hidden,
            *parts,
            flops=2 * capacity * units * step,
        )
        extra = 128 if index == 0 else 0
        sent = call(
            weigh,
            [shape(most, step + extra)] * experts,
            place_hot,
            tags,
            gate_column,
            out,
            swap(away, "dp", 2),
            flops=2 * experts * most * capacity * step,
        )
        returned = [sent[0]] + [swap(sent[c], "expert", c) for c in range(1, experts)]
        flops = 2 * experts * most * tok_dev * step
        if index == 0:
            select, result = call(
                functools.partial(mix, step=step),
                [shape(experts * most, tok_dev), shape(tok_dev, step)],
                *returned,
                flops=flops,
            )
            results.append(result)
        else:
            last = index == len(SHARES) - 1
            ready = results if last else []
            results.append(
                call(
                    functools.partial(mix_more, ready=len(ready)),
                    shape(tok_dev, width if last else step),
                    select,
                    *ready,
                    *returned,
                    flops=flops,
                )
            )
    return results[-1]


def solution(mesh):
    return jax.shard_map(
        per_device,
        mesh=mesh,
        in_specs=(
            P(("dp", "expert"), None),
            P("dp", "expert", None),
            P("dp", "expert", None),
            P("expert", "dp", None),
            P("expert", "dp", None),
            P("expert", "dp", None),
        ),
        out_specs=P(("dp", "expert"), None),
        check_vma=False,
    )
```

time: 164 us -> 120 us (0.73)
  waiting for transfers between devices: 114 us -> 69 us
  starting transfers between devices: 40.2 us -> 34.1 us
  Pallas kernels: 6.47 us -> 12.2 us
  local copies, waits for them, and re-layouts: 0.17 us -> 4.3 us
  other arithmetic: 3.04 us -> 0.01 us
    ppermute x28 -> x24, waiting for transfers between devices: 114 us -> 69 us  [swap(): return lax.ppermute(value, axis, pairs)]
    ppermute x28 -> x24, starting transfers between devices: 40.2 us -> 34.1 us  [swap(): return lax.ppermute(value, axis, pairs)]
    pallas_call x11 -> x13, Pallas kernels: 6.47 us -> 12.2 us  [the longest x11 6.95 us: call(): pl.pallas_call(body, out_shape=out_shape, in_specs=in_specs, out_specs=ja...]
    unnamed x12 -> x20, local copies, waits for them, and re-layouts: 0.03 us -> 4.19 us
    concatenate x5 -> x0, other arithmetic: 3.04 us -> none  [the longest x1 2.11 us: per_device(): have = group[0] if len(group) == 1 else jnp.concatenate(group, axis=0)]
  transfers between devices with their start and end apart: 28 -> 24, of which waited for: 15 -> 14; matrix products, arithmetic and copies ran while one was open for 0% -> 0% of each run, Pallas kernels for 3% -> 9%
where the time goes in v2:
time: 120 us
  waiting for transfers between devices  69 us (58%)
  starting transfers between devices  34.1 us (28%)
  Pallas kernels  12.2 us (10%)
  local copies, waits for them, and re-layouts  4.3 us (4%)
    ppermute x24, waiting for transfers between devices, swap(): return lax.ppermute(value, axis, pairs)  69 us
    ppermute x24, starting transfers between devices, swap(): return lax.ppermute(value, axis, pairs)  34.1 us
    pallas_call x11, Pallas kernels, call(): pl.pallas_call(body, out_shape=out_shape, in_specs=in_specs, out_specs=ja...  6.95 us
    unnamed x20, local copies, waits for them, and re-layouts  4.19 us
    pallas_call x1, Pallas kernels, per_device(): pl.pallas_call(functools.partial(hidden_units, pairs=pairs if whole_lanes...  2.83 us
    pallas_call x1, Pallas kernels, per_device(): pl.pallas_call(opening, out_shape=[shape(rows_shard, units)] * 2, in_spec...  2.4 us
  transfers between devices with their start and end apart: 24, of which 14 were waited for; matrix products, arithmetic and copies ran while one was open for 0% of the time, Pallas kernels for 9%

profile of v2, /device:TPU:0, one launch (start us, length us, event | category | flops | bytes accessed | tf_op | source)
XLA Modules:
  0.0 119.7 jit_solution(843087546039352267)
XLA Ops:
  0.0 2.9 %collective-permute-start = (bf16[128,2048]{1,0:T(8,128)(2,1)}, bf16[128,2048]{1,0:T(8,128)(2,1)S(1)}, u32[]{:S(2)}, u32[]{:S(2)}) collective-permute-start(bf16[128,2048]{1,0:T(8,128)(2,1)} %refs_1_.3), channel_id=1, source_target_pairs={{0,2},{1,3},{2,0},{3,1},{4,6},{5,7},{6,4},{7,5},{8,10},{9,11},{10,... | collective-permute-start | bytes 1572872 | tf_op jit(solution)/shard_map/ppermute | solution.py:18
  2.9 2.4 %shard_map.66 = (bf16[256,1024]{1,0:T(8,128)(2,1)}, bf16[256,1024]{1,0:T(8,128)(2,1)}) custom-call(s32[1]{0:T(128)} %bitcast.3.bit_ref, bf16[1,256,1024]{2,1,0:T(8,128)(2,1)} %gate_ref.1, bf16[1,256,1024]{2,1,0:T(8,128)(2,1)} %up_ref.1), custom_call_target="tpu_custom_call" | custom-call | bytes 2097152 | tf_op jit(solution)/shard_map/pallas_call | solution.py:229
  5.4 3.7 %collective-permute-start.9 = (bf16[256,1024]{1,0:T(8,128)(2,1)}, bf16[256,1024]{1,0:T(8,128)(2,1)S(1)}, u32[]{:S(2)}, u32[]{:S(2)}) collective-permute-start(bf16[256,1024]{1,0:T(8,128)(2,1)} %get-tuple-element.28), channel_id=1, source_target_pairs={{0,24},{4,28},{8,16},{12,20},{16,8},{20,12},{24,0},{28,4},{1,25},{... | collective-permute-start | bytes 1572872 | tf_op jit(solution)/shard_map/ppermute | solution.py:18
  9.0 6.0 %collective-permute-done.refs_2_.refs_0_ = bf16[128,2048]{1,0:T(8,128)(2,1)S(1)} collective-permute-done((bf16[128,2048]{1,0:T(8,128)(2,1)}, bf16[128,2048]{1,0:T(8,128)(2,1)S(1)}, u32[]{:S(2)}, u32[]{:S(2)}) %collective-permute-start) | collective-permute-done | bytes 524320 | tf_op jit(solution)/shard_map/ppermute | solution.py:18
  15.1 1.8 %collective-permute-start.4 = (bf16[256,1024]{1,0:T(8,128)(2,1)}, bf16[256,1024]{1,0:T(8,128)(2,1)}, u32[]{:S(2)}, u32[]{:S(2)}) collective-permute-start(bf16[256,1024]{1,0:T(8,128)(2,1)} %get-tuple-element.27.refs_1_.refs_0_), channel_id=1, source_target_pairs={{0,4},{4,0},{8,12},{12,8},{16,20},{20,16},{24,28},{28,24},{1,5},{5... | collective-permute-start | bytes 1572872 | tf_op jit(solution)/shard_map/ppermute | solution.py:18
  18.0 4.4 %collective-permute-done.9.refs_6_.refs_0_ = bf16[256,1024]{1,0:T(8,128)(2,1)S(1)} collective-permute-done((bf16[256,1024]{1,0:T(8,128)(2,1)}, bf16[256,1024]{1,0:T(8,128)(2,1)S(1)}, u32[]{:S(2)}, u32[]{:S(2)}) %collective-permute-start.9) | collective-permute-done | bytes 524320 | tf_op jit(solution)/shard_map/ppermute | solution.py:18
  22.3 10.5 %collective-permute-start.7 = (bf16[256,1024]{1,0:T(8,128)(2,1)S(1)}, bf16[256,1024]{1,0:T(8,128)(2,1)S(1)}, u32[]{:S(2)}, u32[]{:S(2)}) collective-permute-start(bf16[256,1024]{1,0:T(8,128)(2,1)S(1)} %shard_map.67), channel_id=1, source_target_pairs={{0,16},{4,20},{8,24},{12,28},{16,0},{20,4},{24,8},{28,12},{1,17},{... | collective-permute-start | bytes 1572872 | tf_op jit(solution)/shard_map/ppermute | solution.py:18
  33.7 1.5 %collective-permute-start.6 = (bf16[256,1024]{1,0:T(8,128)(2,1)}, bf16[256,1024]{1,0:T(8,128)(2,1)}, u32[]{:S(2)}, u32[]{:S(2)}) collective-permute-start(bf16[256,1024]{1,0:T(8,128)(2,1)} %collective-permute-done.5.refs_2_), channel_id=1, source_target_pairs={{0,4},{4,0},{8,12},{12,8},{16,20},{20,16},{24,28},{28,24},{1,5},{5... | collective-permute-start | bytes 1572872 | tf_op jit(solution)/shard_map/ppermute | solution.py:18
  38.3 1.8 %shard_map.65.own_ref = bf16[128,2048]{1,0:T(8,128)(2,1)S(1)} custom-call(bf16[512,128]{1,0:T(8,128)(2,1)S(1)} %get-tuple-element.26.refs_0_, bf16[128,2048]{1,0:T(8,128)(2,1)S(1)} %copy-done.3, bf16[128,2048]{1,0:T(8,128)(2,1)S(1)} %collective-permute-done.refs_2_.refs_0_, bf16[128,2048]{1,0:T(8,128)(2,1)S(1)} %copy-done.5, ...), custom_call_target="tpu_custom_call" | custom-call | flops 268435456 | bytes 2752512 | tf_op jit(solution)/shard_map/pallas_call | solution.py:32
  40.1 2.0 %collective-permute-start.3 = (bf16[128,2048]{1,0:T(8,128)(2,1)S(1)}, bf16[128,2048]{1,0:T(8,128)(2,1)S(1)}, u32[]{:S(2)}, u32[]{:S(2)}) collective-permute-start(bf16[128,2048]{1,0:T(8,128)(2,1)S(1)} %shard_map.65.own_ref), channel_id=1, source_target_pairs={{0,8},{4,12},{8,0},{12,4},{16,24},{20,28},{24,16},{28,20},{1,9},{5... | collective-permute-start | bytes 1572872 | tf_op jit(solution)/shard_map/ppermute | solution.py:18
  42.1 21.6 %collective-permute-done.7.refs_4_.refs_0_ = bf16[256,1024]{1,0:T(8,128)(2,1)S(1)} collective-permute-done((bf16[256,1024]{1,0:T(8,128)(2,1)S(1)}, bf16[256,1024]{1,0:T(8,128)(2,1)S(1)}, u32[]{:S(2)}, u32[]{:S(2)}) %collective-permute-start.7) | collective-permute-done | bytes 524320 | tf_op jit(solution)/shard_map/ppermute | solution.py:18
  63.6 1.5 %collective-permute-start.8 = (bf16[256,1024]{1,0:T(8,128)(2,1)S(1)}, bf16[256,1024]{1,0:T(8,128)(2,1)S(1)}, u32[]{:S(2)}, u32[]{:S(2)}) collective-permute-start(bf16[256,1024]{1,0:T(8,128)(2,1)S(1)} %collective-permute-done.7.refs_4_.refs_0_), channel_id=1, source_target_pairs={{0,4},{4,0},{8,12},{12,8},{16,20},{20,16},{24,28},{28,24},{1,5},{5... | collective-permute-start | bytes 1572872 | tf_op jit(solution)/shard_map/ppermute | solution.py:18
  65.1 3.9 %collective-permute-done.11.refs_2_ = bf16[128,1280]{1,0:T(8,128)(2,1)} collective-permute-done((bf16[128,1280]{1,0:T(8,128)(2,1)S(1)}, bf16[128,1280]{1,0:T(8,128)(2,1)}, u32[]{:S(2)}, u32[]{:S(2)}) %collective-permute-start.11) | collective-permute-done | bytes 327712 | tf_op jit(solution)/shard_map/ppermute | solution.py:18
  71.2 7.0 %collective-permute-done.8.refs_5_ = bf16[256,1024]{1,0:T(8,128)(2,1)S(1)} collective-permute-done((bf16[256,1024]{1,0:T(8,128)(2,1)S(1)}, bf16[256,1024]{1,0:T(8,128)(2,1)S(1)}, u32[]{:S(2)}, u32[]{:S(2)}) %collective-permute-start.8) | collective-permute-done | bytes 524320 | tf_op jit(solution)/shard_map/ppermute | solution.py:18
  78.2 2.8 %shard_map.68.refs_0_ = bf16[256,512]{1,0:T(8,128)(2,1)S(1)} custom-call(s32[8]{0:T(128)S(1)} %iota_xor_fusion.where_ref, bf16[128,2048]{1,0:T(8,128)(2,1)S(1)} %shard_map.65.own_ref, bf16[128,2048]{1,0:T(8,128)(2,1)S(1)} %collective-permute-done.3.far_ref, bf16[256,1024]{1,0:T(8,128)(2,1)S(1)} %copy-done.2, ...), custom_call_target="tpu_custom_call" | custom-call | flops 1073741824 | bytes 8388608 | tf_op jit(solution)/shard_map/pallas_call | solution.py:307
  81.1 7.9 %collective-permute-done.12.refs_3_ = bf16[128,2048]{1,0:T(8,128)(2,1)S(1)} collective-permute-done((bf16[128,2048]{1,0:T(8,128)(2,1)S(1)}, bf16[128,2048]{1,0:T(8,128)(2,1)S(1)}, u32[]{:S(2)}, u32[]{:S(2)}) %collective-permute-start.12) | collective-permute-done | bytes 524320 | tf_op jit(solution)/shard_map/ppermute | solution.py:18
  88.9 3.5 %collective-permute-done.13.refs_4_ = bf16[128,1280]{1,0:T(8,128)(2,1)S(1)} collective-permute-done((bf16[128,1280]{1,0:T(8,128)(2,1)}, bf16[128,1280]{1,0:T(8,128)(2,1)S(1)}, u32[]{:S(2)}, u32[]{:S(2)}) %collective-permute-start.13) | collective-permute-done | bytes 327712 | tf_op jit(solution)/shard_map/ppermute | solution.py:18
  92.4 1.8 %shard_map.70 = (f32[128,1280]{1,0:T(8,128)S(1)}, bf16[128,1280]{1,0:T(8,128)(2,1)S(1)}) custom-call(bf16[256,512]{1,0:T(8,128)(2,1)S(1)} %shard_map.68.refs_0_, bf16[128,2048]{1,0:T(8,128)(2,1)S(1)} %bitcast.6, bf16[128,1280]{1,0:T(8,128)(2,1)} %collective-permute-done.11.refs_2_, bf16[128,2048]{1,0:T(8,128)(2,1)S(1)} %collective-permute-done.12.refs_3_, ...), custom_call_target="tpu_custom_call" | custom-call | flops 335544320 | bytes 2949120 | tf_op jit(solution)/shard_map/pallas_call | solution.py:32
  94.3 1.6 %collective-permute-start.19 = (bf16[128,768]{1,0:T(8,128)(2,1)S(1)}, bf16[128,768]{1,0:T(8,128)(2,1)S(1)}, u32[]{:S(2)}, u32[]{:S(2)}) collective-permute-start(bf16[128,768]{1,0:T(8,128)(2,1)S(1)} %collective-permute-done.18.refs_2_), channel_id=1, source_target_pairs={{0,4},{4,0},{8,12},{12,8},{16,20},{20,16},{24,28},{28,24},{1,5},{5... | collective-permute-start | bytes 589832 | tf_op jit(solution)/shard_map/ppermute | solution.py:18
  95.9 4.2 %collective-permute-done.19.refs_4_ = bf16[128,768]{1,0:T(8,128)(2,1)S(1)} collective-permute-done((bf16[128,768]{1,0:T(8,128)(2,1)S(1)}, bf16[128,768]{1,0:T(8,128)(2,1)S(1)}, u32[]{:S(2)}, u32[]{:S(2)}) %collective-permute-start.19) | collective-permute-done | bytes 196640 | tf_op jit(solution)/shard_map/ppermute | solution.py:18
  100.6 2.0 %collective-permute-start.20 = (bf16[128,768]{1,0:T(8,128)(2,1)S(1)}, bf16[128,768]{1,0:T(8,128)(2,1)S(1)}, u32[]{:S(2)}, u32[]{:S(2)}) collective-permute-start(bf16[128,768]{1,0:T(8,128)(2,1)S(1)} %get-tuple-element.38), channel_id=1, source_target_pairs={{0,8},{4,12},{8,0},{12,4},{16,24},{20,28},{24,16},{28,20},{1,9},{5... | collective-permute-start | bytes 589832 | tf_op jit(solution)/shard_map/ppermute | solution.py:18
  108.6 2.7 %collective-permute-done.16.refs_2_ = bf16[64,1408]{1,0:T(8,128)(2,1)S(1)} collective-permute-done((bf16[64,1408]{1,0:T(8,128)(2,1)S(1)}, bf16[64,1408]{1,0:T(8,128)(2,1)S(1)}, u32[]{:S(2)}, u32[]{:S(2)}) %collective-permute-start.16) | collective-permute-done | bytes 180256 | tf_op jit(solution)/shard_map/ppermute | solution.py:18
  111.4 3.0 %collective-permute-done.17.refs_3_ = bf16[64,1408]{1,0:T(8,128)(2,1)S(1)} collective-permute-done((bf16[64,1408]{1,0:T(8,128)(2,1)S(1)}, bf16[64,1408]{1,0:T(8,128)(2,1)S(1)}, u32[]{:S(2)}, u32[]{:S(2)}) %collective-permute-start.17) | collective-permute-done | bytes 180256 | tf_op jit(solution)/shard_map/ppermute | solution.py:18
  115.0 2.4 %collective-permute-done.22.refs_4_ = bf16[64,768]{1,0:T(8,128)(2,1)S(1)} collective-permute-done((bf16[64,768]{1,0:T(8,128)(2,1)S(1)}, bf16[64,768]{1,0:T(8,128)(2,1)S(1)}, u32[]{:S(2)}, u32[]{:S(2)}) %collective-permute-start.22) | collective-permute-done | bytes 98336 | tf_op jit(solution)/shard_map/ppermute | solution.py:18
  (59 shorter events, 16.7 us)
Async XLA Ops:
  0.0 15.1 %collective-permute-start = (bf16[128,2048]{1,0:T(8,128)(2,1)}, bf16[128,2048]{1,0:T(8,128)(2,1)S(1)}, u32[]{:S(2)}, u32[]{:S(2)}) collective-permute-start(bf16[128,2048]{1,0:T(8,128)(2,1)} %refs_1_.3), channel_id=1, source_target_pairs={{0,2},{1,3},{2,0},{3,1},{4,6},{5,7},{6,4},{7,5},{8,10},{9,11},{10,... | collective-permute-start | bytes 1572872 | tf_op jit(solution)/shard_map/ppermute | solution.py:18
  5.4 17.0 %collective-permute-start.9 = (bf16[256,1024]{1,0:T(8,128)(2,1)}, bf16[256,1024]{1,0:T(8,128)(2,1)S(1)}, u32[]{:S(2)}, u32[]{:S(2)}) collective-permute-start(bf16[256,1024]{1,0:T(8,128)(2,1)} %get-tuple-element.28), channel_id=1, source_target_pairs={{0,24},{4,28},{8,16},{12,20},{16,8},{20,12},{24,0},{28,4},{1,25},{... | collective-permute-start | bytes 1572872 | tf_op jit(solution)/shard_map/ppermute | solution.py:18
  9.0 23.8 %collective-permute-start.1 = (bf16[128,2048]{1,0:T(8,128)(2,1)S(1)}, bf16[128,2048]{1,0:T(8,128)(2,1)S(1)}, u32[]{:S(2)}, u32[]{:S(2)}) collective-permute-start(bf16[128,2048]{1,0:T(8,128)(2,1)S(1)} %copy-done.3), channel_id=1, source_target_pairs={{0,1},{1,0},{2,3},{3,2},{4,5},{5,4},{6,7},{7,6},{8,9},{9,8},{10,11... | collective-permute-start | bytes 1572872 | tf_op jit(solution)/shard_map/ppermute | solution.py:18
  9.0 24.7 %collective-permute-start.5 = (bf16[256,1024]{1,0:T(8,128)(2,1)}, bf16[256,1024]{1,0:T(8,128)(2,1)}, u32[]{:S(2)}, u32[]{:S(2)}) collective-permute-start(bf16[256,1024]{1,0:T(8,128)(2,1)} %get-tuple-element.28), channel_id=1, source_target_pairs={{0,8},{4,12},{8,0},{12,4},{16,24},{20,28},{24,16},{28,20},{1,9},{5... | collective-permute-start | bytes 1572872 | tf_op jit(solution)/shard_map/ppermute | solution.py:18
  15.1 21.7 %collective-permute-start.2 = (bf16[128,2048]{1,0:T(8,128)(2,1)S(1)}, bf16[128,2048]{1,0:T(8,128)(2,1)}, u32[]{:S(2)}, u32[]{:S(2)}) collective-permute-start(bf16[128,2048]{1,0:T(8,128)(2,1)S(1)} %collective-permute-done.refs_2_.refs_0_), channel_id=1, source_target_pairs={{0,1},{1,0},{2,3},{3,2},{4,5},{5,4},{6,7},{7,6},{8,9},{9,8},{10,11... | collective-permute-start | bytes 1572872 | tf_op jit(solution)/shard_map/ppermute | solution.py:18
  15.1 25.0 %collective-permute-start.4 = (bf16[256,1024]{1,0:T(8,128)(2,1)}, bf16[256,1024]{1,0:T(8,128)(2,1)}, u32[]{:S(2)}, u32[]{:S(2)}) collective-permute-start(bf16[256,1024]{1,0:T(8,128)(2,1)} %get-tuple-element.27.refs_1_.refs_0_), channel_id=1, source_target_pairs={{0,4},{4,0},{8,12},{12,8},{16,20},{20,16},{24,28},{28,24},{1,5},{5... | collective-permute-start | bytes 1572872 | tf_op jit(solution)/shard_map/ppermute | solution.py:18
  22.3 41.3 %collective-permute-start.7 = (bf16[256,1024]{1,0:T(8,128)(2,1)S(1)}, bf16[256,1024]{1,0:T(8,128)(2,1)S(1)}, u32[]{:S(2)}, u32[]{:S(2)}) collective-permute-start(bf16[256,1024]{1,0:T(8,128)(2,1)S(1)} %shard_map.67), channel_id=1, source_target_pairs={{0,16},{4,20},{8,24},{12,28},{16,0},{20,4},{24,8},{28,12},{1,17},{... | collective-permute-start | bytes 1572872 | tf_op jit(solution)/shard_map/ppermute | solution.py:18
  33.7 35.4 %collective-permute-start.11 = (bf16[128,1280]{1,0:T(8,128)(2,1)S(1)}, bf16[128,1280]{1,0:T(8,128)(2,1)}, u32[]{:S(2)}, u32[]{:S(2)}) collective-permute-start(bf16[128,1280]{1,0:T(8,128)(2,1)S(1)} %shard_map.69), channel_id=1, source_target_pairs={{0,16},{4,20},{8,24},{12,28},{16,0},{20,4},{24,8},{28,12},{1,17},{... | collective-permute-start | bytes 983048 | tf_op jit(solution)/shard_map/ppermute | solution.py:18
  33.7 36.9 %collective-permute-start.6 = (bf16[256,1024]{1,0:T(8,128)(2,1)}, bf16[256,1024]{1,0:T(8,128)(2,1)}, u32[]{:S(2)}, u32[]{:S(2)}) collective-permute-start(bf16[256,1024]{1,0:T(8,128)(2,1)} %collective-permute-done.5.refs_2_), channel_id=1, source_target_pairs={{0,4},{4,0},{8,12},{12,8},{16,20},{20,16},{24,28},{28,24},{1,5},{5... | collective-permute-start | bytes 1572872 | tf_op jit(solution)/shard_map/ppermute | solution.py:18
  36.7 34.4 %collective-permute-start.10 = (bf16[256,1024]{1,0:T(8,128)(2,1)S(1)}, bf16[256,1024]{1,0:T(8,128)(2,1)S(1)}, u32[]{:S(2)}, u32[]{:S(2)}) collective-permute-start(bf16[256,1024]{1,0:T(8,128)(2,1)S(1)} %collective-permute-done.9.refs_6_.refs_0_), channel_id=1, source_target_pairs={{0,4},{4,0},{8,12},{12,8},{16,20},{20,16},{24,28},{28,24},{1,5},{5... | collective-permute-start | bytes 1572872 | tf_op jit(solution)/shard_map/ppermute | solution.py:18
  40.1 31.1 %collective-permute-start.3 = (bf16[128,2048]{1,0:T(8,128)(2,1)S(1)}, bf16[128,2048]{1,0:T(8,128)(2,1)S(1)}, u32[]{:S(2)}, u32[]{:S(2)}) collective-permute-start(bf16[128,2048]{1,0:T(8,128)(2,1)S(1)} %shard_map.65.own_ref), channel_id=1, source_target_pairs={{0,8},{4,12},{8,0},{12,4},{16,24},{20,28},{24,16},{28,20},{1,9},{5... | collective-permute-start | bytes 1572872 | tf_op jit(solution)/shard_map/ppermute | solution.py:18
  63.6 14.6 %collective-permute-start.8 = (bf16[256,1024]{1,0:T(8,128)(2,1)S(1)}, bf16[256,1024]{1,0:T(8,128)(2,1)S(1)}, u32[]{:S(2)}, u32[]{:S(2)}) collective-permute-start(bf16[256,1024]{1,0:T(8,128)(2,1)S(1)} %collective-permute-done.7.refs_4_.refs_0_), channel_id=1, source_target_pairs={{0,4},{4,0},{8,12},{12,8},{16,20},{20,16},{24,28},{28,24},{1,5},{5... | collective-permute-start | bytes 1572872 | tf_op jit(solution)/shard_map/ppermute | solution.py:18
  69.1 19.9 %collective-permute-start.12 = (bf16[128,2048]{1,0:T(8,128)(2,1)S(1)}, bf16[128,2048]{1,0:T(8,128)(2,1)S(1)}, u32[]{:S(2)}, u32[]{:S(2)}) collective-permute-start(bf16[128,2048]{1,0:T(8,128)(2,1)S(1)} %bitcast.5), channel_id=1, source_target_pairs={{0,4},{4,0},{8,12},{12,8},{16,20},{20,16},{24,28},{28,24},{1,5},{5... | collective-permute-start | bytes 1572872 | tf_op jit(solution)/shard_map/ppermute | solution.py:18
  70.6 21.9 %collective-permute-start.13 = (bf16[128,1280]{1,0:T(8,128)(2,1)}, bf16[128,1280]{1,0:T(8,128)(2,1)S(1)}, u32[]{:S(2)}, u32[]{:S(2)}) collective-permute-start(bf16[128,1280]{1,0:T(8,128)(2,1)} %collective-permute-done.11.refs_2_), channel_id=1, source_target_pairs={{0,4},{4,0},{8,12},{12,8},{16,20},{20,16},{24,28},{28,24},{1,5},{5... | collective-permute-start | bytes 983048 | tf_op jit(solution)/shard_map/ppermute | solution.py:18
  71.1 23.2 %collective-permute-start.18 = (bf16[128,768]{1,0:T(8,128)(2,1)S(1)}, bf16[128,768]{1,0:T(8,128)(2,1)S(1)}, u32[]{:S(2)}, u32[]{:S(2)}) collective-permute-start(bf16[128,768]{1,0:T(8,128)(2,1)S(1)} %shard_map.73), channel_id=1, source_target_pairs={{0,16},{4,20},{8,24},{12,28},{16,0},{20,4},{24,8},{28,12},{1,17},{... | collective-permute-start | bytes 589832 | tf_op jit(solution)/shard_map/ppermute | solution.py:18
  94.2 9.2 %collective-permute-start.14 = (bf16[128,1280]{1,0:T(8,128)(2,1)S(1)}, bf16[128,1280]{1,0:T(8,128)(2,1)S(1)}, u32[]{:S(2)}, u32[]{:S(2)}) collective-permute-start(bf16[128,1280]{1,0:T(8,128)(2,1)S(1)} %get-tuple-element.30), channel_id=1, source_target_pairs={{0,8},{4,12},{8,0},{12,4},{16,24},{20,28},{24,16},{28,20},{1,9},{5... | collective-permute-start | bytes 983048 | tf_op jit(solution)/shard_map/ppermute | solution.py:18
  94.3 5.7 %collective-permute-start.19 = (bf16[128,768]{1,0:T(8,128)(2,1)S(1)}, bf16[128,768]{1,0:T(8,128)(2,1)S(1)}, u32[]{:S(2)}, u32[]{:S(2)}) collective-permute-start(bf16[128,768]{1,0:T(8,128)(2,1)S(1)} %collective-permute-done.18.refs_2_), channel_id=1, source_target_pairs={{0,4},{4,0},{8,12},{12,8},{16,20},{20,16},{24,28},{28,24},{1,5},{5... | collective-permute-start | bytes 589832 | tf_op jit(solution)/shard_map/ppermute | solution.py:18
  100.6 5.7 %collective-permute-start.20 = (bf16[128,768]{1,0:T(8,128)(2,1)S(1)}, bf16[128,768]{1,0:T(8,128)(2,1)S(1)}, u32[]{:S(2)}, u32[]{:S(2)}) collective-permute-start(bf16[128,768]{1,0:T(8,128)(2,1)S(1)} %get-tuple-element.38), channel_id=1, source_target_pairs={{0,8},{4,12},{8,0},{12,4},{16,24},{20,28},{24,16},{28,20},{1,9},{5... | collective-permute-start | bytes 589832 | tf_op jit(solution)/shard_map/ppermute | solution.py:18
  103.9 3.5 %collective-permute-start.15 = (bf16[64,1408]{1,0:T(8,128)(2,1)S(1)}, bf16[64,1408]{1,0:T(8,128)(2,1)S(1)}, u32[]{:S(2)}, u32[]{:S(2)}) collective-permute-start(bf16[64,1408]{1,0:T(8,128)(2,1)S(1)} %get-tuple-element.32), channel_id=1, source_target_pairs={{0,1},{1,0},{2,3},{3,2},{4,5},{5,4},{6,7},{7,6},{8,9},{9,8},{10,11... | collective-permute-start | bytes 540680 | tf_op jit(solution)/shard_map/ppermute | solution.py:18
  104.0 7.4 %collective-permute-start.16 = (bf16[64,1408]{1,0:T(8,128)(2,1)S(1)}, bf16[64,1408]{1,0:T(8,128)(2,1)S(1)}, u32[]{:S(2)}, u32[]{:S(2)}) collective-permute-start(bf16[64,1408]{1,0:T(8,128)(2,1)S(1)} %get-tuple-element.33), channel_id=1, source_target_pairs={{0,2},{1,3},{2,0},{3,1},{4,6},{5,7},{6,4},{7,5},{8,10},{9,11},{10,... | collective-permute-start | bytes 540680 | tf_op jit(solution)/shard_map/ppermute | solution.py:18
  104.6 9.8 %collective-permute-start.17 = (bf16[64,1408]{1,0:T(8,128)(2,1)S(1)}, bf16[64,1408]{1,0:T(8,128)(2,1)S(1)}, u32[]{:S(2)}, u32[]{:S(2)}) collective-permute-start(bf16[64,1408]{1,0:T(8,128)(2,1)S(1)} %get-tuple-element.34), channel_id=1, source_target_pairs={{0,3},{1,2},{2,1},{3,0},{4,7},{5,6},{6,5},{7,4},{8,11},{9,10},{10,... | collective-permute-start | bytes 540680 | tf_op jit(solution)/shard_map/ppermute | solution.py:18
  106.7 8.2 %collective-permute-start.21 = (bf16[64,768]{1,0:T(8,128)(2,1)S(1)}, bf16[64,768]{1,0:T(8,128)(2,1)S(1)}, u32[]{:S(2)}, u32[]{:S(2)}) collective-permute-start(bf16[64,768]{1,0:T(8,128)(2,1)S(1)} %get-tuple-element.40), channel_id=1, source_target_pairs={{0,1},{1,0},{2,3},{3,2},{4,5},{5,4},{6,7},{7,6},{8,9},{9,8},{10,11... | collective-permute-start | bytes 294920 | tf_op jit(solution)/shard_map/ppermute | solution.py:18
  106.8 10.6 %collective-permute-start.22 = (bf16[64,768]{1,0:T(8,128)(2,1)S(1)}, bf16[64,768]{1,0:T(8,128)(2,1)S(1)}, u32[]{:S(2)}, u32[]{:S(2)}) collective-permute-start(bf16[64,768]{1,0:T(8,128)(2,1)S(1)} %get-tuple-element.41), channel_id=1, source_target_pairs={{0,2},{1,3},{2,0},{3,1},{4,6},{5,7},{6,4},{7,5},{8,10},{9,11},{10,... | collective-permute-start | bytes 294920 | tf_op jit(solution)/shard_map/ppermute | solution.py:18
  107.4 11.2 %collective-permute-start.23 = (bf16[64,768]{1,0:T(8,128)(2,1)S(1)}, bf16[64,768]{1,0:T(8,128)(2,1)S(1)}, u32[]{:S(2)}, u32[]{:S(2)}) collective-permute-start(bf16[64,768]{1,0:T(8,128)(2,1)S(1)} %get-tuple-element.42), channel_id=1, source_target_pairs={{0,3},{1,2},{2,1},{3,0},{4,7},{5,6},{6,5},{7,4},{8,11},{9,10},{10,... | collective-permute-start | bytes 294920 | tf_op jit(solution)/shard_map/ppermute | solution.py:18
  (10 other events, 40.6 us)

commit v3 on v2

--- a/solution.py
+++ b/solution.py
@@ -9,6 +9,7 @@
 
 SHARES = (5, 3)
 OPENING_LIMIT = 60 * 2**20
+LONG = 10**12
 F32 = jnp.float32
 BF16 = jnp.bfloat16
 
@@ -47,29 +48,45 @@
     return jnp.dot(a, b, preferred_element_type=F32)
 
 
-def opening(bit_ref, gate_ref, up_ref, same_ref, other_ref, sem):
-    pairs = sem.shape[0] // 4
+def opening(bit_ref, gate_ref, up_ref, *refs, flip, pairs):
+    *more, out_ref, sem = refs
+    rows = gate_ref.shape[1]
     wide = gate_ref.shape[2] // (2 * pairs)
     copies = []
-    for flip, target in ((0, same_ref), (1, other_ref)):
-        at = 0
-        for ref in (gate_ref, up_ref):
-            for j in range(pairs):
-                start = pl.multiple_of((2 * j + (bit_ref[0] ^ flip)) * wide, 128)
-                copies.append(
-                    pltpu.make_async_copy(
-                        ref.at[0, :, pl.ds(start, wide)], target.at[:, at : at + wide], sem.at[len(copies)]
-                    )
-                )
-                at += wide
-    for copy in copies:
-        copy.start()
-    for copy in copies:
-        copy.wait()
-
-
-def hand(in_ref, out_ref):
-    out_ref[...] = in_ref[...]
+
+    def copy(source, target):
+        copies.append(pltpu.make_async_copy(source, target, sem.at[len(copies)]))
+
+    at = 0
+    for ref in (gate_ref, up_ref):
+        for j in range(pairs):
+            start = pl.multiple_of((2 * j + (bit_ref[0] ^ flip)) * wide, 128)
+            copy(ref.at[0, :, pl.ds(start, wide)], out_ref.at[:rows, at : at + wide])
+            at += wide
+    for down_ref in more:
+        tall, half = down_ref.shape[1], out_ref.shape[1]
+        for j in range(down_ref.shape[2] // half):
+            copy(
+                down_ref.at[0, :, j * half : (j + 1) * half],
+                out_ref.at[rows + j * tall : rows + (j + 1) * tall],
+            )
+    for item in copies:
+        item.start()
+    for item in copies:
+        item.wait()
+
+
+def join(*refs):
+    out_ref, start = refs[-1], 0
+    for ref in refs[:-1]:
+        out_ref[start : start + ref.shape[0]] = ref[...]
+        start += ref.shape[0]
+
+
+def hand(*refs):
+    half = len(refs) // 2
+    for ref, out_ref in zip(refs[:half], refs[half:]):
+        out_ref[...] = ref[: out_ref.shape[0]]
 
 
 def ranks_of(hits):
@@ -83,11 +100,7 @@
     capacity = rows.shape[1]
     block = (rows // tok_dev) ^ expert_ref[0]
     local = rows % tok_dev
-    bits = experts.bit_length() - 1
-    seat = jnp.zeros_like(block)
-    for bit in range(bits):
-        seat = seat | (((block >> bit) & 1) << (bits - 1 - bit))
-    place = seat * tok_dev + local
+    place = block * tok_dev + local
     count = experts * tok_dev
     pick_ref[...] = (lax.broadcasted_iota(jnp.int32, (count, capacity), 0) == place).astype(BF16)
     hot = lax.broadcasted_iota(jnp.int32, (experts, capacity), 0) == block
@@ -119,19 +132,30 @@
     out_ref[...] = down_ref[0, :, start : start + out_ref.shape[1]]
 
 
-def hidden_units(where_ref, own_ref, far_ref, *refs, pairs):
-    *weights, out_ref, total = refs
+def products(total, where_ref, own_ref, far_ref, arrays, places, fresh):
     capacity = own_ref.shape[0]
-    rows = weights[0].shape[0]
-    for mask, block in enumerate(weights):
-        columns = pl.ds(pl.multiple_of(where_ref[mask] * rows, min(rows, 256)), rows)
+    for array, first, count, mask in places:
+        columns = pl.ds(pl.multiple_of(where_ref[mask] * count, min(count, 256)), count)
+        block = arrays[array][first : first + count, :]
         for side, ref in enumerate((own_ref, far_ref)):
             lines = pl.ds(side * capacity, capacity)
-            product = dot(ref[:, columns], block[...])
-            if mask == 0:
+            product = dot(ref[:, columns], block)
+            if fresh:
                 total[lines, :] = product
             else:
                 total[lines, :] += product
+        fresh = False
+
+
+def first_units(where_ref, own_ref, far_ref, *refs, places):
+    *arrays, total = refs
+    products(total, where_ref, own_ref, far_ref, arrays, places, True)
+
+
+def hidden_units(where_ref, own_ref, far_ref, start_ref, *refs, places, pairs):
+    *arrays, out_ref, total = refs
+    total[...] = start_ref[...]
+    products(total, where_ref, own_ref, far_ref, arrays, places, False)
     half = total.shape[1] // 2
     if pairs == 0:
         gate, up = total[:, :half], total[:, half:]
@@ -150,16 +174,17 @@
 
 
 def down_units(hidden_ref, *refs, places):
-    parts, (out_ref, away_ref) = refs[:-2], refs[-2:]
-    capacity, step = out_ref.shape
-    for side, target in enumerate((out_ref, away_ref)):
-        lines = pl.ds(side * capacity, capacity)
-        total, unit = 0.0, 0
-        for part, at in zip(parts, places):
-            rows = part.shape[0]
-            total = total + dot(hidden_ref[lines, unit : unit + rows], part[:, at : at + step])
-            unit += rows
-        target[...] = total.astype(target.dtype)
+    arrays, (out_ref, away_ref) = refs[:-2], refs[-2:]
+    capacity = out_ref.shape[0]
+    total, unit = 0.0, 0
+    for pieces in places:
+        values = [arrays[a][r : r + n, c : c + w] for a, r, n, c, w in pieces]
+        block = values[0] if len(values) == 1 else jnp.concatenate(values, axis=1)
+        rows = block.shape[0]
+        total = total + dot(hidden_ref[:, unit : unit + rows], block)
+        unit += rows
+    out_ref[...] = total[:capacity]
+    away_ref[...] = total[capacity:].astype(BF16)
 
 
 def weigh(place_ref, tag_ref, weights_ref, out_ref, away_ref, *sent_refs):
@@ -226,15 +251,21 @@
     zbit = replica // 2 % 2
     whole_lanes = block % 128 == 0
     if whole_lanes:
-        same_units, other_units = pl.pallas_call(
-            opening,
-            out_shape=[shape(rows_shard, units)] * 2,
-            in_specs=[pl.BlockSpec(memory_space=pltpu.SMEM)] + [pl.BlockSpec(memory_space=pl.ANY)] * 2,
-            out_specs=[pl.BlockSpec(memory_space=pltpu.VMEM)] * 2,
-            scratch_shapes=[pltpu.SemaphoreType.DMA((4 * pairs,))],
-            compiler_params=pltpu.CompilerParams(vmem_limit_bytes=OPENING_LIMIT),
-            cost_estimate=pl.CostEstimate(flops=0, bytes_accessed=2**21, transcendentals=0),
-        )(zbit[None], w_gate, w_up)
+        def collect(flip, *arrays):
+            count = sum(x.shape[1] * x.shape[2] for x in arrays[2:]) // units
+            return pl.pallas_call(
+                functools.partial(opening, flip=flip, pairs=pairs),
+                out_shape=shape(rows_shard + count, units),
+                in_specs=[pl.BlockSpec(memory_space=pltpu.SMEM)]
+                + [pl.BlockSpec(memory_space=pl.ANY)] * len(arrays),
+                out_specs=pl.BlockSpec(memory_space=pltpu.VMEM),
+                scratch_shapes=[pltpu.SemaphoreType.DMA((2 * pairs + width // units,))],
+                compiler_params=pltpu.CompilerParams(vmem_limit_bytes=OPENING_LIMIT),
+                cost_estimate=pl.CostEstimate(flops=0, bytes_accessed=2**20, transcendentals=0),
+            )(zbit[None], *arrays)
+
+        other_units = collect(1, w_gate, w_up)
+        across = collect(0, w_gate, w_up, w_down)
     else:
         same_units, other_units = (
             jnp.concatenate(
@@ -248,22 +279,34 @@
             )
             for flip in (0, 1)
         )
+        halves = [w_down[0, :, at : at + units] for at in range(0, width, units)]
+        across = jnp.concatenate([same_units, *halves], axis=0)
     far = [mask for mask in range(replicas - 2, 2, -2)]
-    weights = {0: same_units}
-    weights[1] = swap(same_units, "dp", 1)
-    for mask in far[::2]:
-        weights[mask] = swap(other_units, "dp", mask)
+    came = swap(across, "dp", 1)
+    weights = {mask: swap(other_units, "dp", mask) for mask in far[::2]}
+
+    weights[2] = swap(other_units, "dp", 2)
+
+    def down_far(piece):
+        own, bit = [piece], 4
+        while bit < replicas:
+            have = own[0] if len(own) == 1 else jnp.concatenate(own, axis=0)
+            own.append(swap(have, "dp", bit))
+            bit *= 2
+        return own[1:]
+
+    late_same = call(hand, [shape(rows_shard, units)], across)[0]
+    for mask in far[1::2]:
+        weights[mask] = swap(late_same, "dp", mask)
 
     group = [tokens]
-    bit = experts // 2
-    while bit > 0:
-        if bit == 1:
-            ready = group[-1]
-        group += [swap(x, "expert", bit) for x in group]
-        bit //= 2
-    late_units = call(hand, shape(rows_shard, units), same_units, wait=[ready])
-    for mask in far[1::2]:
-        weights[mask] = swap(late_units, "dp", mask)
+    bit = 1
+    while bit < experts:
+        have = group[0]
+        if len(group) > 1:
+            have = call(join, shape(bit * tok_dev, width), *group, wait=[other_units])
+        group.append(swap(have, "expert", bit))
+        bit *= 2
     pick_hot, place_hot, tags = call(
         functools.partial(own_tables, experts=experts, tok_dev=tok_dev),
         [shape(experts * tok_dev, capacity), shape(experts * most, capacity), shape(experts * most, 128)],
@@ -276,46 +319,64 @@
         shape(capacity, width),
         pick_hot,
         *group,
-        flops=2 * experts * tok_dev * capacity * width,
+        wait=[came],
+        flops=LONG,
     )
     picked_z = swap(picked, "dp", 2)
-    weights[2] = swap(other_units, "dp", 2)
-    down_y = swap(w_down[0], "dp", 1)
-    for mask in [2, *far]:
+    group_far = [2, *far[::2]]
+    came_far = [swap(weights[mask], "dp", 1) for mask in group_far]
+    for mask in far[1::2]:
         weights[mask + 1] = swap(weights[mask], "dp", 1)
 
-    down = []
+    down, down_far_y = [], []
     for index in range(len(SHARES)):
         piece = call(
             functools.partial(cut, start=starts[index]),
             shape(down_rows, steps[index]),
             w_down,
-            wait=[weights[far[min(index, len(far) - 1)]]],
-        )
-        own, bit = [piece], 4
-        while bit < replicas:
-            have = own[0] if len(own) == 1 else jnp.concatenate(own, axis=0)
-            own.append(swap(have, "dp", bit))
-            bit *= 2
-        down.append(own[1:])
-
-    arrays = [weights[mask] for mask in range(replicas)]
+            wait=[weights[far[0]]] if index == 0 else [weights[far[-1]]] if index == 1 else down[-1],
+            flops=LONG if index == 0 else 0,
+        )
+        down.append(down_far(piece))
+        down_far_y.append([swap(x, "dp", 1) for x in down[-1]])
+
     order = replica ^ jnp.arange(replicas, dtype=jnp.int32)
+    late = [mask for mask in range(2, replicas) if mask & ~1 in far[1::2]]
+    arrays = [across, came, *came_far, *[weights[mask] for mask in group_far]]
+    places = [(0, 0, rows_shard, 0), (1, 0, rows_shard, 1)]
+    for i, mask in enumerate(group_far):
+        places += [(2 + len(group_far) + i, 0, rows_shard, mask), (2 + i, 0, rows_shard, mask + 1)]
+    late_arrays = [weights[mask] for mask in late]
+    late_places = [(i, 0, rows_shard, mask) for i, mask in enumerate(late)]
     if rows_shard % 128 != 0:
-        arrays = [jnp.take(jnp.stack(arrays), order, axis=0).reshape(-1, units)]
-        order = jnp.zeros((1,), jnp.int32)
+        blocks = {m: arrays[a][r : r + n] for a, r, n, m in places}
+        blocks |= {m: late_arrays[a][r : r + n] for a, r, n, m in late_places}
+        stacked = jnp.take(jnp.stack([blocks[m] for m in range(replicas)]), order, axis=0).reshape(-1, units)
+        parts = stacked.shape[0] // 2
+        arrays, late_arrays = [stacked[:parts]], [stacked[parts:]]
+        places, late_places = [(0, 0, parts, 0)], [(0, 0, parts, 1)]
+        order = jnp.arange(2, dtype=jnp.int32)
+    flops = capacity * width * units
+    start_units = call(
+        functools.partial(first_units, places=places),
+        shape(2 * capacity, units, dtype=F32),
+        order,
+        picked,
+        picked_z,
+        *arrays,
+        flops=3 * flops,
+        scalars=1,
+    )
     hidden = pl.pallas_call(
-        functools.partial(hidden_units, pairs=pairs if whole_lanes else 0),
+        functools.partial(hidden_units, places=late_places, pairs=pairs if whole_lanes else 0),
         out_shape=shape(2 * capacity, units // 2),
         in_specs=[pl.BlockSpec(memory_space=pltpu.SMEM)]
-        + [pl.BlockSpec(memory_space=pltpu.VMEM)] * (2 + len(arrays)),
+        + [pl.BlockSpec(memory_space=pltpu.VMEM)] * (3 + len(late_arrays)),
         out_specs=pl.BlockSpec(memory_space=pltpu.VMEM),
         scratch_shapes=[pltpu.VMEM((2 * capacity, units), F32)],
         compiler_params=pltpu.CompilerParams(vmem_limit_bytes=limit),
-        cost_estimate=pl.CostEstimate(
-            flops=4 * capacity * width * units, bytes_accessed=2**23, transcendentals=0
-        ),
-    )(order, picked, picked_z, *arrays)
+        cost_estimate=pl.CostEstimate(flops=flops, bytes_accessed=2**22, transcendentals=0),
+    )(order, picked, picked_z, start_units, *late_arrays)
     if not whole_lanes:
         index = jnp.arange(2 * pairs, dtype=jnp.int32)
         turn = 2 * ((replica // 4) ^ (index % pairs)) + ((replica % 2) ^ (index // pairs))
@@ -324,9 +385,20 @@
     gate_column = gate_weights[0, 0][:, None]
     results = []
     for index, (start, step, far_rows) in enumerate(zip(starts, steps, down)):
-        parts = [w_down[0], *far_rows, down_y, *[swap(x, "dp", 1) for x in far_rows]]
+        def pieces(array, first, at, end):
+            cuts = [(at, min(end, units)), (max(at, units), end)]
+            return [
+                (array, first + down_rows * (c // units), down_rows, c % units, e - c) for c, e in cuts if c < e
+            ]
+
+        parts = [across, came, *far_rows, *down_far_y[index]]
+        count = len(far_rows)
+        places = [pieces(0, rows_shard, start, start + step)]
+        places += [[(2 + i, 0, x.shape[0], 0, step)] for i, x in enumerate(far_rows)]
+        places += [pieces(1, rows_shard, start, start + step)]
+        places += [[(2 + count + i, 0, x.shape[0], 0, step)] for i, x in enumerate(far_rows)]
         out, away = call(
-            functools.partial(down_units, places=[start if x.shape[1] == width else 0 for x in parts]),
+            functools.partial(down_units, places=places),
             [shape(capacity, step, dtype=F32), shape(capacity, step)],
             hidden,
             *parts,

time: 120 us -> 109 us (0.908)
  waiting for transfers between devices: 69 us -> 50.4 us
  Pallas kernels: 12.2 us -> 20 us
  local copies, waits for them, and re-layouts: 4.3 us -> 2.05 us
  starting transfers between devices: 34.1 us -> 36.2 us
    ppermute x24 -> x22, waiting for transfers between devices: 69 us -> 50.4 us  [swap(): return lax.ppermute(value, axis, pairs)]
    pallas_call x11 -> x13, Pallas kernels: 6.95 us -> 14.1 us  [call(): pl.pallas_call(body, out_shape=out_shape, in_specs=in_specs, out_specs=ja...]
    unnamed x20 -> x16, local copies, waits for them, and re-layouts: 4.19 us -> 1.94 us
    ppermute x24 -> x22, starting transfers between devices: 34.1 us -> 36.2 us  [swap(): return lax.ppermute(value, axis, pairs)]
    pallas_call x2 -> x3, Pallas kernels: 5.23 us -> 5.95 us  [the longest x2 4.25 us: collect(): pl.pallas_call(functools.partial(opening, flip=flip, pairs=pairs), out_sh...]
  transfers between devices with their start and end apart: 24 -> 22, of which waited for: 14 -> 14; matrix products, arithmetic and copies ran while one was open for 0% -> 0% of each run, Pallas kernels for 9% -> 17%
where the time goes in v3:
time: 109 us
  waiting for transfers between devices  50.4 us (46%)
  starting transfers between devices  36.2 us (33%)
  Pallas kernels  20 us (18%)
  local copies, waits for them, and re-layouts  2.05 us (2%)
    ppermute x22, waiting for transfers between devices, swap(): return lax.ppermute(value, axis, pairs)  50.4 us
    ppermute x22, starting transfers between devices, swap(): return lax.ppermute(value, axis, pairs)  36.2 us
    pallas_call x13, Pallas kernels, call(): pl.pallas_call(body, out_shape=out_shape, in_specs=in_specs, out_specs=ja...  14.1 us
    pallas_call x2, Pallas kernels, collect(): pl.pallas_call(functools.partial(opening, flip=flip, pairs=pairs), out_sh...  4.25 us
  transfers between devices with their start and end apart: 22, of which 14 were waited for; matrix products, arithmetic and copies ran while one was open for 0% of the time, Pallas kernels for 17%

profile of v3, /device:TPU:0, one launch (start us, length us, event | category | flops | bytes accessed | tf_op | source)
XLA Modules:
  0.0 108.8 jit_solution(1225709182388433650)
XLA Ops:
  0.5 1.9 %shard_map.66.refs_0_ = bf16[256,1024]{1,0:T(8,128)(2,1)} custom-call(s32[1]{0:T(128)} %bitcast.3.bit_ref, bf16[1,256,1024]{2,1,0:T(8,128)(2,1)} %gate_ref.3, bf16[1,256,1024]{2,1,0:T(8,128)(2,1)} %up_ref.3), custom_call_target="tpu_custom_call" | custom-call | bytes 1048576 | tf_op jit(solution)/shard_map/pallas_call | solution.py:256
  2.4 4.7 %collective-permute-start.6 = (bf16[256,1024]{1,0:T(8,128)(2,1)}, bf16[256,1024]{1,0:T(8,128)(2,1)}, u32[]{:S(2)}, u32[]{:S(2)}) collective-permute-start(bf16[256,1024]{1,0:T(8,128)(2,1)} %shard_map.66.refs_0_), channel_id=1, source_target_pairs={{0,24},{4,28},{8,16},{12,20},{16,8},{20,12},{24,0},{28,4},{1,25},{... | collective-permute-start | bytes 1572872 | tf_op jit(solution)/shard_map/ppermute | solution.py:19
  7.1 2.3 %shard_map.65.refs_3_.refs_0_.refs_1_ = bf16[512,1024]{1,0:T(8,128)(2,1)} custom-call(s32[1]{0:T(128)} %bitcast.3.bit_ref, bf16[1,256,1024]{2,1,0:T(8,128)(2,1)} %gate_ref.3, bf16[1,256,1024]{2,1,0:T(8,128)(2,1)} %up_ref.3, bf16[1,128,2048]{2,1,0:T(8,128)(2,1)} %refs_1_.5), custom_call_target="tpu_custom_call" | custom-call | bytes 1048576 | tf_op jit(solution)/shard_map/pallas_call | solution.py:256
  9.4 1.6 %collective-permute-start = (bf16[512,1024]{1,0:T(8,128)(2,1)}, bf16[512,1024]{1,0:T(8,128)(2,1)}, u32[]{:S(2)}, u32[]{:S(2)}) collective-permute-start(bf16[512,1024]{1,0:T(8,128)(2,1)} %shard_map.65.refs_3_.refs_0_.refs_1_), channel_id=1, source_target_pairs={{0,4},{4,0},{8,12},{12,8},{16,20},{20,16},{24,28},{28,24},{1,5},{5... | collective-permute-start | bytes 3145736 | tf_op jit(solution)/shard_map/ppermute | solution.py:19
  17.4 2.9 %collective-permute-done.6.refs_8_.refs_0_ = bf16[256,1024]{1,0:T(8,128)(2,1)} collective-permute-done((bf16[256,1024]{1,0:T(8,128)(2,1)}, bf16[256,1024]{1,0:T(8,128)(2,1)}, u32[]{:S(2)}, u32[]{:S(2)}) %collective-permute-start.6) | collective-permute-done | bytes 524320 | tf_op jit(solution)/shard_map/ppermute | solution.py:19
  21.1 12.1 %collective-permute-start.10 = (bf16[128,1280]{1,0:T(8,128)(2,1)}, bf16[128,1280]{1,0:T(8,128)(2,1)}, u32[]{:S(2)}, u32[]{:S(2)}) collective-permute-start(bf16[128,1280]{1,0:T(8,128)(2,1)} %shard_map.72), channel_id=1, source_target_pairs={{0,16},{4,20},{8,24},{12,28},{16,0},{20,4},{24,8},{28,12},{1,17},{... | collective-permute-start | bytes 983048 | tf_op jit(solution)/shard_map/ppermute | solution.py:19
  36.6 4.2 %collective-permute-done.2.refs_4_ = bf16[256,2048]{1,0:T(8,128)(2,1)} collective-permute-done((bf16[256,2048]{1,0:T(8,128)(2,1)}, bf16[256,2048]{1,0:T(8,128)(2,1)}, u32[]{:S(2)}, u32[]{:S(2)}) %collective-permute-start.2) | collective-permute-done | bytes 1048608 | tf_op jit(solution)/shard_map/ppermute | solution.py:19
  40.8 1.9 %shard_map.68.refs_1_.own_ref = bf16[128,2048]{1,0:T(8,128)(2,1)S(1)} custom-call(bf16[512,1024]{1,0:T(8,128)(2,1)} %collective-permute-done.refs_0_.refs_4_.refs_2_, bf16[512,128]{1,0:T(8,128)(2,1)S(1)} %get-tuple-element.24.refs_1_, bf16[128,2048]{1,0:T(8,128)(2,1)S(1)} %copy-done.5, bf16[128,2048]{1,0:T(8,128)(2,1)S(1)} %collective-permute-done.1.refs_2_.refs_3_, ...), custom_call_target="tpu_custom_call" | custom-call | flops 999999995904 | bytes 3801088 | tf_op jit(solution)/shard_map/pallas_call | solution.py:33
  44.1 16.2 %collective-permute-done.8.refs_0_ = bf16[256,1024]{1,0:T(8,128)(2,1)} collective-permute-done((bf16[256,1024]{1,0:T(8,128)(2,1)}, bf16[256,1024]{1,0:T(8,128)(2,1)}, u32[]{:S(2)}, u32[]{:S(2)}) %collective-permute-start.8) | collective-permute-done | bytes 524320 | tf_op jit(solution)/shard_map/ppermute | solution.py:19
  61.9 5.1 %collective-permute-done.10.refs_3_ = bf16[128,1280]{1,0:T(8,128)(2,1)} collective-permute-done((bf16[128,1280]{1,0:T(8,128)(2,1)}, bf16[128,1280]{1,0:T(8,128)(2,1)}, u32[]{:S(2)}, u32[]{:S(2)}) %collective-permute-start.10) | collective-permute-done | bytes 327712 | tf_op jit(solution)/shard_map/ppermute | solution.py:19
  68.6 3.8 %collective-permute-done.3.refs_2_.far_ref = bf16[128,2048]{1,0:T(8,128)(2,1)S(1)} collective-permute-done((bf16[128,2048]{1,0:T(8,128)(2,1)S(1)}, bf16[128,2048]{1,0:T(8,128)(2,1)S(1)}, u32[]{:S(2)}, u32[]{:S(2)}) %collective-permute-start.3) | collective-permute-done | bytes 524320 | tf_op jit(solution)/shard_map/ppermute | solution.py:19
  72.5 2.8 %shard_map.69.start_ref = f32[256,1024]{1,0:T(8,128)S(1)} custom-call(s32[8]{0:T(128)S(1)} %iota_xor_fusion.refs_0_.where_ref, bf16[128,2048]{1,0:T(8,128)(2,1)S(1)} %shard_map.68.refs_1_.own_ref, bf16[128,2048]{1,0:T(8,128)(2,1)S(1)} %collective-permute-done.3.refs_2_.far_ref, bf16[512,1024]{1,0:T(8,128)(2,1)S(1)} %copy-done.1, ...), custom_call_target="tpu_custom_call" | custom-call | flops 805306368 | bytes 6291488 | tf_op jit(solution)/shard_map/pallas_call | solution.py:33
  75.4 1.7 %shard_map.71.refs_0_ = bf16[256,512]{1,0:T(8,128)(2,1)S(1)} custom-call(s32[8]{0:T(128)S(1)} %iota_xor_fusion.refs_0_.where_ref, bf16[128,2048]{1,0:T(8,128)(2,1)S(1)} %shard_map.68.refs_1_.own_ref, bf16[128,2048]{1,0:T(8,128)(2,1)S(1)} %collective-permute-done.3.refs_2_.far_ref, f32[256,1024]{1,0:T(8,128)S(1)} %shard_map.69.start_ref, ...), custom_call_target="tpu_custom_call" | custom-call | flops 268435456 | bytes 4194304 | tf_op jit(solution)/shard_map/pallas_call | solution.py:370
  77.1 3.6 %collective-permute-done.11.refs_4_ = bf16[128,1280]{1,0:T(8,128)(2,1)S(1)} collective-permute-done((bf16[128,1280]{1,0:T(8,128)(2,1)}, bf16[128,1280]{1,0:T(8,128)(2,1)S(1)}, u32[]{:S(2)}, u32[]{:S(2)}) %collective-permute-start.11) | collective-permute-done | bytes 327712 | tf_op jit(solution)/shard_map/ppermute | solution.py:19
  80.7 2.1 %shard_map.73 = (f32[128,1280]{1,0:T(8,128)S(1)}, bf16[128,1280]{1,0:T(8,128)(2,1)S(1)}) custom-call(bf16[256,512]{1,0:T(8,128)(2,1)S(1)} %shard_map.71.refs_0_, bf16[512,1024]{1,0:T(8,128)(2,1)S(1)} %copy-done.1, bf16[512,1024]{1,0:T(8,128)(2,1)} %collective-permute-done.refs_0_.refs_4_.refs_2_, bf16[128,1280]{1,0:T(8,128)(2,1)} %collective-permute-done.10.refs_3_, ...), custom_call_target="tpu_custom_call" | custom-call | flops 335544320 | bytes 3997696 | tf_op jit(solution)/shard_map/pallas_call | solution.py:33
  82.9 1.6 %collective-permute-start.17 = (bf16[128,768]{1,0:T(8,128)(2,1)S(1)}, bf16[128,768]{1,0:T(8,128)(2,1)S(1)}, u32[]{:S(2)}, u32[]{:S(2)}) collective-permute-start(bf16[128,768]{1,0:T(8,128)(2,1)S(1)} %collective-permute-done.16.refs_3_), channel_id=1, source_target_pairs={{0,4},{4,0},{8,12},{12,8},{16,20},{20,16},{24,28},{28,24},{1,5},{5... | collective-permute-start | bytes 589832 | tf_op jit(solution)/shard_map/ppermute | solution.py:19
  84.5 4.2 %collective-permute-done.17.refs_4_ = bf16[128,768]{1,0:T(8,128)(2,1)S(1)} collective-permute-done((bf16[128,768]{1,0:T(8,128)(2,1)S(1)}, bf16[128,768]{1,0:T(8,128)(2,1)S(1)}, u32[]{:S(2)}, u32[]{:S(2)}) %collective-permute-start.17) | collective-permute-done | bytes 196640 | tf_op jit(solution)/shard_map/ppermute | solution.py:19
  88.6 1.8 %shard_map.77 = (f32[128,768]{1,0:T(8,128)S(1)}, bf16[128,768]{1,0:T(8,128)(2,1)S(1)}) custom-call(bf16[256,512]{1,0:T(8,128)(2,1)S(1)} %shard_map.71.refs_0_, bf16[512,1024]{1,0:T(8,128)(2,1)S(1)} %copy-done.1, bf16[512,1024]{1,0:T(8,128)(2,1)} %collective-permute-done.refs_0_.refs_4_.refs_2_, bf16[128,768]{1,0:T(8,128)(2,1)S(1)} %collective-permute-done.16.refs_3_, ...), custom_call_target="tpu_custom_call" | custom-call | flops 201326592 | bytes 3342336 | tf_op jit(solution)/shard_map/pallas_call | solution.py:33
  90.5 2.0 %collective-permute-start.18 = (bf16[128,768]{1,0:T(8,128)(2,1)S(1)}, bf16[128,768]{1,0:T(8,128)(2,1)S(1)}, u32[]{:S(2)}, u32[]{:S(2)}) collective-permute-start(bf16[128,768]{1,0:T(8,128)(2,1)S(1)} %get-tuple-element.34), channel_id=1, source_target_pairs={{0,8},{4,12},{8,0},{12,4},{16,24},{20,28},{24,16},{28,20},{1,9},{5... | collective-permute-start | bytes 589832 | tf_op jit(solution)/shard_map/ppermute | solution.py:19
  93.1 1.6 %collective-permute-start.14 = (bf16[64,1408]{1,0:T(8,128)(2,1)S(1)}, bf16[64,1408]{1,0:T(8,128)(2,1)S(1)}, u32[]{:S(2)}, u32[]{:S(2)}) collective-permute-start(bf16[64,1408]{1,0:T(8,128)(2,1)S(1)} %get-tuple-element.29), channel_id=1, source_target_pairs={{0,2},{1,3},{2,0},{3,1},{4,6},{5,7},{6,4},{7,5},{8,10},{9,11},{10,... | collective-permute-start | bytes 540680 | tf_op jit(solution)/shard_map/ppermute | solution.py:19
  96.6 1.6 %collective-permute-start.20 = (bf16[64,768]{1,0:T(8,128)(2,1)S(1)}, bf16[64,768]{1,0:T(8,128)(2,1)S(1)}, u32[]{:S(2)}, u32[]{:S(2)}) collective-permute-start(bf16[64,768]{1,0:T(8,128)(2,1)S(1)} %get-tuple-element.37), channel_id=1, source_target_pairs={{0,2},{1,3},{2,0},{3,1},{4,6},{5,7},{6,4},{7,5},{8,10},{9,11},{10,... | collective-permute-start | bytes 294920 | tf_op jit(solution)/shard_map/ppermute | solution.py:19
  98.5 2.0 %collective-permute-done.14.refs_2_ = bf16[64,1408]{1,0:T(8,128)(2,1)S(1)} collective-permute-done((bf16[64,1408]{1,0:T(8,128)(2,1)S(1)}, bf16[64,1408]{1,0:T(8,128)(2,1)S(1)}, u32[]{:S(2)}, u32[]{:S(2)}) %collective-permute-start.14) | collective-permute-done | bytes 180256 | tf_op jit(solution)/shard_map/ppermute | solution.py:19
  100.5 3.0 %collective-permute-done.15.refs_3_ = bf16[64,1408]{1,0:T(8,128)(2,1)S(1)} collective-permute-done((bf16[64,1408]{1,0:T(8,128)(2,1)S(1)}, bf16[64,1408]{1,0:T(8,128)(2,1)S(1)}, u32[]{:S(2)}, u32[]{:S(2)}) %collective-permute-start.15) | collective-permute-done | bytes 180256 | tf_op jit(solution)/shard_map/ppermute | solution.py:19
  104.1 2.4 %collective-permute-done.20.refs_4_ = bf16[64,768]{1,0:T(8,128)(2,1)S(1)} collective-permute-done((bf16[64,768]{1,0:T(8,128)(2,1)S(1)}, bf16[64,768]{1,0:T(8,128)(2,1)S(1)}, u32[]{:S(2)}, u32[]{:S(2)}) %collective-permute-start.20) | collective-permute-done | bytes 98336 | tf_op jit(solution)/shard_map/ppermute | solution.py:19
  (54 shorter events, 21.7 us)
Async XLA Ops:
  0.0 14.8 %collective-permute-start.1 = (bf16[128,2048]{1,0:T(8,128)(2,1)}, bf16[128,2048]{1,0:T(8,128)(2,1)S(1)}, u32[]{:S(2)}, u32[]{:S(2)}) collective-permute-start(bf16[128,2048]{1,0:T(8,128)(2,1)} %refs_2_.1), channel_id=1, source_target_pairs={{0,1},{1,0},{2,3},{3,2},{4,5},{5,4},{6,7},{7,6},{8,9},{9,8},{10,11... | collective-permute-start | bytes 1572872 | tf_op jit(solution)/shard_map/ppermute | solution.py:19
  2.4 17.9 %collective-permute-start.6 = (bf16[256,1024]{1,0:T(8,128)(2,1)}, bf16[256,1024]{1,0:T(8,128)(2,1)}, u32[]{:S(2)}, u32[]{:S(2)}) collective-permute-start(bf16[256,1024]{1,0:T(8,128)(2,1)} %shard_map.66.refs_0_), channel_id=1, source_target_pairs={{0,24},{4,28},{8,16},{12,20},{16,8},{20,12},{24,0},{28,4},{1,25},{... | collective-permute-start | bytes 1572872 | tf_op jit(solution)/shard_map/ppermute | solution.py:19
  7.1 26.1 %collective-permute-start.4 = (bf16[256,1024]{1,0:T(8,128)(2,1)}, bf16[256,1024]{1,0:T(8,128)(2,1)}, u32[]{:S(2)}, u32[]{:S(2)}) collective-permute-start(bf16[256,1024]{1,0:T(8,128)(2,1)} %shard_map.66.refs_0_), channel_id=1, source_target_pairs={{0,8},{4,12},{8,0},{12,4},{16,24},{20,28},{24,16},{28,20},{1,9},{5... | collective-permute-start | bytes 1572872 | tf_op jit(solution)/shard_map/ppermute | solution.py:19
  9.4 25.7 %collective-permute-start = (bf16[512,1024]{1,0:T(8,128)(2,1)}, bf16[512,1024]{1,0:T(8,128)(2,1)}, u32[]{:S(2)}, u32[]{:S(2)}) collective-permute-start(bf16[512,1024]{1,0:T(8,128)(2,1)} %shard_map.65.refs_3_.refs_0_.refs_1_), channel_id=1, source_target_pairs={{0,4},{4,0},{8,12},{12,8},{16,20},{20,16},{24,28},{28,24},{1,5},{5... | collective-permute-start | bytes 3145736 | tf_op jit(solution)/shard_map/ppermute | solution.py:19
  13.1 47.3 %collective-permute-start.8 = (bf16[256,1024]{1,0:T(8,128)(2,1)}, bf16[256,1024]{1,0:T(8,128)(2,1)}, u32[]{:S(2)}, u32[]{:S(2)}) collective-permute-start(bf16[256,1024]{1,0:T(8,128)(2,1)} %shard_map.70), channel_id=1, source_target_pairs={{0,16},{4,20},{8,24},{12,28},{16,0},{20,4},{24,8},{28,12},{1,17},{... | collective-permute-start | bytes 1572872 | tf_op jit(solution)/shard_map/ppermute | solution.py:19
  15.9 24.9 %collective-permute-start.2 = (bf16[256,2048]{1,0:T(8,128)(2,1)}, bf16[256,2048]{1,0:T(8,128)(2,1)}, u32[]{:S(2)}, u32[]{:S(2)}) collective-permute-start(bf16[256,2048]{1,0:T(8,128)(2,1)} %shard_map.67), channel_id=1, source_target_pairs={{0,2},{1,3},{2,0},{3,1},{4,6},{5,7},{6,4},{7,5},{8,10},{9,11},{10,... | collective-permute-start | bytes 3145736 | tf_op jit(solution)/shard_map/ppermute | solution.py:19
  21.1 45.9 %collective-permute-start.10 = (bf16[128,1280]{1,0:T(8,128)(2,1)}, bf16[128,1280]{1,0:T(8,128)(2,1)}, u32[]{:S(2)}, u32[]{:S(2)}) collective-permute-start(bf16[128,1280]{1,0:T(8,128)(2,1)} %shard_map.72), channel_id=1, source_target_pairs={{0,16},{4,20},{8,24},{12,28},{16,0},{20,4},{24,8},{28,12},{1,17},{... | collective-permute-start | bytes 983048 | tf_op jit(solution)/shard_map/ppermute | solution.py:19
  33.1 35.5 %collective-permute-start.7 = (bf16[256,1024]{1,0:T(8,128)(2,1)}, bf16[256,1024]{1,0:T(8,128)(2,1)}, u32[]{:S(2)}, u32[]{:S(2)}) collective-permute-start(bf16[256,1024]{1,0:T(8,128)(2,1)} %collective-permute-done.6.refs_8_.refs_0_), channel_id=1, source_target_pairs={{0,4},{4,0},{8,12},{12,8},{16,20},{20,16},{24,28},{28,24},{1,5},{5... | collective-permute-start | bytes 1572872 | tf_op jit(solution)/shard_map/ppermute | solution.py:19
  35.1 33.5 %collective-permute-start.5 = (bf16[256,1024]{1,0:T(8,128)(2,1)}, bf16[256,1024]{1,0:T(8,128)(2,1)}, u32[]{:S(2)}, u32[]{:S(2)}) collective-permute-start(bf16[256,1024]{1,0:T(8,128)(2,1)} %collective-permute-done.4.refs_7_), channel_id=1, source_target_pairs={{0,4},{4,0},{8,12},{12,8},{16,20},{20,16},{24,28},{28,24},{1,5},{5... | collective-permute-start | bytes 1572872 | tf_op jit(solution)/shard_map/ppermute | solution.py:19
  40.8 27.7 %copy-start.4 = (bf16[1,128,2048]{2,1,0:T(8,128)(2,1)S(1)}, bf16[1,128,2048]{2,1,0:T(8,128)(2,1)}, u32[]{:S(2)}) copy-start(bf16[1,128,2048]{2,1,0:T(8,128)(2,1)} %refs_1_.5) | copy-start | bytes 1572868
  42.7 29.8 %copy-start.1 = (bf16[512,1024]{1,0:T(8,128)(2,1)S(1)}, bf16[512,1024]{1,0:T(8,128)(2,1)}, u32[]{:S(2)}) copy-start(bf16[512,1024]{1,0:T(8,128)(2,1)} %shard_map.65.refs_3_.refs_0_.refs_1_) | copy-start | bytes 3145732
  42.7 29.8 %collective-permute-start.3 = (bf16[128,2048]{1,0:T(8,128)(2,1)S(1)}, bf16[128,2048]{1,0:T(8,128)(2,1)S(1)}, u32[]{:S(2)}, u32[]{:S(2)}) collective-permute-start(bf16[128,2048]{1,0:T(8,128)(2,1)S(1)} %shard_map.68.refs_1_.own_ref), channel_id=1, source_target_pairs={{0,8},{4,12},{8,0},{12,4},{16,24},{20,28},{24,16},{28,20},{1,9},{5... | collective-permute-start | bytes 1572872 | tf_op jit(solution)/shard_map/ppermute | solution.py:19
  60.3 15.1 %collective-permute-start.9 = (bf16[256,1024]{1,0:T(8,128)(2,1)}, bf16[256,1024]{1,0:T(8,128)(2,1)S(1)}, u32[]{:S(2)}, u32[]{:S(2)}) collective-permute-start(bf16[256,1024]{1,0:T(8,128)(2,1)} %collective-permute-done.8.refs_0_), channel_id=1, source_target_pairs={{0,4},{4,0},{8,12},{12,8},{16,20},{20,16},{24,28},{28,24},{1,5},{5... | collective-permute-start | bytes 1572872 | tf_op jit(solution)/shard_map/ppermute | solution.py:19
  67.0 13.7 %collective-permute-start.11 = (bf16[128,1280]{1,0:T(8,128)(2,1)}, bf16[128,1280]{1,0:T(8,128)(2,1)S(1)}, u32[]{:S(2)}, u32[]{:S(2)}) collective-permute-start(bf16[128,1280]{1,0:T(8,128)(2,1)} %collective-permute-done.10.refs_3_), channel_id=1, source_target_pairs={{0,4},{4,0},{8,12},{12,8},{16,20},{20,16},{24,28},{28,24},{1,5},{5... | collective-permute-start | bytes 983048 | tf_op jit(solution)/shard_map/ppermute | solution.py:19
  68.5 14.4 %collective-permute-start.16 = (bf16[128,768]{1,0:T(8,128)(2,1)S(1)}, bf16[128,768]{1,0:T(8,128)(2,1)S(1)}, u32[]{:S(2)}, u32[]{:S(2)}) collective-permute-start(bf16[128,768]{1,0:T(8,128)(2,1)S(1)} %shard_map.76), channel_id=1, source_target_pairs={{0,16},{4,20},{8,24},{12,28},{16,0},{20,4},{24,8},{28,12},{1,17},{... | collective-permute-start | bytes 589832 | tf_op jit(solution)/shard_map/ppermute | solution.py:19
  82.8 9.8 %collective-permute-start.12 = (bf16[128,1280]{1,0:T(8,128)(2,1)S(1)}, bf16[128,1280]{1,0:T(8,128)(2,1)S(1)}, u32[]{:S(2)}, u32[]{:S(2)}) collective-permute-start(bf16[128,1280]{1,0:T(8,128)(2,1)S(1)} %get-tuple-element.26), channel_id=1, source_target_pairs={{0,8},{4,12},{8,0},{12,4},{16,24},{20,28},{24,16},{28,20},{1,9},{5... | collective-permute-start | bytes 983048 | tf_op jit(solution)/shard_map/ppermute | solution.py:19
  82.9 5.7 %collective-permute-start.17 = (bf16[128,768]{1,0:T(8,128)(2,1)S(1)}, bf16[128,768]{1,0:T(8,128)(2,1)S(1)}, u32[]{:S(2)}, u32[]{:S(2)}) collective-permute-start(bf16[128,768]{1,0:T(8,128)(2,1)S(1)} %collective-permute-done.16.refs_3_), channel_id=1, source_target_pairs={{0,4},{4,0},{8,12},{12,8},{16,20},{20,16},{24,28},{28,24},{1,5},{5... | collective-permute-start | bytes 589832 | tf_op jit(solution)/shard_map/ppermute | solution.py:19
  90.5 5.7 %collective-permute-start.18 = (bf16[128,768]{1,0:T(8,128)(2,1)S(1)}, bf16[128,768]{1,0:T(8,128)(2,1)S(1)}, u32[]{:S(2)}, u32[]{:S(2)}) collective-permute-start(bf16[128,768]{1,0:T(8,128)(2,1)S(1)} %get-tuple-element.34), channel_id=1, source_target_pairs={{0,8},{4,12},{8,0},{12,4},{16,24},{20,28},{24,16},{28,20},{1,9},{5... | collective-permute-start | bytes 589832 | tf_op jit(solution)/shard_map/ppermute | solution.py:19
  93.0 5.2 %collective-permute-start.13 = (bf16[64,1408]{1,0:T(8,128)(2,1)S(1)}, bf16[64,1408]{1,0:T(8,128)(2,1)S(1)}, u32[]{:S(2)}, u32[]{:S(2)}) collective-permute-start(bf16[64,1408]{1,0:T(8,128)(2,1)S(1)} %get-tuple-element.28), channel_id=1, source_target_pairs={{0,1},{1,0},{2,3},{3,2},{4,5},{5,4},{6,7},{7,6},{8,9},{9,8},{10,11... | collective-permute-start | bytes 540680 | tf_op jit(solution)/shard_map/ppermute | solution.py:19
  93.1 7.4 %collective-permute-start.14 = (bf16[64,1408]{1,0:T(8,128)(2,1)S(1)}, bf16[64,1408]{1,0:T(8,128)(2,1)S(1)}, u32[]{:S(2)}, u32[]{:S(2)}) collective-permute-start(bf16[64,1408]{1,0:T(8,128)(2,1)S(1)} %get-tuple-element.29), channel_id=1, source_target_pairs={{0,2},{1,3},{2,0},{3,1},{4,6},{5,7},{6,4},{7,5},{8,10},{9,11},{10,... | collective-permute-start | bytes 540680 | tf_op jit(solution)/shard_map/ppermute | solution.py:19
  94.6 8.8 %collective-permute-start.15 = (bf16[64,1408]{1,0:T(8,128)(2,1)S(1)}, bf16[64,1408]{1,0:T(8,128)(2,1)S(1)}, u32[]{:S(2)}, u32[]{:S(2)}) collective-permute-start(bf16[64,1408]{1,0:T(8,128)(2,1)S(1)} %get-tuple-element.30), channel_id=1, source_target_pairs={{0,3},{1,2},{2,1},{3,0},{4,7},{5,6},{6,5},{7,4},{8,11},{9,10},{10,... | collective-permute-start | bytes 540680 | tf_op jit(solution)/shard_map/ppermute | solution.py:19
  96.5 7.5 %collective-permute-start.19 = (bf16[64,768]{1,0:T(8,128)(2,1)S(1)}, bf16[64,768]{1,0:T(8,128)(2,1)S(1)}, u32[]{:S(2)}, u32[]{:S(2)}) collective-permute-start(bf16[64,768]{1,0:T(8,128)(2,1)S(1)} %get-tuple-element.36), channel_id=1, source_target_pairs={{0,1},{1,0},{2,3},{3,2},{4,5},{5,4},{6,7},{7,6},{8,9},{9,8},{10,11... | collective-permute-start | bytes 294920 | tf_op jit(solution)/shard_map/ppermute | solution.py:19
  96.6 9.8 %collective-permute-start.20 = (bf16[64,768]{1,0:T(8,128)(2,1)S(1)}, bf16[64,768]{1,0:T(8,128)(2,1)S(1)}, u32[]{:S(2)}, u32[]{:S(2)}) collective-permute-start(bf16[64,768]{1,0:T(8,128)(2,1)S(1)} %get-tuple-element.37), channel_id=1, source_target_pairs={{0,2},{1,3},{2,0},{3,1},{4,6},{5,7},{6,4},{7,5},{8,10},{9,11},{10,... | collective-permute-start | bytes 294920 | tf_op jit(solution)/shard_map/ppermute | solution.py:19
  98.2 9.5 %collective-permute-start.21 = (bf16[64,768]{1,0:T(8,128)(2,1)S(1)}, bf16[64,768]{1,0:T(8,128)(2,1)S(1)}, u32[]{:S(2)}, u32[]{:S(2)}) collective-permute-start(bf16[64,768]{1,0:T(8,128)(2,1)S(1)} %get-tuple-element.38), channel_id=1, source_target_pairs={{0,3},{1,2},{2,1},{3,0},{4,7},{5,6},{6,5},{7,4},{8,11},{9,10},{10,... | collective-permute-start | bytes 294920 | tf_op jit(solution)/shard_map/ppermute | solution.py:19
  (6 other events, 14.6 us)

commit v4 on v3

--- a/solution.py
+++ b/solution.py
@@ -7,7 +7,7 @@
 from jax.experimental.pallas import tpu as pltpu
 from jax.sharding import PartitionSpec as P
 
-SHARES = (5, 3)
+SHARES = (9, 7)
 OPENING_LIMIT = 60 * 2**20
 LONG = 10**12
 F32 = jnp.float32
@@ -285,7 +285,6 @@
     came = swap(across, "dp", 1)
     weights = {mask: swap(other_units, "dp", mask) for mask in far[::2]}
 
-    weights[2] = swap(other_units, "dp", 2)
 
     def down_far(piece):
         own, bit = [piece], 4
@@ -295,7 +294,8 @@
             bit *= 2
         return own[1:]
 
-    late_same = call(hand, [shape(rows_shard, units)], across)[0]
+    late_same, late_other = call(hand, [shape(rows_shard, units)] * 2, across, other_units)
+    weights[2] = swap(late_other, "dp", 2)
     for mask in far[1::2]:
         weights[mask] = swap(late_same, "dp", mask)
 
@@ -307,6 +307,13 @@
             have = call(join, shape(bit * tok_dev, width), *group, wait=[other_units])
         group.append(swap(have, "expert", bit))
         bit *= 2
+    piece = call(
+        functools.partial(cut, start=0),
+        shape(down_rows, steps[0]),
+        w_down,
+        wait=[weights[far[0]]],
+        flops=LONG,
+    )
     pick_hot, place_hot, tags = call(
         functools.partial(own_tables, experts=experts, tok_dev=tok_dev),
         [shape(experts * tok_dev, capacity), shape(experts * most, capacity), shape(experts * most, 128)],
@@ -319,7 +326,7 @@
         shape(capacity, width),
         pick_hot,
         *group,
-        wait=[came],
+        wait=[came, piece],
         flops=LONG,
     )
     picked_z = swap(picked, "dp", 2)
@@ -328,24 +335,26 @@
     for mask in far[1::2]:
         weights[mask + 1] = swap(weights[mask], "dp", 1)
 
-    down, down_far_y = [], []
-    for index in range(len(SHARES)):
+    down, down_far_y = [down_far(piece)], []
+    for index in range(1, len(SHARES)):
         piece = call(
             functools.partial(cut, start=starts[index]),
             shape(down_rows, steps[index]),
             w_down,
-            wait=[weights[far[0]]] if index == 0 else [weights[far[-1]]] if index == 1 else down[-1],
-            flops=LONG if index == 0 else 0,
+            wait=[weights[far[-1]], piece],
         )
         down.append(down_far(piece))
-        down_far_y.append([swap(x, "dp", 1) for x in down[-1]])
+    down_far_y.append([swap(x, "dp", 1) for x in down[0]])
 
     order = replica ^ jnp.arange(replicas, dtype=jnp.int32)
-    late = [mask for mask in range(2, replicas) if mask & ~1 in far[1::2]]
+    late = [mask + 1 for mask in far[1::2]]
     arrays = [across, came, *came_far, *[weights[mask] for mask in group_far]]
     places = [(0, 0, rows_shard, 0), (1, 0, rows_shard, 1)]
     for i, mask in enumerate(group_far):
         places += [(2 + len(group_far) + i, 0, rows_shard, mask), (2 + i, 0, rows_shard, mask + 1)]
+    for mask in far[1::2]:
+        places.append((len(arrays), 0, rows_shard, mask))
+        arrays.append(weights[mask])
     late_arrays = [weights[mask] for mask in late]
     late_places = [(i, 0, rows_shard, mask) for i, mask in enumerate(late)]
     if rows_shard % 128 != 0:
@@ -385,6 +394,10 @@
     gate_column = gate_weights[0, 0][:, None]
     results = []
     for index, (start, step, far_rows) in enumerate(zip(starts, steps, down)):
+        if index > 0:
+            held = call(hand, [shape(*x.shape) for x in far_rows], *far_rows, wait=[away])
+            down_far_y.append([swap(x, "dp", 1) for x in held])
+
         def pieces(array, first, at, end):
             cuts = [(at, min(end, units)), (max(at, units), end)]
             return [
@@ -402,7 +415,8 @@
             [shape(capacity, step, dtype=F32), shape(capacity, step)],
             hidden,
             *parts,
-            flops=2 * capacity * units * step,
+            wait=[away, sent[0]] if index else [],
+            flops=LONG if index else 2 * capacity * units * step,
         )
         extra = 128 if index == 0 else 0
         sent = call(

time: 109 us -> 106 us (0.972)
  starting transfers between devices: 36.2 us -> 23.9 us
  waiting for transfers between devices: 50.4 us -> 59.8 us
    ppermute x22, starting transfers between devices: 36.2 us -> 23.9 us  [swap(): return lax.ppermute(value, axis, pairs)]
    ppermute x22, waiting for transfers between devices: 50.4 us -> 59.8 us  [swap(): return lax.ppermute(value, axis, pairs)]
    pallas_call x13 -> x14, Pallas kernels: 14.1 us -> 13.8 us  [call(): pl.pallas_call(body, out_shape=out_shape, in_specs=in_specs, out_specs=ja...]
  transfers between devices with their start and end apart: 22 -> 22, of which waited for: 14 -> 15; matrix products, arithmetic and copies ran while one was open for 0% -> 0% of each run, Pallas kernels for 17% -> 15%
where the time goes in v4:
time: 106 us; the launch traced here: 105 us
  waiting for transfers between devices  59.8 us (56%)
  starting transfers between devices  23.9 us (23%)
  Pallas kernels  19.1 us (18%)
  local copies, waits for them, and re-layouts  2.18 us (2%)
    ppermute x22, waiting for transfers between devices, swap(): return lax.ppermute(value, axis, pairs)  59.8 us
    ppermute x22, starting transfers between devices, swap(): return lax.ppermute(value, axis, pairs)  23.9 us
    pallas_call x14, Pallas kernels, call(): pl.pallas_call(body, out_shape=out_shape, in_specs=in_specs, out_specs=ja...  13.8 us
    pallas_call x2, Pallas kernels, collect(): pl.pallas_call(functools.partial(opening, flip=flip, pairs=pairs), out_sh...  4.24 us
  transfers between devices with their start and end apart: 22, of which 15 were waited for; matrix products, arithmetic and copies ran while one was open for 0% of the time, Pallas kernels for 15%

profile of v4, /device:TPU:0, one launch (start us, length us, event | category | flops | bytes accessed | tf_op | source)
XLA Modules:
  0.0 105.2 jit_solution(7406284616518925691)
XLA Ops:
  0.5 1.9 %shard_map.66.refs_0_.refs_1_ = bf16[256,1024]{1,0:T(8,128)(2,1)} custom-call(s32[1]{0:T(128)} %bitcast.3.bit_ref, bf16[1,256,1024]{2,1,0:T(8,128)(2,1)} %gate_ref.3, bf16[1,256,1024]{2,1,0:T(8,128)(2,1)} %up_ref.3), custom_call_target="tpu_custom_call" | custom-call | bytes 1048576 | tf_op jit(solution)/shard_map/pallas_call | solution.py:256
  2.4 4.7 %collective-permute-start.1 = (bf16[256,1024]{1,0:T(8,128)(2,1)}, bf16[256,1024]{1,0:T(8,128)(2,1)}, u32[]{:S(2)}, u32[]{:S(2)}) collective-permute-start(bf16[256,1024]{1,0:T(8,128)(2,1)} %shard_map.66.refs_0_.refs_1_), channel_id=1, source_target_pairs={{0,24},{4,28},{8,16},{12,20},{16,8},{20,12},{24,0},{28,4},{1,25},{... | collective-permute-start | bytes 1572872 | tf_op jit(solution)/shard_map/ppermute | solution.py:19
  7.1 2.3 %shard_map.65.refs_0_.refs_3_.refs_1_ = bf16[512,1024]{1,0:T(8,128)(2,1)} custom-call(s32[1]{0:T(128)} %bitcast.3.bit_ref, bf16[1,256,1024]{2,1,0:T(8,128)(2,1)} %gate_ref.3, bf16[1,256,1024]{2,1,0:T(8,128)(2,1)} %up_ref.3, bf16[1,128,2048]{2,1,0:T(8,128)(2,1)} %refs_2_.1), custom_call_target="tpu_custom_call" | custom-call | bytes 1048576 | tf_op jit(solution)/shard_map/pallas_call | solution.py:256
  9.4 1.6 %collective-permute-start = (bf16[512,1024]{1,0:T(8,128)(2,1)}, bf16[512,1024]{1,0:T(8,128)(2,1)}, u32[]{:S(2)}, u32[]{:S(2)}) collective-permute-start(bf16[512,1024]{1,0:T(8,128)(2,1)} %shard_map.65.refs_0_.refs_3_.refs_1_), channel_id=1, source_target_pairs={{0,4},{4,0},{8,12},{12,8},{16,20},{20,16},{24,28},{28,24},{1,5},{5... | collective-permute-start | bytes 3145736 | tf_op jit(solution)/shard_map/ppermute | solution.py:19
  17.6 2.7 %collective-permute-done.1.refs_0_.refs_8_ = bf16[256,1024]{1,0:T(8,128)(2,1)} collective-permute-done((bf16[256,1024]{1,0:T(8,128)(2,1)}, bf16[256,1024]{1,0:T(8,128)(2,1)}, u32[]{:S(2)}, u32[]{:S(2)}) %collective-permute-start.1) | collective-permute-done | bytes 524320 | tf_op jit(solution)/shard_map/ppermute | solution.py:19
  20.3 1.7 %collective-permute-start.7 = (bf16[256,1024]{1,0:T(8,128)(2,1)}, bf16[256,1024]{1,0:T(8,128)(2,1)}, u32[]{:S(2)}, u32[]{:S(2)}) collective-permute-start(bf16[256,1024]{1,0:T(8,128)(2,1)} %collective-permute-done.1.refs_0_.refs_8_), channel_id=1, source_target_pairs={{0,4},{4,0},{8,12},{12,8},{16,20},{20,16},{24,28},{28,24},{1,5},{5... | collective-permute-start | bytes 1572872 | tf_op jit(solution)/shard_map/ppermute | solution.py:19
  22.0 10.4 %collective-permute-done.5.refs_7_ = bf16[256,1024]{1,0:T(8,128)(2,1)} collective-permute-done((bf16[256,1024]{1,0:T(8,128)(2,1)}, bf16[256,1024]{1,0:T(8,128)(2,1)}, u32[]{:S(2)}, u32[]{:S(2)}) %collective-permute-start.5) | collective-permute-done | bytes 524320 | tf_op jit(solution)/shard_map/ppermute | solution.py:19
  33.9 1.9 %collective-permute-done.refs_0_.refs_4_.refs_2_ = bf16[512,1024]{1,0:T(8,128)(2,1)} collective-permute-done((bf16[512,1024]{1,0:T(8,128)(2,1)}, bf16[512,1024]{1,0:T(8,128)(2,1)}, u32[]{:S(2)}, u32[]{:S(2)}) %collective-permute-start) | collective-permute-done | bytes 1048608 | tf_op jit(solution)/shard_map/ppermute | solution.py:19
  35.8 5.2 %collective-permute-done.3.refs_5_ = bf16[256,2048]{1,0:T(8,128)(2,1)} collective-permute-done((bf16[256,2048]{1,0:T(8,128)(2,1)}, bf16[256,2048]{1,0:T(8,128)(2,1)}, u32[]{:S(2)}, u32[]{:S(2)}) %collective-permute-start.3) | collective-permute-done | bytes 1048608 | tf_op jit(solution)/shard_map/ppermute | solution.py:19
  41.0 1.9 %shard_map.69.refs_1_.own_ref = bf16[128,2048]{1,0:T(8,128)(2,1)S(1)} custom-call(bf16[512,1024]{1,0:T(8,128)(2,1)} %collective-permute-done.refs_0_.refs_4_.refs_2_, bf16[128,1152]{1,0:T(8,128)(2,1)S(1)} %shard_map.67.refs_1_, bf16[512,128]{1,0:T(8,128)(2,1)S(1)} %get-tuple-element.26.refs_2_, bf16[128,2048]{1,0:T(8,128)(2,1)S(1)} %copy-done.5, ...), custom_call_target="tpu_custom_call" | custom-call | flops 999999995904 | bytes 4096000 | tf_op jit(solution)/shard_map/pallas_call | solution.py:33
  44.3 2.6 %collective-permute-start.10 = (bf16[128,1152]{1,0:T(8,128)(2,1)S(1)}, bf16[128,1152]{1,0:T(8,128)(2,1)S(1)}, u32[]{:S(2)}, u32[]{:S(2)}) collective-permute-start(bf16[128,1152]{1,0:T(8,128)(2,1)S(1)} %shard_map.67.refs_1_), channel_id=1, source_target_pairs={{0,16},{4,20},{8,24},{12,28},{16,0},{20,4},{24,8},{28,12},{1,17},{... | collective-permute-start | bytes 884744 | tf_op jit(solution)/shard_map/ppermute | solution.py:19
  47.0 6.4 %collective-permute-done.8.refs_9_.refs_0_ = bf16[256,1024]{1,0:T(8,128)(2,1)} collective-permute-done((bf16[256,1024]{1,0:T(8,128)(2,1)}, bf16[256,1024]{1,0:T(8,128)(2,1)}, u32[]{:S(2)}, u32[]{:S(2)}) %collective-permute-start.8) | collective-permute-done | bytes 524320 | tf_op jit(solution)/shard_map/ppermute | solution.py:19
  54.9 10.7 %collective-permute-done.10.refs_3_ = bf16[128,1152]{1,0:T(8,128)(2,1)S(1)} collective-permute-done((bf16[128,1152]{1,0:T(8,128)(2,1)S(1)}, bf16[128,1152]{1,0:T(8,128)(2,1)S(1)}, u32[]{:S(2)}, u32[]{:S(2)}) %collective-permute-start.10) | collective-permute-done | bytes 294944 | tf_op jit(solution)/shard_map/ppermute | solution.py:19
  67.2 3.1 %collective-permute-done.4.refs_2_.far_ref = bf16[128,2048]{1,0:T(8,128)(2,1)S(1)} collective-permute-done((bf16[128,2048]{1,0:T(8,128)(2,1)S(1)}, bf16[128,2048]{1,0:T(8,128)(2,1)S(1)}, u32[]{:S(2)}, u32[]{:S(2)}) %collective-permute-start.4) | collective-permute-done | bytes 524320 | tf_op jit(solution)/shard_map/ppermute | solution.py:19
  70.3 3.1 %shard_map.71.start_ref = f32[256,1024]{1,0:T(8,128)S(1)} custom-call(s32[8]{0:T(128)S(1)} %iota_xor_fusion.refs_0_.where_ref, bf16[128,2048]{1,0:T(8,128)(2,1)S(1)} %shard_map.69.refs_1_.own_ref, bf16[128,2048]{1,0:T(8,128)(2,1)S(1)} %collective-permute-done.4.refs_2_.far_ref, bf16[512,1024]{1,0:T(8,128)(2,1)S(1)} %copy-done.1, ...), custom_call_target="tpu_custom_call" | custom-call | flops 805306368 | bytes 6815776 | tf_op jit(solution)/shard_map/pallas_call | solution.py:33
  75.0 2.0 %shard_map.73 = (f32[128,1152]{1,0:T(8,128)S(1)}, bf16[128,1152]{1,0:T(8,128)(2,1)S(1)}) custom-call(bf16[256,512]{1,0:T(8,128)(2,1)S(1)} %shard_map.72.refs_0_.refs_2_, bf16[512,1024]{1,0:T(8,128)(2,1)S(1)} %copy-done.1, bf16[512,1024]{1,0:T(8,128)(2,1)} %collective-permute-done.refs_0_.refs_4_.refs_2_, ...), custom_call_target="tpu_custom_call" | custom-call | flops 301989888 | bytes 3833856 | tf_op jit(solution)/shard_map/pallas_call | solution.py:33
  77.0 2.8 %collective-permute-done.16.refs_1_.refs_5_ = bf16[128,896]{1,0:T(8,128)(2,1)S(1)} collective-permute-done((bf16[128,896]{1,0:T(8,128)(2,1)S(1)}, bf16[128,896]{1,0:T(8,128)(2,1)S(1)}, u32[]{:S(2)}, u32[]{:S(2)}) %collective-permute-start.16) | collective-permute-done | bytes 229408 | tf_op jit(solution)/shard_map/ppermute | solution.py:19
  80.6 5.5 %collective-permute-done.12.refs_4_ = bf16[128,1152]{1,0:T(8,128)(2,1)S(1)} collective-permute-done((bf16[128,1152]{1,0:T(8,128)(2,1)S(1)}, bf16[128,1152]{1,0:T(8,128)(2,1)S(1)}, u32[]{:S(2)}, u32[]{:S(2)}) %collective-permute-start.12) | collective-permute-done | bytes 294944 | tf_op jit(solution)/shard_map/ppermute | solution.py:19
  87.4 1.8 %shard_map.78 = (f32[128,896]{1,0:T(8,128)S(1)}, bf16[128,896]{1,0:T(8,128)(2,1)S(1)}) custom-call(bf16[128,1152]{1,0:T(8,128)(2,1)S(1)} %get-tuple-element.30.refs_0_, bf16[64,1280]{1,0:T(8,128)(2,1)S(1)} %get-tuple-element.31.refs_0_.refs_1_, bf16[256,512]{1,0:T(8,128)(2,1)S(1)} %shard_map.72.refs_0_.refs_2_, bf16[512,1024]{1,0:T(8,128)(2,1)S(1)} %copy-done.1, ...), custom_call_target="tpu_custom_call" | custom-call | flops 999999995904 | bytes 3964928 | tf_op jit(solution)/shard_map/pallas_call | solution.py:33
  89.4 1.6 %collective-permute-start.14 = (bf16[64,1280]{1,0:T(8,128)(2,1)S(1)}, bf16[64,1280]{1,0:T(8,128)(2,1)S(1)}, u32[]{:S(2)}, u32[]{:S(2)}) collective-permute-start(bf16[64,1280]{1,0:T(8,128)(2,1)S(1)} %get-tuple-element.33), channel_id=1, source_target_pairs={{0,2},{1,3},{2,0},{3,1},{4,6},{5,7},{6,4},{7,5},{8,10},{9,11},{10,... | collective-permute-start | bytes 491528 | tf_op jit(solution)/shard_map/ppermute | solution.py:19
  91.2 4.7 %collective-permute-done.18.refs_4_ = bf16[128,896]{1,0:T(8,128)(2,1)S(1)} collective-permute-done((bf16[128,896]{1,0:T(8,128)(2,1)S(1)}, bf16[128,896]{1,0:T(8,128)(2,1)S(1)}, u32[]{:S(2)}, u32[]{:S(2)}) %collective-permute-start.18) | collective-permute-done | bytes 229408 | tf_op jit(solution)/shard_map/ppermute | solution.py:19
  96.3 1.6 %collective-permute-start.20 = (bf16[64,896]{1,0:T(8,128)(2,1)S(1)}, bf16[64,896]{1,0:T(8,128)(2,1)S(1)}, u32[]{:S(2)}, u32[]{:S(2)}) collective-permute-start(bf16[64,896]{1,0:T(8,128)(2,1)S(1)} %get-tuple-element.41), channel_id=1, source_target_pairs={{0,2},{1,3},{2,0},{3,1},{4,6},{5,7},{6,4},{7,5},{8,10},{9,11},{10,... | collective-permute-start | bytes 344072 | tf_op jit(solution)/shard_map/ppermute | solution.py:19
  99.6 2.7 %collective-permute-done.20.refs_4_ = bf16[64,896]{1,0:T(8,128)(2,1)S(1)} collective-permute-done((bf16[64,896]{1,0:T(8,128)(2,1)S(1)}, bf16[64,896]{1,0:T(8,128)(2,1)S(1)}, u32[]{:S(2)}, u32[]{:S(2)}) %collective-permute-start.20) | collective-permute-done | bytes 114720 | tf_op jit(solution)/shard_map/ppermute | solution.py:19
  102.4 1.7 %collective-permute-done.21.refs_5_ = bf16[64,896]{1,0:T(8,128)(2,1)S(1)} collective-permute-done((bf16[64,896]{1,0:T(8,128)(2,1)S(1)}, bf16[64,896]{1,0:T(8,128)(2,1)S(1)}, u32[]{:S(2)}, u32[]{:S(2)}) %collective-permute-start.21) | collective-permute-done | bytes 114720 | tf_op jit(solution)/shard_map/ppermute | solution.py:19
  (55 shorter events, 20.6 us)
Async XLA Ops:
  0.0 15.0 %collective-permute-start.2 = (bf16[128,2048]{1,0:T(8,128)(2,1)}, bf16[128,2048]{1,0:T(8,128)(2,1)S(1)}, u32[]{:S(2)}, u32[]{:S(2)}) collective-permute-start(bf16[128,2048]{1,0:T(8,128)(2,1)} %refs_3_.1), channel_id=1, source_target_pairs={{0,1},{1,0},{2,3},{3,2},{4,5},{5,4},{6,7},{7,6},{8,9},{9,8},{10,11... | collective-permute-start | bytes 1572872 | tf_op jit(solution)/shard_map/ppermute | solution.py:19
  2.4 17.9 %collective-permute-start.1 = (bf16[256,1024]{1,0:T(8,128)(2,1)}, bf16[256,1024]{1,0:T(8,128)(2,1)}, u32[]{:S(2)}, u32[]{:S(2)}) collective-permute-start(bf16[256,1024]{1,0:T(8,128)(2,1)} %shard_map.66.refs_0_.refs_1_), channel_id=1, source_target_pairs={{0,24},{4,28},{8,16},{12,20},{16,8},{20,12},{24,0},{28,4},{1,25},{... | collective-permute-start | bytes 1572872 | tf_op jit(solution)/shard_map/ppermute | solution.py:19
  9.4 26.4 %collective-permute-start = (bf16[512,1024]{1,0:T(8,128)(2,1)}, bf16[512,1024]{1,0:T(8,128)(2,1)}, u32[]{:S(2)}, u32[]{:S(2)}) collective-permute-start(bf16[512,1024]{1,0:T(8,128)(2,1)} %shard_map.65.refs_0_.refs_3_.refs_1_), channel_id=1, source_target_pairs={{0,4},{4,0},{8,12},{12,8},{16,20},{20,16},{24,28},{28,24},{1,5},{5... | collective-permute-start | bytes 3145736 | tf_op jit(solution)/shard_map/ppermute | solution.py:19
  13.3 19.1 %collective-permute-start.5 = (bf16[256,1024]{1,0:T(8,128)(2,1)}, bf16[256,1024]{1,0:T(8,128)(2,1)}, u32[]{:S(2)}, u32[]{:S(2)}) collective-permute-start(bf16[256,1024]{1,0:T(8,128)(2,1)} %get-tuple-element.27), channel_id=1, source_target_pairs={{0,8},{4,12},{8,0},{12,4},{16,24},{20,28},{24,16},{28,20},{1,9},{5... | collective-permute-start | bytes 1572872 | tf_op jit(solution)/shard_map/ppermute | solution.py:19
  13.3 40.0 %collective-permute-start.8 = (bf16[256,1024]{1,0:T(8,128)(2,1)}, bf16[256,1024]{1,0:T(8,128)(2,1)}, u32[]{:S(2)}, u32[]{:S(2)}) collective-permute-start(bf16[256,1024]{1,0:T(8,128)(2,1)} %get-tuple-element.28), channel_id=1, source_target_pairs={{0,16},{4,20},{8,24},{12,28},{16,0},{20,4},{24,8},{28,12},{1,17},{... | collective-permute-start | bytes 1572872 | tf_op jit(solution)/shard_map/ppermute | solution.py:19
  16.1 24.9 %collective-permute-start.3 = (bf16[256,2048]{1,0:T(8,128)(2,1)}, bf16[256,2048]{1,0:T(8,128)(2,1)}, u32[]{:S(2)}, u32[]{:S(2)}) collective-permute-start(bf16[256,2048]{1,0:T(8,128)(2,1)} %shard_map.68), channel_id=1, source_target_pairs={{0,2},{1,3},{2,0},{3,1},{4,6},{5,7},{6,4},{7,5},{8,10},{9,11},{10,... | collective-permute-start | bytes 3145736 | tf_op jit(solution)/shard_map/ppermute | solution.py:19
  20.3 46.9 %collective-permute-start.7 = (bf16[256,1024]{1,0:T(8,128)(2,1)}, bf16[256,1024]{1,0:T(8,128)(2,1)}, u32[]{:S(2)}, u32[]{:S(2)}) collective-permute-start(bf16[256,1024]{1,0:T(8,128)(2,1)} %collective-permute-done.1.refs_0_.refs_8_), channel_id=1, source_target_pairs={{0,4},{4,0},{8,12},{12,8},{16,20},{20,16},{24,28},{28,24},{1,5},{5... | collective-permute-start | bytes 1572872 | tf_op jit(solution)/shard_map/ppermute | solution.py:19
  32.4 34.7 %collective-permute-start.6 = (bf16[256,1024]{1,0:T(8,128)(2,1)}, bf16[256,1024]{1,0:T(8,128)(2,1)}, u32[]{:S(2)}, u32[]{:S(2)}) collective-permute-start(bf16[256,1024]{1,0:T(8,128)(2,1)} %collective-permute-done.5.refs_7_), channel_id=1, source_target_pairs={{0,4},{4,0},{8,12},{12,8},{16,20},{20,16},{24,28},{28,24},{1,5},{5... | collective-permute-start | bytes 1572872 | tf_op jit(solution)/shard_map/ppermute | solution.py:19
  41.0 26.1 %copy-start.4 = (bf16[1,128,2048]{2,1,0:T(8,128)(2,1)S(1)}, bf16[1,128,2048]{2,1,0:T(8,128)(2,1)}, u32[]{:S(2)}) copy-start(bf16[1,128,2048]{2,1,0:T(8,128)(2,1)} %refs_2_.1) | copy-start | bytes 1572868
  42.9 27.5 %copy-start.1 = (bf16[512,1024]{1,0:T(8,128)(2,1)S(1)}, bf16[512,1024]{1,0:T(8,128)(2,1)}, u32[]{:S(2)}) copy-start(bf16[512,1024]{1,0:T(8,128)(2,1)} %shard_map.65.refs_0_.refs_3_.refs_1_) | copy-start | bytes 3145732
  42.9 27.5 %collective-permute-start.4 = (bf16[128,2048]{1,0:T(8,128)(2,1)S(1)}, bf16[128,2048]{1,0:T(8,128)(2,1)S(1)}, u32[]{:S(2)}, u32[]{:S(2)}) collective-permute-start(bf16[128,2048]{1,0:T(8,128)(2,1)S(1)} %shard_map.69.refs_1_.own_ref), channel_id=1, source_target_pairs={{0,8},{4,12},{8,0},{12,4},{16,24},{20,28},{24,16},{28,20},{1,9},{5... | collective-permute-start | bytes 1572872 | tf_op jit(solution)/shard_map/ppermute | solution.py:19
  44.3 21.2 %collective-permute-start.10 = (bf16[128,1152]{1,0:T(8,128)(2,1)S(1)}, bf16[128,1152]{1,0:T(8,128)(2,1)S(1)}, u32[]{:S(2)}, u32[]{:S(2)}) collective-permute-start(bf16[128,1152]{1,0:T(8,128)(2,1)S(1)} %shard_map.67.refs_1_), channel_id=1, source_target_pairs={{0,16},{4,20},{8,24},{12,28},{16,0},{20,4},{24,8},{28,12},{1,17},{... | collective-permute-start | bytes 884744 | tf_op jit(solution)/shard_map/ppermute | solution.py:19
  53.3 20.1 %collective-permute-start.9 = (bf16[256,1024]{1,0:T(8,128)(2,1)}, bf16[256,1024]{1,0:T(8,128)(2,1)S(1)}, u32[]{:S(2)}, u32[]{:S(2)}) collective-permute-start(bf16[256,1024]{1,0:T(8,128)(2,1)} %collective-permute-done.8.refs_9_.refs_0_), channel_id=1, source_target_pairs={{0,4},{4,0},{8,12},{12,8},{16,20},{20,16},{24,28},{28,24},{1,5},{5... | collective-permute-start | bytes 1572872 | tf_op jit(solution)/shard_map/ppermute | solution.py:19
  65.5 9.4 %collective-permute-start.11 = (bf16[128,1152]{1,0:T(8,128)(2,1)S(1)}, bf16[128,1152]{1,0:T(8,128)(2,1)S(1)}, u32[]{:S(2)}, u32[]{:S(2)}) collective-permute-start(bf16[128,1152]{1,0:T(8,128)(2,1)S(1)} %collective-permute-done.10.refs_3_), channel_id=1, source_target_pairs={{0,4},{4,0},{8,12},{12,8},{16,20},{20,16},{24,28},{28,24},{1,5},{5... | collective-permute-start | bytes 884744 | tf_op jit(solution)/shard_map/ppermute | solution.py:19
  67.1 12.7 %collective-permute-start.16 = (bf16[128,896]{1,0:T(8,128)(2,1)S(1)}, bf16[128,896]{1,0:T(8,128)(2,1)S(1)}, u32[]{:S(2)}, u32[]{:S(2)}) collective-permute-start(bf16[128,896]{1,0:T(8,128)(2,1)S(1)} %shard_map.76), channel_id=1, source_target_pairs={{0,16},{4,20},{8,24},{12,28},{16,0},{20,4},{24,8},{28,12},{1,17},{... | collective-permute-start | bytes 688136 | tf_op jit(solution)/shard_map/ppermute | solution.py:19
  77.0 9.1 %collective-permute-start.12 = (bf16[128,1152]{1,0:T(8,128)(2,1)S(1)}, bf16[128,1152]{1,0:T(8,128)(2,1)S(1)}, u32[]{:S(2)}, u32[]{:S(2)}) collective-permute-start(bf16[128,1152]{1,0:T(8,128)(2,1)S(1)} %get-tuple-element.30.refs_0_), channel_id=1, source_target_pairs={{0,8},{4,12},{8,0},{12,4},{16,24},{20,28},{24,16},{28,20},{1,9},{5... | collective-permute-start | bytes 884744 | tf_op jit(solution)/shard_map/ppermute | solution.py:19
  79.8 7.5 %collective-permute-start.17 = (bf16[128,896]{1,0:T(8,128)(2,1)S(1)}, bf16[128,896]{1,0:T(8,128)(2,1)S(1)}, u32[]{:S(2)}, u32[]{:S(2)}) collective-permute-start(bf16[128,896]{1,0:T(8,128)(2,1)S(1)} %shard_map.77), channel_id=1, source_target_pairs={{0,4},{4,0},{8,12},{12,8},{16,20},{20,16},{24,28},{28,24},{1,5},{5... | collective-permute-start | bytes 688136 | tf_op jit(solution)/shard_map/ppermute | solution.py:19
  89.2 6.7 %collective-permute-start.18 = (bf16[128,896]{1,0:T(8,128)(2,1)S(1)}, bf16[128,896]{1,0:T(8,128)(2,1)S(1)}, u32[]{:S(2)}, u32[]{:S(2)}) collective-permute-start(bf16[128,896]{1,0:T(8,128)(2,1)S(1)} %get-tuple-element.38), channel_id=1, source_target_pairs={{0,8},{4,12},{8,0},{12,4},{16,24},{20,28},{24,16},{28,20},{1,9},{5... | collective-permute-start | bytes 688136 | tf_op jit(solution)/shard_map/ppermute | solution.py:19
  89.3 8.6 %collective-permute-start.13 = (bf16[64,1280]{1,0:T(8,128)(2,1)S(1)}, bf16[64,1280]{1,0:T(8,128)(2,1)S(1)}, u32[]{:S(2)}, u32[]{:S(2)}) collective-permute-start(bf16[64,1280]{1,0:T(8,128)(2,1)S(1)} %get-tuple-element.32), channel_id=1, source_target_pairs={{0,1},{1,0},{2,3},{3,2},{4,5},{5,4},{6,7},{7,6},{8,9},{9,8},{10,11... | collective-permute-start | bytes 491528 | tf_op jit(solution)/shard_map/ppermute | solution.py:19
  89.4 8.8 %collective-permute-start.14 = (bf16[64,1280]{1,0:T(8,128)(2,1)S(1)}, bf16[64,1280]{1,0:T(8,128)(2,1)S(1)}, u32[]{:S(2)}, u32[]{:S(2)}) collective-permute-start(bf16[64,1280]{1,0:T(8,128)(2,1)S(1)} %get-tuple-element.33), channel_id=1, source_target_pairs={{0,2},{1,3},{2,0},{3,1},{4,6},{5,7},{6,4},{7,5},{8,10},{9,11},{10,... | collective-permute-start | bytes 491528 | tf_op jit(solution)/shard_map/ppermute | solution.py:19
  90.9 8.1 %collective-permute-start.15 = (bf16[64,1280]{1,0:T(8,128)(2,1)S(1)}, bf16[64,1280]{1,0:T(8,128)(2,1)S(1)}, u32[]{:S(2)}, u32[]{:S(2)}) collective-permute-start(bf16[64,1280]{1,0:T(8,128)(2,1)S(1)} %get-tuple-element.34), channel_id=1, source_target_pairs={{0,3},{1,2},{2,1},{3,0},{4,7},{5,6},{6,5},{7,4},{8,11},{9,10},{10,... | collective-permute-start | bytes 491528 | tf_op jit(solution)/shard_map/ppermute | solution.py:19
  96.3 3.4 %collective-permute-start.19 = (bf16[64,896]{1,0:T(8,128)(2,1)S(1)}, bf16[64,896]{1,0:T(8,128)(2,1)S(1)}, u32[]{:S(2)}, u32[]{:S(2)}) collective-permute-start(bf16[64,896]{1,0:T(8,128)(2,1)S(1)} %get-tuple-element.40), channel_id=1, source_target_pairs={{0,1},{1,0},{2,3},{3,2},{4,5},{5,4},{6,7},{7,6},{8,9},{9,8},{10,11... | collective-permute-start | bytes 344072 | tf_op jit(solution)/shard_map/ppermute | solution.py:19
  96.3 6.0 %collective-permute-start.20 = (bf16[64,896]{1,0:T(8,128)(2,1)S(1)}, bf16[64,896]{1,0:T(8,128)(2,1)S(1)}, u32[]{:S(2)}, u32[]{:S(2)}) collective-permute-start(bf16[64,896]{1,0:T(8,128)(2,1)S(1)} %get-tuple-element.41), channel_id=1, source_target_pairs={{0,2},{1,3},{2,0},{3,1},{4,6},{5,7},{6,4},{7,5},{8,10},{9,11},{10,... | collective-permute-start | bytes 344072 | tf_op jit(solution)/shard_map/ppermute | solution.py:19
  97.9 6.1 %collective-permute-start.21 = (bf16[64,896]{1,0:T(8,128)(2,1)S(1)}, bf16[64,896]{1,0:T(8,128)(2,1)S(1)}, u32[]{:S(2)}, u32[]{:S(2)}) collective-permute-start(bf16[64,896]{1,0:T(8,128)(2,1)S(1)} %get-tuple-element.42), channel_id=1, source_target_pairs={{0,3},{1,2},{2,1},{3,0},{4,7},{5,6},{6,5},{7,4},{8,11},{9,10},{10,... | collective-permute-start | bytes 344072 | tf_op jit(solution)/shard_map/ppermute | solution.py:19
  (6 other events, 19.2 us)

commit v5 on v4

--- a/solution.py
+++ b/solution.py
@@ -173,16 +173,38 @@
             out_ref[:, at : at + block] = (gate / (1.0 + jnp.exp(-gate)) * up).astype(BF16)
 
 
-def down_units(hidden_ref, *refs, places):
-    arrays, (out_ref, away_ref) = refs[:-2], refs[-2:]
+def down_units(*refs, waits, counts, places):
+    hidden_ref, refs = refs[waits], refs[waits + 1 :]
+    far, near, (out_ref, away_ref, rows_ref, sem) = refs[: counts[0]], refs[counts[0] : -4], refs[-4:]
     capacity = out_ref.shape[0]
+    copies, later = [], []
+    for index, pieces in enumerate(places):
+        at = 0
+        for array, row, rows, column, columns in pieces:
+            if array < counts[0]:
+                copies.append(
+                    pltpu.make_async_copy(
+                        far[array].at[row : row + rows, column : column + columns],
+                        rows_ref.at[array, :, at : at + columns],
+                        sem.at[len(copies)],
+                    )
+                )
+            at += columns
+    for copy in copies:
+        copy.start()
     total, unit = 0.0, 0
     for pieces in places:
-        values = [arrays[a][r : r + n, c : c + w] for a, r, n, c, w in pieces]
-        block = values[0] if len(values) == 1 else jnp.concatenate(values, axis=1)
-        rows = block.shape[0]
-        total = total + dot(hidden_ref[:, unit : unit + rows], block)
+        array, row, rows, column, columns = pieces[0]
+        if array < counts[0]:
+            later.append((unit, rows, array))
+        else:
+            block = near[array - counts[0]][row : row + rows, column : column + columns]
+            total = total + dot(hidden_ref[:, unit : unit + rows], block)
         unit += rows
+    for copy in copies:
+        copy.wait()
+    for unit, rows, array in later:
+        total = total + dot(hidden_ref[:, unit : unit + rows], rows_ref[array])
     out_ref[...] = total[:capacity]
     away_ref[...] = total[capacity:].astype(BF16)
 
@@ -410,14 +432,26 @@
         places += [[(2 + i, 0, x.shape[0], 0, step)] for i, x in enumerate(far_rows)]
         places += [pieces(1, rows_shard, start, start + step)]
         places += [[(2 + count + i, 0, x.shape[0], 0, step)] for i, x in enumerate(far_rows)]
-        out, away = call(
-            functools.partial(down_units, places=places),
-            [shape(capacity, step, dtype=F32), shape(capacity, step)],
-            hidden,
-            *parts,
-            wait=[away, sent[0]] if index else [],
-            flops=LONG if index else 2 * capacity * units * step,
-        )
+        waits = [away, sent[0]] if index else []
+        out, away = pl.pallas_call(
+            functools.partial(down_units, waits=len(waits), counts=(2, len(parts) - 2), places=places),
+            out_shape=[shape(capacity, step, dtype=F32), shape(capacity, step)],
+            in_specs=[pl.BlockSpec(memory_space=pl.ANY)] * len(waits)
+            + [pl.BlockSpec(memory_space=pltpu.VMEM)]
+            + [pl.BlockSpec(memory_space=pl.ANY)] * 2
+            + [pl.BlockSpec(memory_space=pltpu.VMEM)] * (len(parts) - 2),
+            out_specs=[pl.BlockSpec(memory_space=pltpu.VMEM)] * 2,
+            scratch_shapes=[
+                pltpu.VMEM((2, down_rows, step), BF16),
+                pltpu.SemaphoreType.DMA((2 * (width // units),)),
+            ],
+            compiler_params=pltpu.CompilerParams(vmem_limit_bytes=limit),
+            cost_estimate=pl.CostEstimate(
+                flops=LONG if index else 2 * capacity * units * step,
+                bytes_accessed=2**22,
+                transcendentals=0,
+            ),
+        )(*waits, hidden, *parts)
         extra = 128 if index == 0 else 0
         sent = call(
             weigh,

time: 106 us -> 105 us (level)
    pallas_call x14 -> x12, Pallas kernels: 13.8 us -> 9.95 us  [call(): pl.pallas_call(body, out_shape=out_shape, in_specs=in_specs, out_specs=ja...]
    pallas_call x0 -> x2, Pallas kernels: none -> 3.05 us  [per_device(): pl.pallas_call(functools.partial(down_units, waits=len(waits), counts=(2,...]
where the time goes in v5:
time: 105 us
  waiting for transfers between devices  60.3 us (57%)
  starting transfers between devices  23.9 us (23%)
  Pallas kernels  18.3 us (17%)
  local copies, waits for them, and re-layouts  2.23 us (2%)
    ppermute x22, waiting for transfers between devices, swap(): return lax.ppermute(value, axis, pairs)  60.3 us
    ppermute x22, starting transfers between devices, swap(): return lax.ppermute(value, axis, pairs)  23.9 us
    pallas_call x12, Pallas kernels, call(): pl.pallas_call(body, out_shape=out_shape, in_specs=in_specs, out_specs=ja...  9.95 us
    pallas_call x2, Pallas kernels, collect(): pl.pallas_call(functools.partial(opening, flip=flip, pairs=pairs), out_sh...  4.24 us
    pallas_call x2, Pallas kernels, per_device(): pl.pallas_call(functools.partial(down_units, waits=len(waits), counts=(2,...  3.05 us
    unnamed x16, local copies, waits for them, and re-layouts  2.12 us
  transfers between devices with their start and end apart: 22, of which 15 were waited for; matrix products, arithmetic and copies ran while one was open for 0% of the time, Pallas kernels for 15%

profile of v5, /device:TPU:0, one launch (start us, length us, event | category | flops | bytes accessed | tf_op | source)
XLA Modules:
  0.0 104.9 jit_solution(5373912800996871041)
XLA Ops:
  0.5 1.9 %shard_map.66.refs_0_.refs_1_ = bf16[256,1024]{1,0:T(8,128)(2,1)} custom-call(s32[1]{0:T(128)} %bitcast.3.bit_ref, bf16[1,256,1024]{2,1,0:T(8,128)(2,1)} %gate_ref.3, bf16[1,256,1024]{2,1,0:T(8,128)(2,1)} %up_ref.3), custom_call_target="tpu_custom_call" | custom-call | bytes 1048576 | tf_op jit(solution)/shard_map/pallas_call | solution.py:278
  2.4 4.7 %collective-permute-start.1 = (bf16[256,1024]{1,0:T(8,128)(2,1)}, bf16[256,1024]{1,0:T(8,128)(2,1)}, u32[]{:S(2)}, u32[]{:S(2)}) collective-permute-start(bf16[256,1024]{1,0:T(8,128)(2,1)} %shard_map.66.refs_0_.refs_1_), channel_id=1, source_target_pairs={{0,24},{4,28},{8,16},{12,20},{16,8},{20,12},{24,0},{28,4},{1,25},{... | collective-permute-start | bytes 1572872 | tf_op jit(solution)/shard_map/ppermute | solution.py:19
  7.1 2.3 %shard_map.65.refs_0_.refs_3_.refs_1_ = bf16[512,1024]{1,0:T(8,128)(2,1)} custom-call(s32[1]{0:T(128)} %bitcast.3.bit_ref, bf16[1,256,1024]{2,1,0:T(8,128)(2,1)} %gate_ref.3, bf16[1,256,1024]{2,1,0:T(8,128)(2,1)} %up_ref.3, bf16[1,128,2048]{2,1,0:T(8,128)(2,1)} %refs_2_.1), custom_call_target="tpu_custom_call" | custom-call | bytes 1048576 | tf_op jit(solution)/shard_map/pallas_call | solution.py:278
  9.4 1.6 %collective-permute-start = (bf16[512,1024]{1,0:T(8,128)(2,1)}, bf16[512,1024]{1,0:T(8,128)(2,1)}, u32[]{:S(2)}, u32[]{:S(2)}) collective-permute-start(bf16[512,1024]{1,0:T(8,128)(2,1)} %shard_map.65.refs_0_.refs_3_.refs_1_), channel_id=1, source_target_pairs={{0,4},{4,0},{8,12},{12,8},{16,20},{20,16},{24,28},{28,24},{1,5},{5... | collective-permute-start | bytes 3145736 | tf_op jit(solution)/shard_map/ppermute | solution.py:19
  17.6 2.7 %collective-permute-done.1.refs_0_.refs_8_ = bf16[256,1024]{1,0:T(8,128)(2,1)} collective-permute-done((bf16[256,1024]{1,0:T(8,128)(2,1)}, bf16[256,1024]{1,0:T(8,128)(2,1)}, u32[]{:S(2)}, u32[]{:S(2)}) %collective-permute-start.1) | collective-permute-done | bytes 524320 | tf_op jit(solution)/shard_map/ppermute | solution.py:19
  20.3 1.7 %collective-permute-start.7 = (bf16[256,1024]{1,0:T(8,128)(2,1)}, bf16[256,1024]{1,0:T(8,128)(2,1)}, u32[]{:S(2)}, u32[]{:S(2)}) collective-permute-start(bf16[256,1024]{1,0:T(8,128)(2,1)} %collective-permute-done.1.refs_0_.refs_8_), channel_id=1, source_target_pairs={{0,4},{4,0},{8,12},{12,8},{16,20},{20,16},{24,28},{28,24},{1,5},{5... | collective-permute-start | bytes 1572872 | tf_op jit(solution)/shard_map/ppermute | solution.py:19
  22.0 10.4 %collective-permute-done.5.refs_7_ = bf16[256,1024]{1,0:T(8,128)(2,1)} collective-permute-done((bf16[256,1024]{1,0:T(8,128)(2,1)}, bf16[256,1024]{1,0:T(8,128)(2,1)}, u32[]{:S(2)}, u32[]{:S(2)}) %collective-permute-start.5) | collective-permute-done | bytes 524320 | tf_op jit(solution)/shard_map/ppermute | solution.py:19
  32.4 1.5 %collective-permute-start.6 = (bf16[256,1024]{1,0:T(8,128)(2,1)}, bf16[256,1024]{1,0:T(8,128)(2,1)}, u32[]{:S(2)}, u32[]{:S(2)}) collective-permute-start(bf16[256,1024]{1,0:T(8,128)(2,1)} %collective-permute-done.5.refs_7_), channel_id=1, source_target_pairs={{0,4},{4,0},{8,12},{12,8},{16,20},{20,16},{24,28},{28,24},{1,5},{5... | collective-permute-start | bytes 1572872 | tf_op jit(solution)/shard_map/ppermute | solution.py:19
  33.9 1.9 %collective-permute-done.refs_0_.refs_4_.refs_2_ = bf16[512,1024]{1,0:T(8,128)(2,1)} collective-permute-done((bf16[512,1024]{1,0:T(8,128)(2,1)}, bf16[512,1024]{1,0:T(8,128)(2,1)}, u32[]{:S(2)}, u32[]{:S(2)}) %collective-permute-start) | collective-permute-done | bytes 1048608 | tf_op jit(solution)/shard_map/ppermute | solution.py:19
  35.8 5.2 %collective-permute-done.3.refs_5_ = bf16[256,2048]{1,0:T(8,128)(2,1)} collective-permute-done((bf16[256,2048]{1,0:T(8,128)(2,1)}, bf16[256,2048]{1,0:T(8,128)(2,1)}, u32[]{:S(2)}, u32[]{:S(2)}) %collective-permute-start.3) | collective-permute-done | bytes 1048608 | tf_op jit(solution)/shard_map/ppermute | solution.py:19
  41.0 1.9 %shard_map.69.refs_1_.own_ref = bf16[128,2048]{1,0:T(8,128)(2,1)S(1)} custom-call(bf16[512,1024]{1,0:T(8,128)(2,1)} %collective-permute-done.refs_0_.refs_4_.refs_2_, bf16[128,1152]{1,0:T(8,128)(2,1)S(1)} %shard_map.67.refs_1_, bf16[512,128]{1,0:T(8,128)(2,1)S(1)} %get-tuple-element.26.refs_2_, bf16[128,2048]{1,0:T(8,128)(2,1)S(1)} %copy-done.5, ...), custom_call_target="tpu_custom_call" | custom-call | flops 999999995904 | bytes 4096000 | tf_op jit(solution)/shard_map/pallas_call | solution.py:33
  44.3 2.6 %collective-permute-start.10 = (bf16[128,1152]{1,0:T(8,128)(2,1)S(1)}, bf16[128,1152]{1,0:T(8,128)(2,1)S(1)}, u32[]{:S(2)}, u32[]{:S(2)}) collective-permute-start(bf16[128,1152]{1,0:T(8,128)(2,1)S(1)} %shard_map.67.refs_1_), channel_id=1, source_target_pairs={{0,16},{4,20},{8,24},{12,28},{16,0},{20,4},{24,8},{28,12},{1,17},{... | collective-permute-start | bytes 884744 | tf_op jit(solution)/shard_map/ppermute | solution.py:19
  47.0 6.4 %collective-permute-done.8.refs_9_.refs_0_ = bf16[256,1024]{1,0:T(8,128)(2,1)} collective-permute-done((bf16[256,1024]{1,0:T(8,128)(2,1)}, bf16[256,1024]{1,0:T(8,128)(2,1)}, u32[]{:S(2)}, u32[]{:S(2)}) %collective-permute-start.8) | collective-permute-done | bytes 524320 | tf_op jit(solution)/shard_map/ppermute | solution.py:19
  54.9 10.7 %collective-permute-done.10.refs_3_ = bf16[128,1152]{1,0:T(8,128)(2,1)S(1)} collective-permute-done((bf16[128,1152]{1,0:T(8,128)(2,1)S(1)}, bf16[128,1152]{1,0:T(8,128)(2,1)S(1)}, u32[]{:S(2)}, u32[]{:S(2)}) %collective-permute-start.10) | collective-permute-done | bytes 294944 | tf_op jit(solution)/shard_map/ppermute | solution.py:19
  67.2 3.1 %collective-permute-done.4.refs_2_.far_ref = bf16[128,2048]{1,0:T(8,128)(2,1)S(1)} collective-permute-done((bf16[128,2048]{1,0:T(8,128)(2,1)S(1)}, bf16[128,2048]{1,0:T(8,128)(2,1)S(1)}, u32[]{:S(2)}, u32[]{:S(2)}) %collective-permute-start.4) | collective-permute-done | bytes 524320 | tf_op jit(solution)/shard_map/ppermute | solution.py:19
  70.3 3.1 %shard_map.71.start_ref = f32[256,1024]{1,0:T(8,128)S(1)} custom-call(s32[8]{0:T(128)S(1)} %iota_xor_fusion.refs_0_.where_ref, bf16[128,2048]{1,0:T(8,128)(2,1)S(1)} %shard_map.69.refs_1_.own_ref, bf16[128,2048]{1,0:T(8,128)(2,1)S(1)} %collective-permute-done.4.refs_2_.far_ref, bf16[512,1024]{1,0:T(8,128)(2,1)S(1)} %copy-done.1, ...), custom_call_target="tpu_custom_call" | custom-call | flops 805306368 | bytes 6815776 | tf_op jit(solution)/shard_map/pallas_call | solution.py:33
  75.0 1.6 %shard_map.73 = (f32[128,1152]{1,0:T(8,128)S(1)}, bf16[128,1152]{1,0:T(8,128)(2,1)S(1)}) custom-call(bf16[256,512]{1,0:T(8,128)(2,1)S(1)} %shard_map.72.refs_0_.refs_2_, bf16[512,1024]{1,0:T(8,128)(2,1)S(1)} %copy-done.1, bf16[512,1024]{1,0:T(8,128)(2,1)} %collective-permute-done.refs_0_.refs_4_.refs_2_, ...), custom_call_target="tpu_custom_call" | custom-call | flops 301989888 | bytes 4194304 | tf_op jit(solution)/shard_map/pallas_call | solution.py:436
  76.6 3.2 %collective-permute-done.16.refs_1_.refs_5_ = bf16[128,896]{1,0:T(8,128)(2,1)S(1)} collective-permute-done((bf16[128,896]{1,0:T(8,128)(2,1)S(1)}, bf16[128,896]{1,0:T(8,128)(2,1)S(1)}, u32[]{:S(2)}, u32[]{:S(2)}) %collective-permute-start.16) | collective-permute-done | bytes 229408 | tf_op jit(solution)/shard_map/ppermute | solution.py:19
  80.6 5.4 %collective-permute-done.12.refs_4_ = bf16[128,1152]{1,0:T(8,128)(2,1)S(1)} collective-permute-done((bf16[128,1152]{1,0:T(8,128)(2,1)S(1)}, bf16[128,1152]{1,0:T(8,128)(2,1)S(1)}, u32[]{:S(2)}, u32[]{:S(2)}) %collective-permute-start.12) | collective-permute-done | bytes 294944 | tf_op jit(solution)/shard_map/ppermute | solution.py:19
  89.0 1.6 %collective-permute-start.14 = (bf16[64,1280]{1,0:T(8,128)(2,1)S(1)}, bf16[64,1280]{1,0:T(8,128)(2,1)S(1)}, u32[]{:S(2)}, u32[]{:S(2)}) collective-permute-start(bf16[64,1280]{1,0:T(8,128)(2,1)S(1)} %get-tuple-element.33), channel_id=1, source_target_pairs={{0,2},{1,3},{2,0},{3,1},{4,6},{5,7},{6,4},{7,5},{8,10},{9,11},{10,... | collective-permute-start | bytes 491528 | tf_op jit(solution)/shard_map/ppermute | solution.py:19
  90.9 4.6 %collective-permute-done.18.refs_4_ = bf16[128,896]{1,0:T(8,128)(2,1)S(1)} collective-permute-done((bf16[128,896]{1,0:T(8,128)(2,1)S(1)}, bf16[128,896]{1,0:T(8,128)(2,1)S(1)}, u32[]{:S(2)}, u32[]{:S(2)}) %collective-permute-start.18) | collective-permute-done | bytes 229408 | tf_op jit(solution)/shard_map/ppermute | solution.py:19
  95.9 1.6 %collective-permute-start.20 = (bf16[64,896]{1,0:T(8,128)(2,1)S(1)}, bf16[64,896]{1,0:T(8,128)(2,1)S(1)}, u32[]{:S(2)}, u32[]{:S(2)}) collective-permute-start(bf16[64,896]{1,0:T(8,128)(2,1)S(1)} %get-tuple-element.41), channel_id=1, source_target_pairs={{0,2},{1,3},{2,0},{3,1},{4,6},{5,7},{6,4},{7,5},{8,10},{9,11},{10,... | collective-permute-start | bytes 344072 | tf_op jit(solution)/shard_map/ppermute | solution.py:19
  99.3 2.7 %collective-permute-done.20.refs_4_ = bf16[64,896]{1,0:T(8,128)(2,1)S(1)} collective-permute-done((bf16[64,896]{1,0:T(8,128)(2,1)S(1)}, bf16[64,896]{1,0:T(8,128)(2,1)S(1)}, u32[]{:S(2)}, u32[]{:S(2)}) %collective-permute-start.20) | collective-permute-done | bytes 114720 | tf_op jit(solution)/shard_map/ppermute | solution.py:19
  101.9 1.8 %collective-permute-done.21.refs_5_ = bf16[64,896]{1,0:T(8,128)(2,1)S(1)} collective-permute-done((bf16[64,896]{1,0:T(8,128)(2,1)S(1)}, bf16[64,896]{1,0:T(8,128)(2,1)S(1)}, u32[]{:S(2)}, u32[]{:S(2)}) %collective-permute-start.21) | collective-permute-done | bytes 114720 | tf_op jit(solution)/shard_map/ppermute | solution.py:19
  (55 shorter events, 20.7 us)
Async XLA Ops:
  0.0 15.0 %collective-permute-start.2 = (bf16[128,2048]{1,0:T(8,128)(2,1)}, bf16[128,2048]{1,0:T(8,128)(2,1)S(1)}, u32[]{:S(2)}, u32[]{:S(2)}) collective-permute-start(bf16[128,2048]{1,0:T(8,128)(2,1)} %refs_3_.1), channel_id=1, source_target_pairs={{0,1},{1,0},{2,3},{3,2},{4,5},{5,4},{6,7},{7,6},{8,9},{9,8},{10,11... | collective-permute-start | bytes 1572872 | tf_op jit(solution)/shard_map/ppermute | solution.py:19
  2.4 17.9 %collective-permute-start.1 = (bf16[256,1024]{1,0:T(8,128)(2,1)}, bf16[256,1024]{1,0:T(8,128)(2,1)}, u32[]{:S(2)}, u32[]{:S(2)}) collective-permute-start(bf16[256,1024]{1,0:T(8,128)(2,1)} %shard_map.66.refs_0_.refs_1_), channel_id=1, source_target_pairs={{0,24},{4,28},{8,16},{12,20},{16,8},{20,12},{24,0},{28,4},{1,25},{... | collective-permute-start | bytes 1572872 | tf_op jit(solution)/shard_map/ppermute | solution.py:19
  9.4 26.4 %collective-permute-start = (bf16[512,1024]{1,0:T(8,128)(2,1)}, bf16[512,1024]{1,0:T(8,128)(2,1)}, u32[]{:S(2)}, u32[]{:S(2)}) collective-permute-start(bf16[512,1024]{1,0:T(8,128)(2,1)} %shard_map.65.refs_0_.refs_3_.refs_1_), channel_id=1, source_target_pairs={{0,4},{4,0},{8,12},{12,8},{16,20},{20,16},{24,28},{28,24},{1,5},{5... | collective-permute-start | bytes 3145736 | tf_op jit(solution)/shard_map/ppermute | solution.py:19
  13.3 19.1 %collective-permute-start.5 = (bf16[256,1024]{1,0:T(8,128)(2,1)}, bf16[256,1024]{1,0:T(8,128)(2,1)}, u32[]{:S(2)}, u32[]{:S(2)}) collective-permute-start(bf16[256,1024]{1,0:T(8,128)(2,1)} %get-tuple-element.27), channel_id=1, source_target_pairs={{0,8},{4,12},{8,0},{12,4},{16,24},{20,28},{24,16},{28,20},{1,9},{5... | collective-permute-start | bytes 1572872 | tf_op jit(solution)/shard_map/ppermute | solution.py:19
  13.3 40.0 %collective-permute-start.8 = (bf16[256,1024]{1,0:T(8,128)(2,1)}, bf16[256,1024]{1,0:T(8,128)(2,1)}, u32[]{:S(2)}, u32[]{:S(2)}) collective-permute-start(bf16[256,1024]{1,0:T(8,128)(2,1)} %get-tuple-element.28), channel_id=1, source_target_pairs={{0,16},{4,20},{8,24},{12,28},{16,0},{20,4},{24,8},{28,12},{1,17},{... | collective-permute-start | bytes 1572872 | tf_op jit(solution)/shard_map/ppermute | solution.py:19
  16.1 24.9 %collective-permute-start.3 = (bf16[256,2048]{1,0:T(8,128)(2,1)}, bf16[256,2048]{1,0:T(8,128)(2,1)}, u32[]{:S(2)}, u32[]{:S(2)}) collective-permute-start(bf16[256,2048]{1,0:T(8,128)(2,1)} %shard_map.68), channel_id=1, source_target_pairs={{0,2},{1,3},{2,0},{3,1},{4,6},{5,7},{6,4},{7,5},{8,10},{9,11},{10,... | collective-permute-start | bytes 3145736 | tf_op jit(solution)/shard_map/ppermute | solution.py:19
  20.3 46.9 %collective-permute-start.7 = (bf16[256,1024]{1,0:T(8,128)(2,1)}, bf16[256,1024]{1,0:T(8,128)(2,1)}, u32[]{:S(2)}, u32[]{:S(2)}) collective-permute-start(bf16[256,1024]{1,0:T(8,128)(2,1)} %collective-permute-done.1.refs_0_.refs_8_), channel_id=1, source_target_pairs={{0,4},{4,0},{8,12},{12,8},{16,20},{20,16},{24,28},{28,24},{1,5},{5... | collective-permute-start | bytes 1572872 | tf_op jit(solution)/shard_map/ppermute | solution.py:19
  32.4 34.7 %collective-permute-start.6 = (bf16[256,1024]{1,0:T(8,128)(2,1)}, bf16[256,1024]{1,0:T(8,128)(2,1)}, u32[]{:S(2)}, u32[]{:S(2)}) collective-permute-start(bf16[256,1024]{1,0:T(8,128)(2,1)} %collective-permute-done.5.refs_7_), channel_id=1, source_target_pairs={{0,4},{4,0},{8,12},{12,8},{16,20},{20,16},{24,28},{28,24},{1,5},{5... | collective-permute-start | bytes 1572872 | tf_op jit(solution)/shard_map/ppermute | solution.py:19
  41.0 26.1 %copy-start.4 = (bf16[1,128,2048]{2,1,0:T(8,128)(2,1)S(1)}, bf16[1,128,2048]{2,1,0:T(8,128)(2,1)}, u32[]{:S(2)}) copy-start(bf16[1,128,2048]{2,1,0:T(8,128)(2,1)} %refs_2_.1) | copy-start | bytes 1572868
  42.9 27.5 %copy-start.1 = (bf16[512,1024]{1,0:T(8,128)(2,1)S(1)}, bf16[512,1024]{1,0:T(8,128)(2,1)}, u32[]{:S(2)}) copy-start(bf16[512,1024]{1,0:T(8,128)(2,1)} %shard_map.65.refs_0_.refs_3_.refs_1_) | copy-start | bytes 3145732
  42.9 27.5 %collective-permute-start.4 = (bf16[128,2048]{1,0:T(8,128)(2,1)S(1)}, bf16[128,2048]{1,0:T(8,128)(2,1)S(1)}, u32[]{:S(2)}, u32[]{:S(2)}) collective-permute-start(bf16[128,2048]{1,0:T(8,128)(2,1)S(1)} %shard_map.69.refs_1_.own_ref), channel_id=1, source_target_pairs={{0,8},{4,12},{8,0},{12,4},{16,24},{20,28},{24,16},{28,20},{1,9},{5... | collective-permute-start | bytes 1572872 | tf_op jit(solution)/shard_map/ppermute | solution.py:19
  44.3 21.2 %collective-permute-start.10 = (bf16[128,1152]{1,0:T(8,128)(2,1)S(1)}, bf16[128,1152]{1,0:T(8,128)(2,1)S(1)}, u32[]{:S(2)}, u32[]{:S(2)}) collective-permute-start(bf16[128,1152]{1,0:T(8,128)(2,1)S(1)} %shard_map.67.refs_1_), channel_id=1, source_target_pairs={{0,16},{4,20},{8,24},{12,28},{16,0},{20,4},{24,8},{28,12},{1,17},{... | collective-permute-start | bytes 884744 | tf_op jit(solution)/shard_map/ppermute | solution.py:19
  53.3 20.1 %collective-permute-start.9 = (bf16[256,1024]{1,0:T(8,128)(2,1)}, bf16[256,1024]{1,0:T(8,128)(2,1)S(1)}, u32[]{:S(2)}, u32[]{:S(2)}) collective-permute-start(bf16[256,1024]{1,0:T(8,128)(2,1)} %collective-permute-done.8.refs_9_.refs_0_), channel_id=1, source_target_pairs={{0,4},{4,0},{8,12},{12,8},{16,20},{20,16},{24,28},{28,24},{1,5},{5... | collective-permute-start | bytes 1572872 | tf_op jit(solution)/shard_map/ppermute | solution.py:19
  65.5 9.4 %collective-permute-start.11 = (bf16[128,1152]{1,0:T(8,128)(2,1)S(1)}, bf16[128,1152]{1,0:T(8,128)(2,1)S(1)}, u32[]{:S(2)}, u32[]{:S(2)}) collective-permute-start(bf16[128,1152]{1,0:T(8,128)(2,1)S(1)} %collective-permute-done.10.refs_3_), channel_id=1, source_target_pairs={{0,4},{4,0},{8,12},{12,8},{16,20},{20,16},{24,28},{28,24},{1,5},{5... | collective-permute-start | bytes 884744 | tf_op jit(solution)/shard_map/ppermute | solution.py:19
  67.1 12.8 %collective-permute-start.16 = (bf16[128,896]{1,0:T(8,128)(2,1)S(1)}, bf16[128,896]{1,0:T(8,128)(2,1)S(1)}, u32[]{:S(2)}, u32[]{:S(2)}) collective-permute-start(bf16[128,896]{1,0:T(8,128)(2,1)S(1)} %shard_map.76), channel_id=1, source_target_pairs={{0,16},{4,20},{8,24},{12,28},{16,0},{20,4},{24,8},{28,12},{1,17},{... | collective-permute-start | bytes 688136 | tf_op jit(solution)/shard_map/ppermute | solution.py:19
  76.6 9.5 %collective-permute-start.12 = (bf16[128,1152]{1,0:T(8,128)(2,1)S(1)}, bf16[128,1152]{1,0:T(8,128)(2,1)S(1)}, u32[]{:S(2)}, u32[]{:S(2)}) collective-permute-start(bf16[128,1152]{1,0:T(8,128)(2,1)S(1)} %get-tuple-element.30.refs_0_), channel_id=1, source_target_pairs={{0,8},{4,12},{8,0},{12,4},{16,24},{20,28},{24,16},{28,20},{1,9},{5... | collective-permute-start | bytes 884744 | tf_op jit(solution)/shard_map/ppermute | solution.py:19
  79.9 7.5 %collective-permute-start.17 = (bf16[128,896]{1,0:T(8,128)(2,1)S(1)}, bf16[128,896]{1,0:T(8,128)(2,1)S(1)}, u32[]{:S(2)}, u32[]{:S(2)}) collective-permute-start(bf16[128,896]{1,0:T(8,128)(2,1)S(1)} %shard_map.77), channel_id=1, source_target_pairs={{0,4},{4,0},{8,12},{12,8},{16,20},{20,16},{24,28},{28,24},{1,5},{5... | collective-permute-start | bytes 688136 | tf_op jit(solution)/shard_map/ppermute | solution.py:19
  88.9 6.6 %collective-permute-start.18 = (bf16[128,896]{1,0:T(8,128)(2,1)S(1)}, bf16[128,896]{1,0:T(8,128)(2,1)S(1)}, u32[]{:S(2)}, u32[]{:S(2)}) collective-permute-start(bf16[128,896]{1,0:T(8,128)(2,1)S(1)} %get-tuple-element.38), channel_id=1, source_target_pairs={{0,8},{4,12},{8,0},{12,4},{16,24},{20,28},{24,16},{28,20},{1,9},{5... | collective-permute-start | bytes 688136 | tf_op jit(solution)/shard_map/ppermute | solution.py:19
  88.9 8.5 %collective-permute-start.13 = (bf16[64,1280]{1,0:T(8,128)(2,1)S(1)}, bf16[64,1280]{1,0:T(8,128)(2,1)S(1)}, u32[]{:S(2)}, u32[]{:S(2)}) collective-permute-start(bf16[64,1280]{1,0:T(8,128)(2,1)S(1)} %get-tuple-element.32), channel_id=1, source_target_pairs={{0,1},{1,0},{2,3},{3,2},{4,5},{5,4},{6,7},{7,6},{8,9},{9,8},{10,11... | collective-permute-start | bytes 491528 | tf_op jit(solution)/shard_map/ppermute | solution.py:19
  89.0 8.8 %collective-permute-start.14 = (bf16[64,1280]{1,0:T(8,128)(2,1)S(1)}, bf16[64,1280]{1,0:T(8,128)(2,1)S(1)}, u32[]{:S(2)}, u32[]{:S(2)}) collective-permute-start(bf16[64,1280]{1,0:T(8,128)(2,1)S(1)} %get-tuple-element.33), channel_id=1, source_target_pairs={{0,2},{1,3},{2,0},{3,1},{4,6},{5,7},{6,4},{7,5},{8,10},{9,11},{10,... | collective-permute-start | bytes 491528 | tf_op jit(solution)/shard_map/ppermute | solution.py:19
  90.6 8.1 %collective-permute-start.15 = (bf16[64,1280]{1,0:T(8,128)(2,1)S(1)}, bf16[64,1280]{1,0:T(8,128)(2,1)S(1)}, u32[]{:S(2)}, u32[]{:S(2)}) collective-permute-start(bf16[64,1280]{1,0:T(8,128)(2,1)S(1)} %get-tuple-element.34), channel_id=1, source_target_pairs={{0,3},{1,2},{2,1},{3,0},{4,7},{5,6},{6,5},{7,4},{8,11},{9,10},{10,... | collective-permute-start | bytes 491528 | tf_op jit(solution)/shard_map/ppermute | solution.py:19
  95.8 3.4 %collective-permute-start.19 = (bf16[64,896]{1,0:T(8,128)(2,1)S(1)}, bf16[64,896]{1,0:T(8,128)(2,1)S(1)}, u32[]{:S(2)}, u32[]{:S(2)}) collective-permute-start(bf16[64,896]{1,0:T(8,128)(2,1)S(1)} %get-tuple-element.40), channel_id=1, source_target_pairs={{0,1},{1,0},{2,3},{3,2},{4,5},{5,4},{6,7},{7,6},{8,9},{9,8},{10,11... | collective-permute-start | bytes 344072 | tf_op jit(solution)/shard_map/ppermute | solution.py:19
  95.9 6.0 %collective-permute-start.20 = (bf16[64,896]{1,0:T(8,128)(2,1)S(1)}, bf16[64,896]{1,0:T(8,128)(2,1)S(1)}, u32[]{:S(2)}, u32[]{:S(2)}) collective-permute-start(bf16[64,896]{1,0:T(8,128)(2,1)S(1)} %get-tuple-element.41), channel_id=1, source_target_pairs={{0,2},{1,3},{2,0},{3,1},{4,6},{5,7},{6,4},{7,5},{8,10},{9,11},{10,... | collective-permute-start | bytes 344072 | tf_op jit(solution)/shard_map/ppermute | solution.py:19
  97.5 6.2 %collective-permute-start.21 = (bf16[64,896]{1,0:T(8,128)(2,1)S(1)}, bf16[64,896]{1,0:T(8,128)(2,1)S(1)}, u32[]{:S(2)}, u32[]{:S(2)}) collective-permute-start(bf16[64,896]{1,0:T(8,128)(2,1)S(1)} %get-tuple-element.42), channel_id=1, source_target_pairs={{0,3},{1,2},{2,1},{3,0},{4,7},{5,6},{6,5},{7,4},{8,11},{9,10},{10,... | collective-permute-start | bytes 344072 | tf_op jit(solution)/shard_map/ppermute | solution.py:19
  (6 other events, 19.2 us)

commit v6 on v5

--- a/solution.py
+++ b/solution.py
@@ -173,10 +173,10 @@
             out_ref[:, at : at + block] = (gate / (1.0 + jnp.exp(-gate)) * up).astype(BF16)
 
 
-def down_units(*refs, waits, counts, places):
+def down_units(*refs, waits, counts, places, side):
     hidden_ref, refs = refs[waits], refs[waits + 1 :]
-    far, near, (out_ref, away_ref, rows_ref, sem) = refs[: counts[0]], refs[counts[0] : -4], refs[-4:]
-    capacity = out_ref.shape[0]
+    far, near, (out_ref, rows_ref, sem) = refs[: counts[0]], refs[counts[0] : -3], refs[-3:]
+    lines = pl.ds(side * out_ref.shape[0], out_ref.shape[0])
     copies, later = [], []
     for index, pieces in enumerate(places):
         at = 0
@@ -199,14 +199,13 @@
             later.append((unit, rows, array))
         else:
             block = near[array - counts[0]][row : row + rows, column : column + columns]
-            total = total + dot(hidden_ref[:, unit : unit + rows], block)
+            total = total + dot(hidden_ref[lines, unit : unit + rows], block)
         unit += rows
     for copy in copies:
         copy.wait()
     for unit, rows, array in later:
-        total = total + dot(hidden_ref[:, unit : unit + rows], rows_ref[array])
-    out_ref[...] = total[:capacity]
-    away_ref[...] = total[capacity:].astype(BF16)
+        total = total + dot(hidden_ref[lines, unit : unit + rows], rows_ref[array])
+    out_ref[...] = total.astype(out_ref.dtype)
 
 
 def weigh(place_ref, tag_ref, weights_ref, out_ref, away_ref, *sent_refs):
@@ -433,25 +432,33 @@
         places += [pieces(1, rows_shard, start, start + step)]
         places += [[(2 + count + i, 0, x.shape[0], 0, step)] for i, x in enumerate(far_rows)]
         waits = [away, sent[0]] if index else []
-        out, away = pl.pallas_call(
-            functools.partial(down_units, waits=len(waits), counts=(2, len(parts) - 2), places=places),
-            out_shape=[shape(capacity, step, dtype=F32), shape(capacity, step)],
-            in_specs=[pl.BlockSpec(memory_space=pl.ANY)] * len(waits)
-            + [pl.BlockSpec(memory_space=pltpu.VMEM)]
-            + [pl.BlockSpec(memory_space=pl.ANY)] * 2
-            + [pl.BlockSpec(memory_space=pltpu.VMEM)] * (len(parts) - 2),
-            out_specs=[pl.BlockSpec(memory_space=pltpu.VMEM)] * 2,
-            scratch_shapes=[
-                pltpu.VMEM((2, down_rows, step), BF16),
-                pltpu.SemaphoreType.DMA((2 * (width // units),)),
-            ],
-            compiler_params=pltpu.CompilerParams(vmem_limit_bytes=limit),
-            cost_estimate=pl.CostEstimate(
-                flops=LONG if index else 2 * capacity * units * step,
-                bytes_accessed=2**22,
-                transcendentals=0,
-            ),
-        )(*waits, hidden, *parts)
+        halves = []
+        for side, dtype in ((1, BF16), (0, F32)):
+            halves.append(
+                pl.pallas_call(
+                    functools.partial(
+                        down_units, waits=len(waits), counts=(2, len(parts) - 2), places=places, side=side
+                    ),
+                    out_shape=shape(capacity, step, dtype=dtype),
+                    in_specs=[pl.BlockSpec(memory_space=pl.ANY)] * len(waits)
+                    + [pl.BlockSpec(memory_space=pltpu.VMEM)]
+                    + [pl.BlockSpec(memory_space=pl.ANY)] * 2
+                    + [pl.BlockSpec(memory_space=pltpu.VMEM)] * (len(parts) - 2),
+                    out_specs=pl.BlockSpec(memory_space=pltpu.VMEM),
+                    scratch_shapes=[
+                        pltpu.VMEM((2, down_rows, step), BF16),
+                        pltpu.SemaphoreType.DMA((2 * (width // units),)),
+                    ],
+                    compiler_params=pltpu.CompilerParams(vmem_limit_bytes=limit),
+                    cost_estimate=pl.CostEstimate(
+                        flops=LONG if index and side else capacity * units * step,
+                        bytes_accessed=2**22,
+                        transcendentals=0,
+                    ),
+                )(*waits, hidden, *parts)
+            )
+            waits = halves[:1]
+        away, out = halves
         extra = 128 if index == 0 else 0
         sent = call(
             weigh,

time: 105 us -> 105 us (level)
  waiting for transfers between devices: 60.3 us -> 57.6 us
  Pallas kernels: 18.3 us -> 20.8 us
    ppermute x22, waiting for transfers between devices: 60.3 us -> 57.6 us  [swap(): return lax.ppermute(value, axis, pairs)]
    pallas_call x2 -> x4, Pallas kernels: 3.05 us -> 5.56 us  [per_device(): pl.pallas_call(functools.partial(down_units, waits=len(waits), counts=(2,...]
  transfers between devices with their start and end apart: 22 -> 22, of which waited for: 15 -> 15; matrix products, arithmetic and copies ran while one was open for 0% -> 0% of each run, Pallas kernels for 15% -> 17%
where the time goes in v6:
time: 105 us
  waiting for transfers between devices  57.6 us (55%)
  starting transfers between devices  23.9 us (23%)
  Pallas kernels  20.8 us (20%)
  local copies, waits for them, and re-layouts  2.23 us (2%)
    ppermute x22, waiting for transfers between devices, swap(): return lax.ppermute(value, axis, pairs)  57.6 us
    ppermute x22, starting transfers between devices, swap(): return lax.ppermute(value, axis, pairs)  23.9 us
    pallas_call x12, Pallas kernels, call(): pl.pallas_call(body, out_shape=out_shape, in_specs=in_specs, out_specs=ja...  9.99 us
    pallas_call x4, Pallas kernels, per_device(): pl.pallas_call(functools.partial(down_units, waits=len(waits), counts=(2,...  5.56 us
    pallas_call x2, Pallas kernels, collect(): pl.pallas_call(functools.partial(opening, flip=flip, pairs=pairs), out_sh...  4.25 us
    unnamed x16, local copies, waits for them, and re-layouts  2.12 us
  transfers between devices with their start and end apart: 22, of which 15 were waited for; matrix products, arithmetic and copies ran while one was open for 0% of the time, Pallas kernels for 17%

profile of v6, /device:TPU:0, one launch (start us, length us, event | category | flops | bytes accessed | tf_op | source)
XLA Modules:
  0.0 104.8 jit_solution(3741657197391801653)
XLA Ops:
  0.5 1.9 %shard_map.66.refs_0_.refs_1_ = bf16[256,1024]{1,0:T(8,128)(2,1)} custom-call(s32[1]{0:T(128)} %bitcast.3.bit_ref, bf16[1,256,1024]{2,1,0:T(8,128)(2,1)} %gate_ref.3, bf16[1,256,1024]{2,1,0:T(8,128)(2,1)} %up_ref.3), custom_call_target="tpu_custom_call" | custom-call | bytes 1048576 | tf_op jit(solution)/shard_map/pallas_call | solution.py:277
  2.4 4.7 %collective-permute-start.1 = (bf16[256,1024]{1,0:T(8,128)(2,1)}, bf16[256,1024]{1,0:T(8,128)(2,1)}, u32[]{:S(2)}, u32[]{:S(2)}) collective-permute-start(bf16[256,1024]{1,0:T(8,128)(2,1)} %shard_map.66.refs_0_.refs_1_), channel_id=1, source_target_pairs={{0,24},{4,28},{8,16},{12,20},{16,8},{20,12},{24,0},{28,4},{1,25},{... | collective-permute-start | bytes 1572872 | tf_op jit(solution)/shard_map/ppermute | solution.py:19
  7.1 2.3 %shard_map.65.refs_0_.refs_3_.refs_1_.refs_2_ = bf16[512,1024]{1,0:T(8,128)(2,1)} custom-call(s32[1]{0:T(128)} %bitcast.3.bit_ref, bf16[1,256,1024]{2,1,0:T(8,128)(2,1)} %gate_ref.3, bf16[1,256,1024]{2,1,0:T(8,128)(2,1)} %up_ref.3, bf16[1,128,2048]{2,1,0:T(8,128)(2,1)} %refs_2_.1), custom_call_target="tpu_custom_call" | custom-call | bytes 1048576 | tf_op jit(solution)/shard_map/pallas_call | solution.py:277
  9.4 1.6 %collective-permute-start = (bf16[512,1024]{1,0:T(8,128)(2,1)}, bf16[512,1024]{1,0:T(8,128)(2,1)}, u32[]{:S(2)}, u32[]{:S(2)}) collective-permute-start(bf16[512,1024]{1,0:T(8,128)(2,1)} %shard_map.65.refs_0_.refs_3_.refs_1_.refs_2_), channel_id=1, source_target_pairs={{0,4},{4,0},{8,12},{12,8},{16,20},{20,16},{24,28},{28,24},{1,5},{5... | collective-permute-start | bytes 3145736 | tf_op jit(solution)/shard_map/ppermute | solution.py:19
  17.6 2.7 %collective-permute-done.1.refs_0_.refs_8_ = bf16[256,1024]{1,0:T(8,128)(2,1)} collective-permute-done((bf16[256,1024]{1,0:T(8,128)(2,1)}, bf16[256,1024]{1,0:T(8,128)(2,1)}, u32[]{:S(2)}, u32[]{:S(2)}) %collective-permute-start.1) | collective-permute-done | bytes 524320 | tf_op jit(solution)/shard_map/ppermute | solution.py:19
  20.3 1.7 %collective-permute-start.7 = (bf16[256,1024]{1,0:T(8,128)(2,1)}, bf16[256,1024]{1,0:T(8,128)(2,1)}, u32[]{:S(2)}, u32[]{:S(2)}) collective-permute-start(bf16[256,1024]{1,0:T(8,128)(2,1)} %collective-permute-done.1.refs_0_.refs_8_), channel_id=1, source_target_pairs={{0,4},{4,0},{8,12},{12,8},{16,20},{20,16},{24,28},{28,24},{1,5},{5... | collective-permute-start | bytes 1572872 | tf_op jit(solution)/shard_map/ppermute | solution.py:19
  22.0 10.4 %collective-permute-done.5.refs_7_ = bf16[256,1024]{1,0:T(8,128)(2,1)} collective-permute-done((bf16[256,1024]{1,0:T(8,128)(2,1)}, bf16[256,1024]{1,0:T(8,128)(2,1)}, u32[]{:S(2)}, u32[]{:S(2)}) %collective-permute-start.5) | collective-permute-done | bytes 524320 | tf_op jit(solution)/shard_map/ppermute | solution.py:19
  32.4 1.5 %collective-permute-start.6 = (bf16[256,1024]{1,0:T(8,128)(2,1)}, bf16[256,1024]{1,0:T(8,128)(2,1)}, u32[]{:S(2)}, u32[]{:S(2)}) collective-permute-start(bf16[256,1024]{1,0:T(8,128)(2,1)} %collective-permute-done.5.refs_7_), channel_id=1, source_target_pairs={{0,4},{4,0},{8,12},{12,8},{16,20},{20,16},{24,28},{28,24},{1,5},{5... | collective-permute-start | bytes 1572872 | tf_op jit(solution)/shard_map/ppermute | solution.py:19
  33.9 1.9 %collective-permute-done.refs_0_.refs_4_.refs_2_.refs_3_ = bf16[512,1024]{1,0:T(8,128)(2,1)} collective-permute-done((bf16[512,1024]{1,0:T(8,128)(2,1)}, bf16[512,1024]{1,0:T(8,128)(2,1)}, u32[]{:S(2)}, u32[]{:S(2)}) %collective-permute-start) | collective-permute-done | bytes 1048608 | tf_op jit(solution)/shard_map/ppermute | solution.py:19
  35.8 5.2 %collective-permute-done.3.refs_5_ = bf16[256,2048]{1,0:T(8,128)(2,1)} collective-permute-done((bf16[256,2048]{1,0:T(8,128)(2,1)}, bf16[256,2048]{1,0:T(8,128)(2,1)}, u32[]{:S(2)}, u32[]{:S(2)}) %collective-permute-start.3) | collective-permute-done | bytes 1048608 | tf_op jit(solution)/shard_map/ppermute | solution.py:19
  41.0 1.9 %shard_map.69.refs_1_.own_ref = bf16[128,2048]{1,0:T(8,128)(2,1)S(1)} custom-call(bf16[512,1024]{1,0:T(8,128)(2,1)} %collective-permute-done.refs_0_.refs_4_.refs_2_.refs_3_, bf16[128,1152]{1,0:T(8,128)(2,1)S(1)} %shard_map.67.refs_1_, bf16[512,128]{1,0:T(8,128)(2,1)S(1)} %get-tuple-element.22.refs_2_, bf16[128,2048]{1,0:T(8,128)(2,1)S(1)} %copy-done.5, ...), custom_call_target="tpu_custom_call" | custom-call | flops 999999995904 | bytes 4096000 | tf_op jit(solution)/shard_map/pallas_call | solution.py:33
  44.4 2.6 %collective-permute-start.10 = (bf16[128,1152]{1,0:T(8,128)(2,1)S(1)}, bf16[128,1152]{1,0:T(8,128)(2,1)S(1)}, u32[]{:S(2)}, u32[]{:S(2)}) collective-permute-start(bf16[128,1152]{1,0:T(8,128)(2,1)S(1)} %shard_map.67.refs_1_), channel_id=1, source_target_pairs={{0,16},{4,20},{8,24},{12,28},{16,0},{20,4},{24,8},{28,12},{1,17},{... | collective-permute-start | bytes 884744 | tf_op jit(solution)/shard_map/ppermute | solution.py:19
  47.0 6.3 %collective-permute-done.8.refs_9_.refs_0_ = bf16[256,1024]{1,0:T(8,128)(2,1)} collective-permute-done((bf16[256,1024]{1,0:T(8,128)(2,1)}, bf16[256,1024]{1,0:T(8,128)(2,1)}, u32[]{:S(2)}, u32[]{:S(2)}) %collective-permute-start.8) | collective-permute-done | bytes 524320 | tf_op jit(solution)/shard_map/ppermute | solution.py:19
  53.3 1.5 %collective-permute-start.9 = (bf16[256,1024]{1,0:T(8,128)(2,1)}, bf16[256,1024]{1,0:T(8,128)(2,1)S(1)}, u32[]{:S(2)}, u32[]{:S(2)}) collective-permute-start(bf16[256,1024]{1,0:T(8,128)(2,1)} %collective-permute-done.8.refs_9_.refs_0_), channel_id=1, source_target_pairs={{0,4},{4,0},{8,12},{12,8},{16,20},{20,16},{24,28},{28,24},{1,5},{5... | collective-permute-start | bytes 1572872 | tf_op jit(solution)/shard_map/ppermute | solution.py:19
  54.9 10.7 %collective-permute-done.10.refs_3_.refs_4_ = bf16[128,1152]{1,0:T(8,128)(2,1)S(1)} collective-permute-done((bf16[128,1152]{1,0:T(8,128)(2,1)S(1)}, bf16[128,1152]{1,0:T(8,128)(2,1)S(1)}, u32[]{:S(2)}, u32[]{:S(2)}) %collective-permute-start.10) | collective-permute-done | bytes 294944 | tf_op jit(solution)/shard_map/ppermute | solution.py:19
  67.2 3.1 %collective-permute-done.4.refs_2_.far_ref = bf16[128,2048]{1,0:T(8,128)(2,1)S(1)} collective-permute-done((bf16[128,2048]{1,0:T(8,128)(2,1)S(1)}, bf16[128,2048]{1,0:T(8,128)(2,1)S(1)}, u32[]{:S(2)}, u32[]{:S(2)}) %collective-permute-start.4) | collective-permute-done | bytes 524320 | tf_op jit(solution)/shard_map/ppermute | solution.py:19
  70.3 3.1 %shard_map.71.start_ref = f32[256,1024]{1,0:T(8,128)S(1)} custom-call(s32[8]{0:T(128)S(1)} %iota_xor_fusion.refs_0_.where_ref, bf16[128,2048]{1,0:T(8,128)(2,1)S(1)} %shard_map.69.refs_1_.own_ref, bf16[128,2048]{1,0:T(8,128)(2,1)S(1)} %collective-permute-done.4.refs_2_.far_ref, bf16[512,1024]{1,0:T(8,128)(2,1)S(1)} %copy-done.1, ...), custom_call_target="tpu_custom_call" | custom-call | flops 805306368 | bytes 6815776 | tf_op jit(solution)/shard_map/pallas_call | solution.py:33
  76.5 3.3 %collective-permute-done.16.refs_1_.refs_5_.refs_4_ = bf16[128,896]{1,0:T(8,128)(2,1)S(1)} collective-permute-done((bf16[128,896]{1,0:T(8,128)(2,1)S(1)}, bf16[128,896]{1,0:T(8,128)(2,1)S(1)}, u32[]{:S(2)}, u32[]{:S(2)}) %collective-permute-start.16) | collective-permute-done | bytes 229408 | tf_op jit(solution)/shard_map/ppermute | solution.py:19
  82.1 4.0 %collective-permute-done.12.refs_4_ = bf16[128,1152]{1,0:T(8,128)(2,1)S(1)} collective-permute-done((bf16[128,1152]{1,0:T(8,128)(2,1)S(1)}, bf16[128,1152]{1,0:T(8,128)(2,1)S(1)}, u32[]{:S(2)}, u32[]{:S(2)}) %collective-permute-start.12) | collective-permute-done | bytes 294944 | tf_op jit(solution)/shard_map/ppermute | solution.py:19
  88.9 1.6 %collective-permute-start.14 = (bf16[64,1280]{1,0:T(8,128)(2,1)S(1)}, bf16[64,1280]{1,0:T(8,128)(2,1)S(1)}, u32[]{:S(2)}, u32[]{:S(2)}) collective-permute-start(bf16[64,1280]{1,0:T(8,128)(2,1)S(1)} %get-tuple-element.27), channel_id=1, source_target_pairs={{0,2},{1,3},{2,0},{3,1},{4,6},{5,7},{6,4},{7,5},{8,10},{9,11},{10,... | collective-permute-start | bytes 491528 | tf_op jit(solution)/shard_map/ppermute | solution.py:19
  92.1 3.2 %collective-permute-done.18.refs_4_ = bf16[128,896]{1,0:T(8,128)(2,1)S(1)} collective-permute-done((bf16[128,896]{1,0:T(8,128)(2,1)S(1)}, bf16[128,896]{1,0:T(8,128)(2,1)S(1)}, u32[]{:S(2)}, u32[]{:S(2)}) %collective-permute-start.18) | collective-permute-done | bytes 229408 | tf_op jit(solution)/shard_map/ppermute | solution.py:19
  95.8 1.6 %collective-permute-start.20 = (bf16[64,896]{1,0:T(8,128)(2,1)S(1)}, bf16[64,896]{1,0:T(8,128)(2,1)S(1)}, u32[]{:S(2)}, u32[]{:S(2)}) collective-permute-start(bf16[64,896]{1,0:T(8,128)(2,1)S(1)} %get-tuple-element.33), channel_id=1, source_target_pairs={{0,2},{1,3},{2,0},{3,1},{4,6},{5,7},{6,4},{7,5},{8,10},{9,11},{10,... | collective-permute-start | bytes 344072 | tf_op jit(solution)/shard_map/ppermute | solution.py:19
  99.1 2.7 %collective-permute-done.20.refs_4_ = bf16[64,896]{1,0:T(8,128)(2,1)S(1)} collective-permute-done((bf16[64,896]{1,0:T(8,128)(2,1)S(1)}, bf16[64,896]{1,0:T(8,128)(2,1)S(1)}, u32[]{:S(2)}, u32[]{:S(2)}) %collective-permute-start.20) | collective-permute-done | bytes 114720 | tf_op jit(solution)/shard_map/ppermute | solution.py:19
  101.8 1.7 %collective-permute-done.21.refs_5_ = bf16[64,896]{1,0:T(8,128)(2,1)S(1)} collective-permute-done((bf16[64,896]{1,0:T(8,128)(2,1)S(1)}, bf16[64,896]{1,0:T(8,128)(2,1)S(1)}, u32[]{:S(2)}, u32[]{:S(2)}) %collective-permute-start.21) | collective-permute-done | bytes 114720 | tf_op jit(solution)/shard_map/ppermute | solution.py:19
  (57 shorter events, 23.2 us)
Async XLA Ops:
  0.0 15.0 %collective-permute-start.2 = (bf16[128,2048]{1,0:T(8,128)(2,1)}, bf16[128,2048]{1,0:T(8,128)(2,1)S(1)}, u32[]{:S(2)}, u32[]{:S(2)}) collective-permute-start(bf16[128,2048]{1,0:T(8,128)(2,1)} %refs_3_.1), channel_id=1, source_target_pairs={{0,1},{1,0},{2,3},{3,2},{4,5},{5,4},{6,7},{7,6},{8,9},{9,8},{10,11... | collective-permute-start | bytes 1572872 | tf_op jit(solution)/shard_map/ppermute | solution.py:19
  2.4 17.9 %collective-permute-start.1 = (bf16[256,1024]{1,0:T(8,128)(2,1)}, bf16[256,1024]{1,0:T(8,128)(2,1)}, u32[]{:S(2)}, u32[]{:S(2)}) collective-permute-start(bf16[256,1024]{1,0:T(8,128)(2,1)} %shard_map.66.refs_0_.refs_1_), channel_id=1, source_target_pairs={{0,24},{4,28},{8,16},{12,20},{16,8},{20,12},{24,0},{28,4},{1,25},{... | collective-permute-start | bytes 1572872 | tf_op jit(solution)/shard_map/ppermute | solution.py:19
  9.4 26.4 %collective-permute-start = (bf16[512,1024]{1,0:T(8,128)(2,1)}, bf16[512,1024]{1,0:T(8,128)(2,1)}, u32[]{:S(2)}, u32[]{:S(2)}) collective-permute-start(bf16[512,1024]{1,0:T(8,128)(2,1)} %shard_map.65.refs_0_.refs_3_.refs_1_.refs_2_), channel_id=1, source_target_pairs={{0,4},{4,0},{8,12},{12,8},{16,20},{20,16},{24,28},{28,24},{1,5},{5... | collective-permute-start | bytes 3145736 | tf_op jit(solution)/shard_map/ppermute | solution.py:19
  13.3 19.1 %collective-permute-start.5 = (bf16[256,1024]{1,0:T(8,128)(2,1)}, bf16[256,1024]{1,0:T(8,128)(2,1)}, u32[]{:S(2)}, u32[]{:S(2)}) collective-permute-start(bf16[256,1024]{1,0:T(8,128)(2,1)} %get-tuple-element.23), channel_id=1, source_target_pairs={{0,8},{4,12},{8,0},{12,4},{16,24},{20,28},{24,16},{28,20},{1,9},{5... | collective-permute-start | bytes 1572872 | tf_op jit(solution)/shard_map/ppermute | solution.py:19
  13.3 40.0 %collective-permute-start.8 = (bf16[256,1024]{1,0:T(8,128)(2,1)}, bf16[256,1024]{1,0:T(8,128)(2,1)}, u32[]{:S(2)}, u32[]{:S(2)}) collective-permute-start(bf16[256,1024]{1,0:T(8,128)(2,1)} %get-tuple-element.24), channel_id=1, source_target_pairs={{0,16},{4,20},{8,24},{12,28},{16,0},{20,4},{24,8},{28,12},{1,17},{... | collective-permute-start | bytes 1572872 | tf_op jit(solution)/shard_map/ppermute | solution.py:19
  16.1 24.9 %collective-permute-start.3 = (bf16[256,2048]{1,0:T(8,128)(2,1)}, bf16[256,2048]{1,0:T(8,128)(2,1)}, u32[]{:S(2)}, u32[]{:S(2)}) collective-permute-start(bf16[256,2048]{1,0:T(8,128)(2,1)} %shard_map.68), channel_id=1, source_target_pairs={{0,2},{1,3},{2,0},{3,1},{4,6},{5,7},{6,4},{7,5},{8,10},{9,11},{10,... | collective-permute-start | bytes 3145736 | tf_op jit(solution)/shard_map/ppermute | solution.py:19
  20.3 46.9 %collective-permute-start.7 = (bf16[256,1024]{1,0:T(8,128)(2,1)}, bf16[256,1024]{1,0:T(8,128)(2,1)}, u32[]{:S(2)}, u32[]{:S(2)}) collective-permute-start(bf16[256,1024]{1,0:T(8,128)(2,1)} %collective-permute-done.1.refs_0_.refs_8_), channel_id=1, source_target_pairs={{0,4},{4,0},{8,12},{12,8},{16,20},{20,16},{24,28},{28,24},{1,5},{5... | collective-permute-start | bytes 1572872 | tf_op jit(solution)/shard_map/ppermute | solution.py:19
  32.4 34.7 %collective-permute-start.6 = (bf16[256,1024]{1,0:T(8,128)(2,1)}, bf16[256,1024]{1,0:T(8,128)(2,1)}, u32[]{:S(2)}, u32[]{:S(2)}) collective-permute-start(bf16[256,1024]{1,0:T(8,128)(2,1)} %collective-permute-done.5.refs_7_), channel_id=1, source_target_pairs={{0,4},{4,0},{8,12},{12,8},{16,20},{20,16},{24,28},{28,24},{1,5},{5... | collective-permute-start | bytes 1572872 | tf_op jit(solution)/shard_map/ppermute | solution.py:19
  41.0 26.0 %copy-start.4 = (bf16[1,128,2048]{2,1,0:T(8,128)(2,1)S(1)}, bf16[1,128,2048]{2,1,0:T(8,128)(2,1)}, u32[]{:S(2)}) copy-start(bf16[1,128,2048]{2,1,0:T(8,128)(2,1)} %refs_2_.1) | copy-start | bytes 1572868
  42.9 27.4 %copy-start.1 = (bf16[512,1024]{1,0:T(8,128)(2,1)S(1)}, bf16[512,1024]{1,0:T(8,128)(2,1)}, u32[]{:S(2)}) copy-start(bf16[512,1024]{1,0:T(8,128)(2,1)} %shard_map.65.refs_0_.refs_3_.refs_1_.refs_2_) | copy-start | bytes 3145732
  42.9 27.4 %collective-permute-start.4 = (bf16[128,2048]{1,0:T(8,128)(2,1)S(1)}, bf16[128,2048]{1,0:T(8,128)(2,1)S(1)}, u32[]{:S(2)}, u32[]{:S(2)}) collective-permute-start(bf16[128,2048]{1,0:T(8,128)(2,1)S(1)} %shard_map.69.refs_1_.own_ref), channel_id=1, source_target_pairs={{0,8},{4,12},{8,0},{12,4},{16,24},{20,28},{24,16},{28,20},{1,9},{5... | collective-permute-start | bytes 1572872 | tf_op jit(solution)/shard_map/ppermute | solution.py:19
  44.4 21.2 %collective-permute-start.10 = (bf16[128,1152]{1,0:T(8,128)(2,1)S(1)}, bf16[128,1152]{1,0:T(8,128)(2,1)S(1)}, u32[]{:S(2)}, u32[]{:S(2)}) collective-permute-start(bf16[128,1152]{1,0:T(8,128)(2,1)S(1)} %shard_map.67.refs_1_), channel_id=1, source_target_pairs={{0,16},{4,20},{8,24},{12,28},{16,0},{20,4},{24,8},{28,12},{1,17},{... | collective-permute-start | bytes 884744 | tf_op jit(solution)/shard_map/ppermute | solution.py:19
  53.3 20.1 %collective-permute-start.9 = (bf16[256,1024]{1,0:T(8,128)(2,1)}, bf16[256,1024]{1,0:T(8,128)(2,1)S(1)}, u32[]{:S(2)}, u32[]{:S(2)}) collective-permute-start(bf16[256,1024]{1,0:T(8,128)(2,1)} %collective-permute-done.8.refs_9_.refs_0_), channel_id=1, source_target_pairs={{0,4},{4,0},{8,12},{12,8},{16,20},{20,16},{24,28},{28,24},{1,5},{5... | collective-permute-start | bytes 1572872 | tf_op jit(solution)/shard_map/ppermute | solution.py:19
  65.5 9.5 %collective-permute-start.11 = (bf16[128,1152]{1,0:T(8,128)(2,1)S(1)}, bf16[128,1152]{1,0:T(8,128)(2,1)S(1)}, u32[]{:S(2)}, u32[]{:S(2)}) collective-permute-start(bf16[128,1152]{1,0:T(8,128)(2,1)S(1)} %collective-permute-done.10.refs_3_.refs_4_), channel_id=1, source_target_pairs={{0,4},{4,0},{8,12},{12,8},{16,20},{20,16},{24,28},{28,24},{1,5},{5... | collective-permute-start | bytes 884744 | tf_op jit(solution)/shard_map/ppermute | solution.py:19
  67.1 12.8 %collective-permute-start.16 = (bf16[128,896]{1,0:T(8,128)(2,1)S(1)}, bf16[128,896]{1,0:T(8,128)(2,1)S(1)}, u32[]{:S(2)}, u32[]{:S(2)}) collective-permute-start(bf16[128,896]{1,0:T(8,128)(2,1)S(1)} %shard_map.77), channel_id=1, source_target_pairs={{0,16},{4,20},{8,24},{12,28},{16,0},{20,4},{24,8},{28,12},{1,17},{... | collective-permute-start | bytes 688136 | tf_op jit(solution)/shard_map/ppermute | solution.py:19
  76.4 9.6 %collective-permute-start.12 = (bf16[128,1152]{1,0:T(8,128)(2,1)S(1)}, bf16[128,1152]{1,0:T(8,128)(2,1)S(1)}, u32[]{:S(2)}, u32[]{:S(2)}) collective-permute-start(bf16[128,1152]{1,0:T(8,128)(2,1)S(1)} %shard_map.73.refs_0_), channel_id=1, source_target_pairs={{0,8},{4,12},{8,0},{12,4},{16,24},{20,28},{24,16},{28,20},{1,9},{5... | collective-permute-start | bytes 884744 | tf_op jit(solution)/shard_map/ppermute | solution.py:19
  79.9 7.5 %collective-permute-start.17 = (bf16[128,896]{1,0:T(8,128)(2,1)S(1)}, bf16[128,896]{1,0:T(8,128)(2,1)S(1)}, u32[]{:S(2)}, u32[]{:S(2)}) collective-permute-start(bf16[128,896]{1,0:T(8,128)(2,1)S(1)} %shard_map.78), channel_id=1, source_target_pairs={{0,4},{4,0},{8,12},{12,8},{16,20},{20,16},{24,28},{28,24},{1,5},{5... | collective-permute-start | bytes 688136 | tf_op jit(solution)/shard_map/ppermute | solution.py:19
  88.7 6.6 %collective-permute-start.18 = (bf16[128,896]{1,0:T(8,128)(2,1)S(1)}, bf16[128,896]{1,0:T(8,128)(2,1)S(1)}, u32[]{:S(2)}, u32[]{:S(2)}) collective-permute-start(bf16[128,896]{1,0:T(8,128)(2,1)S(1)} %shard_map.79.refs_0_), channel_id=1, source_target_pairs={{0,8},{4,12},{8,0},{12,4},{16,24},{20,28},{24,16},{28,20},{1,9},{5... | collective-permute-start | bytes 688136 | tf_op jit(solution)/shard_map/ppermute | solution.py:19
  88.8 8.6 %collective-permute-start.13 = (bf16[64,1280]{1,0:T(8,128)(2,1)S(1)}, bf16[64,1280]{1,0:T(8,128)(2,1)S(1)}, u32[]{:S(2)}, u32[]{:S(2)}) collective-permute-start(bf16[64,1280]{1,0:T(8,128)(2,1)S(1)} %get-tuple-element.26), channel_id=1, source_target_pairs={{0,1},{1,0},{2,3},{3,2},{4,5},{5,4},{6,7},{7,6},{8,9},{9,8},{10,11... | collective-permute-start | bytes 491528 | tf_op jit(solution)/shard_map/ppermute | solution.py:19
  88.9 8.8 %collective-permute-start.14 = (bf16[64,1280]{1,0:T(8,128)(2,1)S(1)}, bf16[64,1280]{1,0:T(8,128)(2,1)S(1)}, u32[]{:S(2)}, u32[]{:S(2)}) collective-permute-start(bf16[64,1280]{1,0:T(8,128)(2,1)S(1)} %get-tuple-element.27), channel_id=1, source_target_pairs={{0,2},{1,3},{2,0},{3,1},{4,6},{5,7},{6,4},{7,5},{8,10},{9,11},{10,... | collective-permute-start | bytes 491528 | tf_op jit(solution)/shard_map/ppermute | solution.py:19
  90.4 8.1 %collective-permute-start.15 = (bf16[64,1280]{1,0:T(8,128)(2,1)S(1)}, bf16[64,1280]{1,0:T(8,128)(2,1)S(1)}, u32[]{:S(2)}, u32[]{:S(2)}) collective-permute-start(bf16[64,1280]{1,0:T(8,128)(2,1)S(1)} %get-tuple-element.28), channel_id=1, source_target_pairs={{0,3},{1,2},{2,1},{3,0},{4,7},{5,6},{6,5},{7,4},{8,11},{9,10},{10,... | collective-permute-start | bytes 491528 | tf_op jit(solution)/shard_map/ppermute | solution.py:19
  95.7 3.4 %collective-permute-start.19 = (bf16[64,896]{1,0:T(8,128)(2,1)S(1)}, bf16[64,896]{1,0:T(8,128)(2,1)S(1)}, u32[]{:S(2)}, u32[]{:S(2)}) collective-permute-start(bf16[64,896]{1,0:T(8,128)(2,1)S(1)} %get-tuple-element.32), channel_id=1, source_target_pairs={{0,1},{1,0},{2,3},{3,2},{4,5},{5,4},{6,7},{7,6},{8,9},{9,8},{10,11... | collective-permute-start | bytes 344072 | tf_op jit(solution)/shard_map/ppermute | solution.py:19
  95.8 6.0 %collective-permute-start.20 = (bf16[64,896]{1,0:T(8,128)(2,1)S(1)}, bf16[64,896]{1,0:T(8,128)(2,1)S(1)}, u32[]{:S(2)}, u32[]{:S(2)}) collective-permute-start(bf16[64,896]{1,0:T(8,128)(2,1)S(1)} %get-tuple-element.33), channel_id=1, source_target_pairs={{0,2},{1,3},{2,0},{3,1},{4,6},{5,7},{6,4},{7,5},{8,10},{9,11},{10,... | collective-permute-start | bytes 344072 | tf_op jit(solution)/shard_map/ppermute | solution.py:19
  97.4 6.2 %collective-permute-start.21 = (bf16[64,896]{1,0:T(8,128)(2,1)S(1)}, bf16[64,896]{1,0:T(8,128)(2,1)S(1)}, u32[]{:S(2)}, u32[]{:S(2)}) collective-permute-start(bf16[64,896]{1,0:T(8,128)(2,1)S(1)} %get-tuple-element.34), channel_id=1, source_target_pairs={{0,3},{1,2},{2,1},{3,0},{4,7},{5,6},{6,5},{7,4},{8,11},{9,10},{10,... | collective-permute-start | bytes 344072 | tf_op jit(solution)/shard_map/ppermute | solution.py:19
  (6 other events, 19.2 us)
